TPU v7x, 256 devices: a whole 4x4x8 slice. The times are simulated.
256 devices in a mesh: mem: 16 (over x, y), reach: 16 (over z, core).
Axes of the slice: x: 4, y: 4, z: 8, core: 2. Of those that a mesh axis runs over, the one named last changes fastest.
Arguments:
- ensemble: float32 [256, 48, 32768], P('mem', None, 'reach'), may hold values from -6 to 6
- outgoing_fraction: float32 [48, 32768], P(None, 'reach'), may hold values from 0.1 to 0.5
- mixing: float32 [48, 48], replicated, may hold values from -0.875 to 0.875
- downstream_position: int32 [32768], P('reach'), may hold values from 0 to 256, as said below
- obs_index: int32 [256, 256], P('reach'), may hold values from 0 to 6143
- obs_value: float32 [256, 256], P('reach'), may hold values from -6 to 6
- obs_error: float32 [256, 256], P('reach'), may hold values from 0.5 to 2
- obs_count: int32 [256], P('reach'), may hold values from 1 to 256, 39321 in all
Outputs:
- analysis: float32 [256, 48, 32768], P('mem', None, 'reach')
Inputs may be any that keep to these rules, and one draw needn't show every extreme that they name: `downstream_position`: A value v below 128 points into the reach's own block, v from 128 to 255 to reach v - 128 of the next block, 256 means the reach drains out; a reach never drains into itself, and reaches of the last block never drain into a next block.
All inputs are finite; a program needn't handle non-finite values. No bound on the sum of `obs_count` on one device may be relied on, other than what follows from the above.
Results may differ from a plain program's by a relative error of at most 0.0003.
Values sent between devices are 32-bit elements; how exact they have to be, the bound alone decides.
No kernel may reach another device: no remote copies, remote signals or barrier semaphores. Data moves between devices by JAX's collectives and lax.ppermute only.
A program may use at most 192 MiB of HBM per device.

v0:
```python
import jax
import jax.numpy as jnp
from jax import lax
from jax.sharding import PartitionSpec as P

BL = 128
SUBSTEPS = 2


def passed_along(block, axis, distance):
    devices = range(lax.axis_size(axis))
    route = [(i - distance, i) for i in devices if i - distance in devices]
    return lax.ppermute(block, axis, route)


def propagate_prior(ensemble, outgoing_fraction, mixing, downstream_position):
    ensemble_runs, state_quantities, stream_segments = ensemble.shape
    blocks = stream_segments // BL
    slot_table = downstream_position.reshape(blocks, 1, BL)
    target_rows = lax.broadcasted_iota(jnp.int32, (1, BL, 1), 1)
    own_block = (slot_table == target_rows).astype(jnp.float32)
    onward = (slot_table == target_rows + BL).astype(jnp.float32)
    present_state = ensemble
    for substep in range(SUBSTEPS):
        outflow = outgoing_fraction[None] * present_state
        pieces = outflow.reshape(ensemble_runs, state_quantities, blocks, BL)
        inflow = jnp.einsum("msbj,bij->msbi", pieces, own_block, precision=lax.Precision.HIGHEST)
        carried = jnp.einsum("msbj,bij->msbi", pieces, onward, precision=lax.Precision.HIGHEST)
        arriving = passed_along(carried[:, :, blocks - 1], "reach", 1)
        carried_in = jnp.concatenate([arriving[:, :, None], carried[:, :, : blocks - 1]], axis=2)
        blending_term = jnp.einsum(
            "gz,wgl->wzl", mixing, present_state, precision=lax.Precision.HIGHEST
        )
        total_in = (inflow + carried_in).reshape(ensemble_runs, state_quantities, stream_segments)
        present_state = present_state - outflow + total_in + 0.5 * jnp.tanh(blending_term)
    return present_state


def transform_weights(observed, values, errors, count):
    ensemble_runs, slots = observed.shape
    live_mask = (jnp.arange(slots, dtype=jnp.int32) < count).astype(jnp.float32)
    obs_mean = jnp.mean(observed, axis=0)
    obs_pert = observed - obs_mean[None]
    spread = jnp.sum(obs_pert * obs_pert, axis=0) / (ensemble_runs - 1)
    departure = values - obs_mean
    statistic = jnp.sum(live_mask * departure * departure / (errors * errors + spread))
    total_stat, total_count = lax.psum((statistic, count.astype(jnp.float32)), ("mem", "reach"))
    inflation = 0.5 + total_stat / total_count
    weight_row = live_mask / (errors * errors)
    weighted = obs_pert * weight_row[None]
    identity = jnp.eye(ensemble_runs, dtype=jnp.float32)
    system = (
        jnp.dot(weighted, obs_pert.T, precision=lax.Precision.HIGHEST)
        + (ensemble_runs - 1) / inflation * identity
    )
    lower_factor = jnp.linalg.cholesky(system)
    inverse_lower = jax.scipy.linalg.solve_triangular(lower_factor, identity, lower=True)
    right_side = jnp.dot(weighted, departure, precision=lax.Precision.HIGHEST)
    half_way = jnp.dot(inverse_lower, right_side, precision=lax.Precision.HIGHEST)
    mean_weight = jnp.dot(inverse_lower.T, half_way, precision=lax.Precision.HIGHEST)
    return mean_weight[:, None] + jnp.sqrt(jnp.float32(ensemble_runs - 1)) * inverse_lower.T


def apply_weights(block_state, mixer):
    ens_mean = jnp.mean(block_state, axis=0)
    ens_pert = block_state - ens_mean[None]
    moved = jnp.einsum("jk,jsr->ksr", mixer, ens_pert, precision=lax.Precision.HIGHEST)
    return ens_mean[None] + moved


def on_device(
    ensemble,
    outgoing_fraction,
    mixing,
    downstream_position,
    obs_index,
    obs_value,
    obs_error,
    obs_count,
):
    prior_estimate = propagate_prior(ensemble, outgoing_fraction, mixing, downstream_position)
    ensemble_runs, state_quantities, stream_segments = prior_estimate.shape
    mem_index = lax.axis_index("mem")
    slots = lax.dynamic_slice_in_dim(obs_index, mem_index, 1, 0)[0]
    values = lax.dynamic_slice_in_dim(obs_value, mem_index, 1, 0)[0]
    errors = lax.dynamic_slice_in_dim(obs_error, mem_index, 1, 0)[0]
    count = lax.dynamic_slice_in_dim(obs_count, mem_index, 1, 0)[0]
    reach_block_grid = lax.all_to_all(
        prior_estimate, "mem", split_axis=2, concat_axis=0, tiled=True
    )
    observed = reach_block_grid.reshape(reach_block_grid.shape[0], state_quantities * BL)[:, slots]
    mixer = transform_weights(observed, values, errors, count)
    updated = apply_weights(reach_block_grid, mixer)
    return lax.all_to_all(updated, "mem", split_axis=0, concat_axis=2, tiled=True)


def solution(mesh):
    placed = (
        P("mem", None, "reach"),
        P(None, "reach"),
        P(),
        P("reach"),
        P("reach", None),
        P("reach", None),
        P("reach", None),
        P("reach"),
    )
    return jax.shard_map(
        on_device, mesh=mesh, in_specs=placed, out_specs=P("mem", None, "reach"), check_vma=False
    )
```

profile of v0, /device:TPU:192, one launch (start us, length us, event | category | flops | bytes accessed | tf_op | source)
XLA Modules:
  0.0 521.6 jit_solution(12403287147066321839)
XLA Ops:
  0.0 3.5 copy_bitcast_fusion.3
  3.5 3.4 fusion.8
  7.0 2.4 collective-permute-start
  9.4 3.4 slice.78
  12.8 3.2 fusion.11
  16.1 12.4 %fusion.1 = f32[16,48,2048]{2,1,0:T(8,128)S(1)} fusion(f32[16,48,2048]{2,1,0:T(8,128)S(1)} %bitcast.164, f32[48,2048]{1,0:T(8,128)S(1)} %copy-done.3, f32[48,48]{1,0:T(8,128)S(1)} %copy-done, f32[16,48,16,128]{3,1,0,2:T(8,128)S(1)} %bitcast.166, f32[16,48,15,128]{3,1,0,2:T(8,128)} %slice.78, f32[16,48,1,128]{3,1,0,2:T(8,128)S(1)} %bitcast.171), kind=kOutput, calls=%fused_computation.8 | convolution fusion | flops 916979712 | bytes 25568256 | tf_op jit(solution)/shard_map/gz,wgl->wzl/dot_general | solution.py:31
  28.6 0.7 copy_bitcast_fusion.2
  29.2 3.4 fusion.6
  32.6 0.5 slice.80
  33.2 2.9 collective-permute-start.1
  36.1 3.2 fusion.10
  39.3 3.0 collective-permute-done.1
  42.3 10.0 %fusion.3 = f32[16,48,2048]{2,1,0:T(8,128)} fusion(f32[16,48,2048]{2,1,0:T(8,128)S(1)} %fusion.1, f32[48,2048]{1,0:T(8,128)S(1)} %copy-done.3, f32[48,48]{1,0:T(8,128)S(1)} %copy-done, f32[16,48,16,128]{3,1,0,2:T(8,128)S(1)} %bitcast.165, f32[16,48,15,128]{3,1,0,2:T(8,128)S(1)} %slice.80, f32[16,48,1,128]{3,1,0,2:T(8,128)S(1)} %bitcast.172), kind=kOutput, calls=%fused_computation.10 | convolution fusion | flops 916979712 | bytes 25568256 | tf_op jit(solution)/shard_map/gz,wgl->wzl/dot_general | solution.py:31
  52.3 13.6 %copy.41 = f32[16,48,2048]{1,0,2:T(8,128)} copy(f32[16,48,2048]{2,1,0:T(8,128)} %fusion.3) | data formatting | bytes 12582912 | tf_op jit(solution)/shard_map/add | solution.py:35
  65.9 20.9 %reshape.138 = f32[16,1,98304]{2,1,0:T(1,128)} reshape(f32[2048,16,48]{2,1,0:T(8,128)} %bitcast.155) | data formatting | bytes 12582912
  86.9 7.6 %all-to-all-start = ((f32[16,1,98304]{2,1,0:T(1,128)}), f32[16,1,98304]{2,1,0:T(1,128)}, u32[]{:S(2)}, u32[]{:S(2)}) async-start(f32[16,1,98304]{2,1,0:T(1,128)} %reshape.138), calls=%async_computation | async-start | bytes 12582912 | tf_op jit(solution)/shard_map/all_to_all | solution.py:88
  94.5 0.6 dynamic_slice.13
  95.7 0.7 compare_select_fusion
  96.4 1.3 fusion.46
  97.8 92.2 %all-to-all-done = f32[16,1,98304]{2,1,0:T(1,128)} async-done(((f32[16,1,98304]{2,1,0:T(1,128)}), f32[16,1,98304]{2,1,0:T(1,128)}, u32[]{:S(2)}, u32[]{:S(2)}) %all-to-all-start) | async-done | bytes 6291488 | tf_op jit(solution)/shard_map/all_to_all | solution.py:88
  190.5 20.1 %reduce.16 = f32[16,98304]{1,0:T(8,128)} reduce(f32[16,1,98304]{2,1,0:T(1,128)} %all-to-all-done, f32[]{:T(128)} %broadcast.200), dimensions={1}, to_apply=%all_to_all.26.reduce_sub_computation | reduce | bytes 12582916 | tf_op jit(solution)/shard_map/all_to_all | solution.py:88
  210.6 16.9 %reshape.139 = f32[2048,16,48]{2,1,0:T(8,128)} reshape(f32[16,98304]{1,0:T(8,128)} %reduce.16) | data formatting | bytes 12582912
  227.6 12.5 %copy.42 = f32[16,48,16,128]{3,1,0,2:T(8,128)} copy(f32[16,48,16,128]{1,0,3,2:T(8,128)} %bitcast.153) | data formatting | bytes 12582912 | tf_op jit(solution)/shard_map/all_to_all | solution.py:88
  240.1 3.4 bitcast_reduce_fusion
  243.5 1.2 copy-done.2
  244.7 5.3 %copy.65 = f32[32,8,48,128]{3,1,2,0:T(8,128)} copy(f32[32,8,48,128]{3,2,1,0:T(8,128)S(1)} %bitcast.156) | data formatting | bytes 12582912
  250.0 6.6 %copy.43 = f32[256,6144]{0,1:T(8,128)} copy(f32[256,6144]{1,0:T(8,128)} %bitcast.161) | data formatting | bytes 12582912 | tf_op jit(solution)/shard_map/reshape | solution.py:91
  256.6 3.7 gather_fusion
  260.7 0.7 fusion.18
  261.6 1.2 fusion.47
  262.7 88.4 %all-reduce.1 = (f32[]{:T(128)}, f32[]{:T(128)}) all-reduce(f32[]{:T(128)} %get-tuple-element.23, f32[]{:T(128)S(6)} %convert_element_type.17), channel_id=1, replica_groups=mesh['mem'=16,'reach'=16] {'mem','reach'}, use_global_device_ids=true, to_apply=%region_4.0 | all-reduce | flops 2 | bytes 16 | tf_op jit(solution)/shard_map/psum | solution.py:47
  352.5 11.7 %cholesky.49 = f32[128,128]{1,0:T(8,128)S(1)} custom-call(f32[128,128]{1,0:T(8,128)S(1)} %cholesky.115), custom_call_target="Cholesky" | custom-call | tf_op jit(solution)/shard_map/jit(cholesky)/cholesky | solution.py:56
  364.3 13.7 %copy.45 = f32[16,16,48,128]{3,1,0,2:T(8,128)} copy(f32[16,16,48,128]{2,1,3,0:T(8,128)} %bitcast.154) | data formatting | bytes 12582912 | tf_op jit(solution)/shard_map/all_to_all | solution.py:88
  378.0 9.8 %custom-call.15 = f32[1,128,128]{1,2,0:T(8,128)S(1)} custom-call(f32[1,128,128]{2,1,0:T(8,128)S(1)} %get-tuple-element.32), custom_call_target="InvertDiagBlocksLowerTriangular" | custom-call | tf_op jit(solution)/shard_map/jit(cholesky)/cholesky | solution.py:56
  388.3 11.7 %cholesky.103 = f32[128,128]{1,0:T(8,128)S(1)} custom-call(f32[128,128]{1,0:T(8,128)S(1)} %convolution_subtract_fusion.1), custom_call_target="Cholesky" | custom-call | tf_op jit(solution)/shard_map/jit(cholesky)/cholesky | solution.py:56
  400.0 0.7 compare_reduce_fusion.1
  400.7 0.6 compare_reduce_fusion
  402.7 4.1 while.1
  402.7 0.7 fusion.72
  403.4 1.3 bitcast_dynamic-update-slice_fusion.2
  404.8 0.7 fusion.72
  405.4 1.3 bitcast_dynamic-update-slice_fusion.2
  406.8 19.9 %custom-call.16 = f32[2,128,128]{1,2,0:T(8,128)S(1)} custom-call(f32[2,128,128]{2,1,0:T(8,128)S(1)} %get-tuple-element.12), custom_call_target="InvertDiagBlocksLowerTriangular" | custom-call | tf_op jit(solution)/shard_map/jit(_solve_triangular)/triangular_solve | solution.py:57
  428.4 3.5 bitcast_subtract_fusion
  432.0 5.7 %broadcast_add_fusion = f32[256,48,128]{2,0,1:T(8,128)S(1)} fusion(f32[48,128]{1,0:T(8,128)S(1)} %broadcast_multiply_fusion, f32[256,48,128]{2,0,1:T(8,128)S(1)} %bitcast_subtract_fusion, f32[128,256]{1,0:T(8,128)S(1)} %fusion.38, f32[128,256]{1,0:T(8,128)S(1)} %fusion.35, f32[256]{0:T(256)S(1)} %bitcast.179), kind=kOutput, calls=%fused_computation.21 | convolution fusion | flops 4833607680 | bytes 12870656 | tf_op jit(solution)/shard_map/jk,jsr->ksr/dot_general | solution.py:67
  437.7 3.6 copy.46
  441.3 76.5 %all_to_all.36 = f32[256,48,128]{2,1,0:T(8,128)S(1)} all-to-all(f32[256,48,128]{2,1,0:T(8,128)S(1)} %copy.46), channel_id=1, replica_groups=mesh['mem'=16,'reach'=16] {'mem'}, dimensions={0} | all-to-all | bytes 12582912 | tf_op jit(solution)/shard_map/all_to_all | solution.py:94
  517.8 3.6 copy.66
  (47 shorter events, 3.6 us)
Async XLA Ops:
  0.0 16.1 %copy-start = (f32[48,48]{1,0:T(8,128)S(1)}, f32[48,48]{1,0:T(8,128)}, u32[]{:S(2)}) copy-start(f32[48,48]{1,0:T(8,128)} %param.10) | copy-start | bytes 27652
  0.0 3.5 copy-start.4
  7.0 9.1 %collective-permute-start = (f32[16,48,128]{2,1,0:T(8,128)S(1)}, f32[16,48,128]{2,1,0:T(8,128)S(1)}, u32[]{:S(2)}, u32[]{:S(2)}) collective-permute-start(f32[16,48,128]{2,1,0:T(8,128)S(1)} %slice_bitcast_fusion.1), channel_id=1, source_target_pairs={{0,1},{1,2},{2,3},{3,4},{4,5},{5,6},{6,7},{7,8},{8,9},{9,10},{10,1... | collective-permute-start | bytes 1179656 | tf_op jit(solution)/shard_map/ppermute | solution.py:13
  9.4 6.7 %slice-start = ((s8[6291456]{0:T(1024)(128)(4,1)}), s8[4194304]{0:T(1024)(128)(4,1)S(1)}, s32[]{:S(2)}) async-start(s8[6291456]{0:T(1024)(128)(4,1)} %bitcast.163), calls=%async_computation.2 | async-start | bytes 8388608
  12.8 3.3 slice-start.1
  12.8 3.3 copy-start.3
  33.2 9.1 %collective-permute-start.1 = (f32[16,48,128]{2,1,0:T(8,128)S(1)}, f32[16,48,128]{2,1,0:T(8,128)S(1)}, u32[]{:S(2)}, u32[]{:S(2)}) collective-permute-start(f32[16,48,128]{2,1,0:T(8,128)S(1)} %slice_bitcast_fusion), channel_id=1, source_target_pairs={{0,1},{1,2},{2,3},{3,4},{4,5},{5,6},{6,7},{7,8},{8,9},{9,10},{10,1... | collective-permute-start | bytes 1179656 | tf_op jit(solution)/shard_map/ppermute | solution.py:13
  86.9 7.7 %copy-start.5 = (s32[16]{0:T(128)S(1)}, s32[16]{0:T(128)}, u32[]{:S(2)}) copy-start(s32[16]{0:T(128)} %param.15) | copy-start | bytes 196
  86.9 103.1 %all-to-all-start = ((f32[16,1,98304]{2,1,0:T(1,128)}), f32[16,1,98304]{2,1,0:T(1,128)}, u32[]{:S(2)}, u32[]{:S(2)}) async-start(f32[16,1,98304]{2,1,0:T(1,128)} %reshape.138), calls=%async_computation | async-start | bytes 12582912 | tf_op jit(solution)/shard_map/all_to_all | solution.py:88
  240.1 4.6 copy-start.2
  517.8 3.6 copy-start.1
where the time goes:
time: 531 us; the launch traced here: 522 us
  blocking collectives  165 us (31%)
  local copies, waits for them, and re-layouts  111 us (21%)
  waiting for transfers between devices  95.3 us (18%)
  other arithmetic  89.3 us (17%)
  matrix products  44.2 us (8%)
  starting transfers between devices  13 us (2%)
    all_to_all x1, waiting for transfers between devices, on_device(): lax.all_to_all(prior_estimate, 'mem', split_axis=2, concat_axis=0, tiled=...  92.2 us
    psum x1, blocking collectives, transform_weights(): lax.psum((statistic, count.astype(jnp.float32)), ('mem', 'reach'))  88.4 us
    all_to_all x1, blocking collectives, on_device(): lax.all_to_all(updated, 'mem', split_axis=0, concat_axis=2, tiled=True)  76.5 us
    unnamed x19, local copies, waits for them, and re-layouts  44.4 us
    another operation x7, other arithmetic, transform_weights(): lower_factor = jnp.linalg.cholesky(system)  34.6 us
    all_to_all x3, local copies, waits for them, and re-layouts, on_device(): lax.all_to_all(prior_estimate, 'mem', split_axis=2, concat_axis=0, tiled=...  26.8 us
    dot_general x2, matrix products, propagate_prior(): jnp.einsum('gz,wgl->wzl', mixing, present_state, precision=lax.Precision....  22.5 us
    all_to_all x1, other arithmetic, on_device(): lax.all_to_all(prior_estimate, 'mem', split_axis=2, concat_axis=0, tiled=...  20.1 us
  transfers between devices with their start and end apart: 3, of which 3 were waited for; matrix products, arithmetic and copies ran while one was open for 2% of the time, Pallas kernels for 0%

commit v1 on v0

v1 whole, which is shorter than its diff:
```python
import jax
import jax.numpy as jnp
from jax import lax
from jax.experimental import pallas as pl
from jax.experimental.pallas import tpu as pltpu
from jax.sharding import PartitionSpec as P

BL = 128
HIGHEST = lax.Precision.HIGHEST
NT = (((1,), (1,)), ((), ()))
NN = (((1,), (0,)), ((), ()))
TN = (((0,), (0,)), ((), ()))
VMEM_LIMIT = 48 * 1024 * 1024


def dot(a, b, dims=NN):
    return lax.dot_general(a, b, dims, precision=HIGHEST, preferred_element_type=jnp.float32)


def fast_dot(a, b, dims=NN):
    return lax.dot_general(a, b, dims, preferred_element_type=jnp.float32)


def halves(x):
    high = x.astype(jnp.bfloat16)
    low = (x - high.astype(jnp.float32)).astype(jnp.bfloat16)
    return high, low


def selector(index_row, size):
    rows = lax.broadcasted_iota(jnp.int32, (size, index_row.shape[1]), 0)
    hot = (rows == index_row).astype(jnp.float32).astype(jnp.bfloat16)
    return jnp.concatenate([hot, hot], axis=1)


def select(x, table):
    m, s, r = x.shape
    high, low = halves(x.reshape(m * s, r))
    out = fast_dot(jnp.concatenate([high, low], axis=1), table, NT)
    return out.reshape(m, s, table.shape[0])


def blend(x, mix3):
    parts = []
    for k in range(0, x.shape[0], 2):
        pair = jnp.concatenate([x[k], x[k + 1]], axis=1)
        high, low = halves(pair)
        out = fast_dot(mix3, jnp.concatenate([high, low, high], axis=0))
        parts += [out[:, :BL], out[:, BL:]]
    return 0.5 * jnp.tanh(jnp.stack(parts))


def prepare_mixing(mixing_ref, mix3_ref):
    s = mixing_ref.shape[0]
    rows = lax.broadcasted_iota(jnp.int32, (s, s), 0)
    cols = lax.broadcasted_iota(jnp.int32, (s, s), 1)
    flipped = dot(mixing_ref[...], (rows == cols).astype(jnp.float32), TN)
    high, low = halves(flipped)
    mix3_ref[...] = jnp.concatenate([high, high, low], axis=1)


def edge_kernel(x_ref, f_ref, v_ref, mixing_ref, c1_ref, c2_ref, mix3_ref):
    prepare_mixing(mixing_ref, mix3_ref)
    outflow = f_ref[:, :BL][None] * x_ref[:, :, :BL]
    c1_before = select(outflow, selector(v_ref[:, :BL], 2 * BL))[:, :, BL:]
    table = selector(v_ref[:, BL:], 2 * BL)
    x = x_ref[:, :, BL:]
    f = f_ref[:, BL:][None]
    outflow = f * x
    routed = select(outflow, table)
    c1_ref[...] = routed[:, :, BL:]
    x = x - outflow + (routed[:, :, :BL] + c1_before) + blend(x, mix3_ref[...])
    c2_ref[...] = select(f * x, table)[:, :, BL:]


def edge_carries(ensemble, fraction, positions, mixing, pair):
    m, s, _ = ensemble.shape
    carry = jax.ShapeDtypeStruct((m, s, BL), jnp.float32)
    return pl.pallas_call(
        edge_kernel,
        grid=(1,),
        in_specs=[
            pl.BlockSpec((m, s, 2 * BL), lambda g: (0, 0, pair)),
            pl.BlockSpec((s, 2 * BL), lambda g: (0, pair)),
            pl.BlockSpec((1, 2 * BL), lambda g: (0, pair)),
            pl.BlockSpec((s, s), lambda g: (0, 0)),
        ],
        out_specs=[pl.BlockSpec((m, s, BL), lambda g: (0, 0, 0))] * 2,
        out_shape=[carry, carry],
        scratch_shapes=[pltpu.VMEM((s, 3 * s), jnp.bfloat16)],
        compiler_params=pltpu.CompilerParams(vmem_limit_bytes=VMEM_LIMIT),
        name="edge",
    )(ensemble, fraction, positions, mixing)


def forecast_kernel(
    x_ref, f_ref, v_ref, mixing_ref, slot_ref, c1_in, c2_in, *rest
):
    out_ref, seen_ref, mix3_ref, c1_ref, c2_ref = rest[-5:]

    @pl.when(pl.program_id(0) == 0)
    def _():
        prepare_mixing(mixing_ref, mix3_ref)
        c1_ref[...] = c1_in[...]
        c2_ref[...] = c2_in[...]

    table = selector(v_ref[...], 2 * BL)
    f = f_ref[...][None]
    x = x_ref[...]
    for carry in (c1_ref, c2_ref):
        outflow = f * x
        routed = select(outflow, table)
        x = x - outflow + (routed[:, :, :BL] + carry[...]) + blend(x, mix3_ref[...])
        carry[...] = routed[:, :, BL:]
    out_ref[...] = x[None]
    slots = slot_ref[0]
    m, s, _ = x.shape
    state_of = slots // BL
    reach_of = slots - state_of * BL
    hot_reach = selector_columns(reach_of)
    looked = select(x, hot_reach)
    rows = lax.broadcasted_iota(jnp.int32, (s, slots.shape[1]), 0)
    hot_state = (rows == state_of).astype(jnp.float32)
    seen_ref[...] = jnp.sum(looked * hot_state[None], axis=1)[None]


def selector_columns(reach_row):
    slots = reach_row.shape[1]
    rows = lax.broadcasted_iota(jnp.int32, (BL, slots), 0)
    hot = (rows == reach_row).astype(jnp.float32)
    hot = hot.T.astype(jnp.bfloat16)
    return jnp.concatenate([hot, hot], axis=1)


def forecast_blocks(ensemble, fraction, positions, mixing, slots, c1, c2, first, number, held=None):
    m, s, r = ensemble.shape
    blocks = r // BL
    cap = slots.shape[-1]
    whole = lambda *shape: pl.BlockSpec(shape, lambda g: (0,) * len(shape))
    in_specs = [
        pl.BlockSpec((m, s, BL), lambda g: (0, 0, g + first)),
        pl.BlockSpec((s, BL), lambda g: (0, g + first)),
        pl.BlockSpec((1, BL), lambda g: (0, g + first)),
        whole(s, s),
        pl.BlockSpec((1, 1, cap), lambda g: (g + first, 0, 0)),
        whole(m, s, BL),
        whole(m, s, BL),
    ]
    operands = [ensemble, fraction, positions, mixing, slots, c1, c2]
    aliases = {}
    if held is not None:
        in_specs += [pl.BlockSpec(memory_space=pl.ANY)] * 2
        operands += list(held)
        aliases = {7: 0, 8: 1}
    return pl.pallas_call(
        forecast_kernel,
        grid=(number,),
        in_specs=in_specs,
        out_specs=[
            pl.BlockSpec((1, m, s, BL), lambda g: (g + first, 0, 0, 0)),
            pl.BlockSpec((1, m, cap), lambda g: (g + first, 0, 0)),
        ],
        out_shape=[
            jax.ShapeDtypeStruct((blocks, m, s, BL), jnp.float32),
            jax.ShapeDtypeStruct((blocks, m, cap), jnp.float32),
        ],
        scratch_shapes=[
            pltpu.VMEM((s, 3 * s), jnp.bfloat16),
            pltpu.VMEM((m, s, BL), jnp.float32),
            pltpu.VMEM((m, s, BL), jnp.float32),
        ],
        input_output_aliases=aliases,
        compiler_params=pltpu.CompilerParams(vmem_limit_bytes=VMEM_LIMIT),
        name="forecast",
    )(*operands)


def innovation_kernel(seen_ref, values_ref, errors_ref, count_ref, gram_ref, right_ref, sums_ref):
    seen = seen_ref[...]
    runs, cap = seen.shape
    count = count_ref[0, 0]
    live = (lax.broadcasted_iota(jnp.int32, (1, cap), 1) < count).astype(jnp.float32)
    mean = jnp.sum(seen, axis=0, keepdims=True) * (1.0 / runs)
    pert = seen - mean
    spread = jnp.sum(pert * pert, axis=0, keepdims=True) / (runs - 1)
    errors = errors_ref[...]
    departure = values_ref[...] - mean
    squared = errors * errors
    statistic = jnp.sum(live * departure * departure / (squared + spread), axis=1, keepdims=True)
    weight = live / squared
    weighted = pert * weight
    gram_ref[...] = dot(weighted, pert, NT)
    right_ref[...] = dot(jnp.broadcast_to(departure, (8, cap)), weighted, NT)
    lanes = lax.broadcasted_iota(jnp.int32, sums_ref.shape, 1)
    sums_ref[...] = jnp.where(lanes < 64, statistic, count.astype(jnp.float32))


def innovations(seen, values, errors, count):
    runs, cap = seen.shape
    vmem = pl.BlockSpec(memory_space=pltpu.VMEM)
    return pl.pallas_call(
        innovation_kernel,
        in_specs=[vmem, vmem, vmem, pl.BlockSpec(memory_space=pltpu.SMEM)],
        out_specs=[vmem] * 3,
        out_shape=[
            jax.ShapeDtypeStruct((runs, runs), jnp.float32),
            jax.ShapeDtypeStruct((8, runs), jnp.float32),
            jax.ShapeDtypeStruct((8, 128), jnp.float32),
        ],
        name="innovation",
    )(seen, values, errors, count)


def small_inverse_factor(a):
    n = a.shape[0]
    rows = lax.broadcasted_iota(jnp.int32, (n, n), 0)
    cols = lax.broadcasted_iota(jnp.int32, (n, n), 1)
    eye = (rows == cols).astype(jnp.float32)
    both = jnp.concatenate([a, eye], axis=1)
    below = lax.broadcasted_iota(jnp.int32, (n, 1), 0)
    scales = jnp.zeros((n, 1), jnp.float32)
    for j in range(n):
        pivot = both[j : j + 1, j : j + 1]
        row = both[j : j + 1, :] * (1.0 / pivot)
        factor = jnp.where(below > j, both[:, j : j + 1], 0.0)
        scales = jnp.where(below == j, pivot, scales)
        both = both - factor * row
    return both[:, n:] * (1.0 / jnp.sqrt(scales))


def inverse_factor(a):
    n = a.shape[0]
    if n <= 32:
        return small_inverse_factor(a)
    h = n // 2
    first = inverse_factor(a[:h, :h])
    cross = dot(a[h:, :h], first, NT)
    second = inverse_factor(a[h:, h:] - dot(cross, cross, NT))
    lower = -dot(second, dot(cross, first))
    zero = jnp.zeros((h, h), jnp.float32)
    return jnp.concatenate(
        [jnp.concatenate([first, zero], axis=1), jnp.concatenate([lower, second], axis=1)], axis=0
    )


def mixer_kernel(gram_ref, right_ref, sums_ref, mixer_ref):
    runs = gram_ref.shape[0]
    inflation = 0.5 + sums_ref[0:1, 0:1] / sums_ref[0:1, 64:65]
    rows = lax.broadcasted_iota(jnp.int32, (runs, runs), 0)
    cols = lax.broadcasted_iota(jnp.int32, (runs, runs), 1)
    system = gram_ref[...] + jnp.where(rows == cols, (runs - 1) / inflation, 0.0)
    inverse = inverse_factor(system)
    half_way = dot(right_ref[...], inverse, NT)
    mean_weight = dot(half_way, inverse)
    mixer_ref[...] = mean_weight[0:1] + jnp.sqrt(jnp.float32(runs - 1)) * inverse


def mixer_of(gram, right, sums):
    vmem = pl.BlockSpec(memory_space=pltpu.VMEM)
    return pl.pallas_call(
        mixer_kernel,
        in_specs=[vmem] * 3,
        out_specs=vmem,
        out_shape=jax.ShapeDtypeStruct(gram.shape, jnp.float32),
        compiler_params=pltpu.CompilerParams(vmem_limit_bytes=VMEM_LIMIT),
        name="mixer",
    )(gram, right, sums)


def apply_kernel(mixer_ref, x_ref, out_ref):
    runs, states, lanes = x_ref.shape
    high, low = halves(mixer_ref[...])
    wide = jnp.concatenate([high, low, high], axis=1)
    x_rows = x_ref.reshape(runs * states, lanes)
    out_rows = out_ref.reshape(runs * states, lanes)
    for s in range(0, states, 2):
        x = jnp.concatenate(
            [x_rows[pl.ds(s + i, runs, stride=states), :] for i in range(2)], axis=1
        )
        mean = jnp.sum(x, axis=0, keepdims=True) * (1.0 / runs)
        x_high, x_low = halves(x - mean)
        out = mean + fast_dot(wide, jnp.concatenate([x_high, x_high, x_low], axis=0))
        for i in range(2):
            out_rows[pl.ds(s + i, runs, stride=states), :] = out[:, i * lanes : (i + 1) * lanes]


def apply_mixer(mixer, x):
    runs, states, lanes = x.shape
    chunk = 8
    block = pl.BlockSpec((runs, chunk, lanes), lambda g: (0, g, 0))
    return pl.pallas_call(
        apply_kernel,
        grid=(states // chunk,),
        in_specs=[pl.BlockSpec((runs, runs), lambda g: (0, 0)), block],
        out_specs=block,
        out_shape=jax.ShapeDtypeStruct(x.shape, jnp.float32),
        compiler_params=pltpu.CompilerParams(vmem_limit_bytes=VMEM_LIMIT),
        name="apply",
    )(mixer, x)


def unpack_kernel(x_ref, out_ref):
    for b in range(x_ref.shape[0]):
        out_ref[:, :, b * BL : (b + 1) * BL] = x_ref[b]


def unpack(x):
    blocks, m, s, lanes = x.shape
    return pl.pallas_call(
        unpack_kernel,
        grid=(m // 2,),
        in_specs=[pl.BlockSpec((blocks, 2, s, lanes), lambda g: (0, g, 0, 0))],
        out_specs=pl.BlockSpec((2, s, blocks * lanes), lambda g: (g, 0, 0)),
        out_shape=jax.ShapeDtypeStruct((m, s, blocks * lanes), jnp.float32),
        compiler_params=pltpu.CompilerParams(vmem_limit_bytes=VMEM_LIMIT),
        name="unpack",
    )(x)


def butterfly_sum(x, axes):
    for axis in axes:
        size = lax.axis_size(axis)
        step = 1
        while step < size:
            x = x + lax.ppermute(x, axis, [(i, i ^ step) for i in range(size)])
            step *= 2
    return x


def on_device(
    ensemble,
    outgoing_fraction,
    mixing,
    downstream_position,
    obs_index,
    obs_value,
    obs_error,
    obs_count,
):
    m, s, r = ensemble.shape
    blocks = r // BL
    cap = obs_index.shape[1]
    mem_index = lax.axis_index("mem")
    reaches = lax.axis_size("reach")
    positions = downstream_position.reshape(1, r)
    slots = obs_index.reshape(blocks, 1, cap)
    values = lax.dynamic_slice_in_dim(obs_value, mem_index, 1, 0)
    errors = lax.dynamic_slice_in_dim(obs_error, mem_index, 1, 0)
    count = lax.dynamic_slice_in_dim(obs_count, mem_index, 1, 0).reshape(1, 1)

    routing = (ensemble, outgoing_fraction, positions, mixing)
    route = [(i, i + 1) for i in range(reaches - 1)]
    halo = [lax.ppermute(c, "reach", route) for c in edge_carries(*routing, blocks // 2 - 1)]
    inner = edge_carries(*routing, 0)
    held = forecast_blocks(*routing, slots, *inner, 2, blocks - 2)
    forecast, seen = forecast_blocks(*routing, slots, *halo, 0, 2, held)

    seen = lax.all_to_all(seen, "mem", split_axis=0, concat_axis=0, tiled=True)
    gathered = lax.all_to_all(forecast, "mem", split_axis=0, concat_axis=0, tiled=True)
    runs = blocks * m
    gram, right, sums = innovations(seen.reshape(runs, cap), values, errors, count)
    sums = butterfly_sum(sums, ("reach", "mem"))
    mixer = mixer_of(gram, right, sums)
    updated = apply_mixer(mixer, gathered.reshape(runs, s, BL))
    returned = lax.all_to_all(
        updated.reshape(blocks, m, s, BL), "mem", split_axis=0, concat_axis=0, tiled=True
    )
    return unpack(returned)


def solution(mesh):
    placed = (
        P("mem", None, "reach"),
        P(None, "reach"),
        P(),
        P("reach"),
        P("reach", None),
        P("reach", None),
        P("reach", None),
        P("reach"),
    )
    return jax.shard_map(
        on_device, mesh=mesh, in_specs=placed, out_specs=P("mem", None, "reach"), check_vma=False
    )
```

time: 531 us -> 276 us (0.52); the launches traced: 522 us -> 273 us
  local copies, waits for them, and re-layouts: 111 us -> 6.06 us
  other arithmetic: 89.3 us -> 0.7 us
  blocking collectives: 165 us -> 90.7 us
  Pallas kernels: 0 us -> 70.1 us
  matrix products: 44.2 us -> 0 us
  waiting for transfers between devices: 95.3 us -> 57.2 us
  starting transfers between devices: 13 us -> 47.7 us
    all_to_all x1, waiting for transfers between devices: 92.2 us -> 0.01 us  [on_device(): lax.all_to_all(forecast, 'mem', split_axis=0, concat_axis=0, tiled=True)]
    psum x1 -> x0, blocking collectives: 88.4 us -> none  [transform_weights(): lax.psum((statistic, count.astype(jnp.float32)), ('mem', 'reach'))]
    pallas_call x0 -> x8, Pallas kernels: none -> 70.1 us  [the longest x1 28 us: mixer_of(): pl.pallas_call(mixer_kernel, in_specs=[vmem] * 3, out_specs=vmem, out_sha...]
    another operation x10 -> x0, other arithmetic: 54.6 us -> none  [the longest x7 34.6 us: transform_weights(): lower_factor = jnp.linalg.cholesky(system)]
    ppermute x2 -> x10, waiting for transfers between devices: 3.07 us -> 57.2 us  [the longest x8 57.2 us: butterfly_sum(): x = x + lax.ppermute(x, axis, [(i, i ^ step) for i in range(size)])]
    unnamed x19 -> x14, local copies, waits for them, and re-layouts: 44.4 us -> 4.08 us
    ppermute x2 -> x10, starting transfers between devices: 5.33 us -> 42.9 us  [the longest x8 38 us: butterfly_sum(): x = x + lax.ppermute(x, axis, [(i, i ^ step) for i in range(size)])]
    all_to_all x4 -> x0, local copies, waits for them, and re-layouts: 30.3 us -> none  [the longest x3 26.8 us: on_device(): lax.all_to_all(prior_estimate, 'mem', split_axis=2, concat_axis=0, tiled=...]
  transfers between devices with their start and end apart: 3 -> 11, of which waited for: 3 -> 8; matrix products, arithmetic and copies ran while one was open for 2% -> 1% of each run, Pallas kernels for 0% -> 18%
where the time goes in v1:
time: 276 us; the launch traced here: 273 us
  blocking collectives  90.7 us (33%)
  Pallas kernels  70.1 us (25%)
  waiting for transfers between devices  57.2 us (21%)
  starting transfers between devices  47.7 us (17%)
  local copies, waits for them, and re-layouts  6.06 us (2%)
    all_to_all x1, blocking collectives, on_device(): lax.all_to_all(updated.reshape(blocks, m, s, BL), 'mem', split_axis=0, co...  75.1 us
    ppermute x8, waiting for transfers between devices, butterfly_sum(): x = x + lax.ppermute(x, axis, [(i, i ^ step) for i in range(size)])  57.2 us
    ppermute x8, starting transfers between devices, butterfly_sum(): x = x + lax.ppermute(x, axis, [(i, i ^ step) for i in range(size)])  38 us
    pallas_call x1, Pallas kernels, mixer_of(): pl.pallas_call(mixer_kernel, in_specs=[vmem] * 3, out_specs=vmem, out_sha...  28 us
    pallas_call x2, Pallas kernels, forecast_blocks(): pl.pallas_call(forecast_kernel, grid=(number,), in_specs=in_specs, out_sp...  18.5 us
    all_to_all x1, blocking collectives, on_device(): seen = lax.all_to_all(seen, 'mem', split_axis=0, concat_axis=0, tiled=True)  15.6 us
    pallas_call x1, Pallas kernels, apply_mixer(): pl.pallas_call(apply_kernel, grid=(states // chunk,), in_specs=[pl.BlockS...  8.67 us
    pallas_call x1, Pallas kernels, unpack(): pl.pallas_call(unpack_kernel, grid=(m // 2,), in_specs=[pl.BlockSpec((blo...  7.88 us
  transfers between devices with their start and end apart: 11, of which 8 were waited for; matrix products, arithmetic and copies ran while one was open for 1% of the time, Pallas kernels for 18%

profile of v1, /device:TPU:192, one launch (start us, length us, event | category | flops | bytes accessed | tf_op | source)
XLA Modules:
  0.0 272.6 jit_solution(7717562042939320627)
XLA Ops:
  0.0 0.0 copy-start
  0.0 1.0 copy-done
  1.0 0.0 copy-start.1
  1.0 0.7 copy-done.1
  1.7 0.0 copy-start.3
  1.7 0.7 copy-done.3
  2.4 2.0 edge.2
  4.5 1.9 collective-permute-start
  6.4 3.0 %collective-permute-start.1 = (f32[16,48,128]{2,1,0:T(8,128)S(1)}, f32[16,48,128]{2,1,0:T(8,128)S(1)}, u32[]{:S(2)}, u32[]{:S(2)}) collective-permute-start(f32[16,48,128]{2,1,0:T(8,128)S(1)} %get-tuple-element.17), channel_id=1, source_target_pairs={{0,1},{1,2},{2,3},{3,4},{4,5},{5,6},{6,7},{7,8},{8,9},{9,10},{10,1... | collective-permute-start | bytes 1179656 | tf_op jit(solution)/shard_map/ppermute | solution.py:353
  9.4 2.0 edge.3
  11.4 0.0 copy-done.5
  11.4 14.9 %forecast.2 = (f32[16,16,48,128]{3,2,1,0:T(8,128)}, f32[16,16,256]{2,1,0:T(8,128)S(1)}) custom-call(f32[16,48,2048]{2,1,0:T(8,128)} %x_ref.7, f32[48,2048]{1,0:T(8,128)S(1)} %copy-done, s32[1,2048]{1,0:T(1,128)S(1)} %bitcast.7, f32[48,48]{1,0:T(8,128)S(1)} %copy-done.1, s32[16,1,256]{2,1,0:T(1,128)S(1)} %reshape.19.slot_ref, ...), custom_call_target="tpu_custom_call" | custom-call | tf_op jit(solution)/shard_map/forecast/pallas_call | solution.py:155
  26.4 0.0 collective-permute-done.c1_in
  26.4 0.0 collective-permute-done.1.c2_in
  26.4 3.6 %forecast.3 = (f32[16,16,48,128]{3,2,1,0:T(8,128)}, f32[16,16,256]{2,1,0:T(8,128)S(1)}) custom-call(f32[16,48,2048]{2,1,0:T(8,128)} %x_ref.7, f32[48,2048]{1,0:T(8,128)S(1)} %copy-done, s32[1,2048]{1,0:T(1,128)S(1)} %bitcast.8, f32[48,48]{1,0:T(8,128)S(1)} %copy-done.1, ...), custom_call_target="tpu_custom_call", output_to_operand_aliasing={{0}: (7, {}), {1}: (8, {})} | custom-call | tf_op jit(solution)/shard_map/forecast/pallas_call | solution.py:155
  30.0 15.6 %all_to_all.15 = f32[16,16,256]{2,1,0:T(8,128)} all-to-all(f32[16,16,256]{2,1,0:T(8,128)S(1)} %get-tuple-element.22), channel_id=1, replica_groups=mesh['mem'=16,'reach'=16] {'mem'}, dimensions={0} | all-to-all | bytes 524288 | tf_op jit(solution)/shard_map/all_to_all | solution.py:358
  45.6 0.0 copy-start.6
  45.6 4.8 %all-to-all-start.1 = ((f32[16,16,48,128]{3,2,1,0:T(8,128)}), f32[16,16,48,128]{3,2,1,0:T(8,128)}, u32[]{:S(2)}, u32[]{:S(2)}) async-start(f32[16,16,48,128]{3,2,1,0:T(8,128)} %get-tuple-element.26), calls=%async_computation.1 | async-start | bytes 12582912 | tf_op jit(solution)/shard_map/all_to_all | solution.py:359
  50.4 0.0 copy-done.6
  50.4 0.7 dynamic_slice.11
  51.1 1.3 constant_dynamic-slice_fusion
  52.4 3.0 %innovation.1 = (f32[256,256]{1,0:T(8,128)}, f32[8,256]{1,0:T(8,128)}, f32[8,128]{1,0:T(8,128)}) custom-call(f32[256,256]{1,0:T(8,128)} %bitcast.10, f32[1,256]{1,0:T(1,128)} %get-tuple-element.28.values_ref, f32[1,256]{1,0:T(1,128)} %get-tuple-element.27.errors_ref, s32[1,1]{1,0:T(1,128)} %bitcast.2.count_ref), custom_call_target="tpu_custom_call" | custom-call | tf_op jit(solution)/shard_map/innovation/pallas_call | solution.py:201
  55.4 0.0 collective-permute-start.2
  55.4 1.4 collective-permute-done.2
  56.7 0.7 add.30
  57.4 0.0 collective-permute-start.3
  57.4 3.6 %collective-permute-done.3 = f32[8,128]{1,0:T(8,128)S(1)} collective-permute-done((f32[8,128]{1,0:T(8,128)S(1)}, f32[8,128]{1,0:T(8,128)S(1)}, u32[]{:S(2)}, u32[]{:S(2)}) %collective-permute-start.3) | collective-permute-done | bytes 4128 | tf_op jit(solution)/shard_map/ppermute | solution.py:325
  61.0 1.4 collective-permute-start.4
  62.5 3.1 %collective-permute-done.4 = f32[8,128]{1,0:T(8,128)S(1)} collective-permute-done((f32[8,128]{1,0:T(8,128)S(1)}, f32[8,128]{1,0:T(8,128)S(1)}, u32[]{:S(2)}, u32[]{:S(2)}) %collective-permute-start.4) | collective-permute-done | bytes 4128 | tf_op jit(solution)/shard_map/ppermute | solution.py:325
  65.5 2.5 collective-permute-start.5
  68.1 5.0 %collective-permute-done.5 = f32[8,128]{1,0:T(8,128)S(1)} collective-permute-done((f32[8,128]{1,0:T(8,128)S(1)}, f32[8,128]{1,0:T(8,128)S(1)}, u32[]{:S(2)}, u32[]{:S(2)}) %collective-permute-start.5) | collective-permute-done | bytes 4128 | tf_op jit(solution)/shard_map/ppermute | solution.py:325
  73.1 1.7 collective-permute-start.6
  74.8 27.3 %collective-permute-done.6 = f32[8,128]{1,0:T(8,128)S(1)} collective-permute-done((f32[8,128]{1,0:T(8,128)S(1)}, f32[8,128]{1,0:T(8,128)S(1)}, u32[]{:S(2)}, u32[]{:S(2)}) %collective-permute-start.6) | collective-permute-done | bytes 4128 | tf_op jit(solution)/shard_map/ppermute | solution.py:325
  102.1 0.0 collective-permute-start.7
  102.1 5.3 %collective-permute-done.7 = f32[8,128]{1,0:T(8,128)S(1)} collective-permute-done((f32[8,128]{1,0:T(8,128)S(1)}, f32[8,128]{1,0:T(8,128)S(1)}, u32[]{:S(2)}, u32[]{:S(2)}) %collective-permute-start.7) | collective-permute-done | bytes 4128 | tf_op jit(solution)/shard_map/ppermute | solution.py:325
  107.4 32.2 %collective-permute-start.8 = (f32[8,128]{1,0:T(8,128)S(1)}, f32[8,128]{1,0:T(8,128)S(1)}, u32[]{:S(2)}, u32[]{:S(2)}) collective-permute-start(f32[8,128]{1,0:T(8,128)S(1)} %add.35), channel_id=1, source_target_pairs={{0,64},{16,80},{32,96},{48,112},{64,0},{80,16},{96,32},{112,48},{1... | collective-permute-start | bytes 12296 | tf_op jit(solution)/shard_map/ppermute | solution.py:325
  139.6 6.5 %collective-permute-done.8 = f32[8,128]{1,0:T(8,128)S(1)} collective-permute-done((f32[8,128]{1,0:T(8,128)S(1)}, f32[8,128]{1,0:T(8,128)S(1)}, u32[]{:S(2)}, u32[]{:S(2)}) %collective-permute-start.8) | collective-permute-done | bytes 4128 | tf_op jit(solution)/shard_map/ppermute | solution.py:325
  146.1 0.0 collective-permute-start.9
  146.1 5.1 %collective-permute-done.9 = f32[8,128]{1,0:T(8,128)S(1)} collective-permute-done((f32[8,128]{1,0:T(8,128)S(1)}, f32[8,128]{1,0:T(8,128)S(1)}, u32[]{:S(2)}, u32[]{:S(2)}) %collective-permute-start.9) | collective-permute-done | bytes 4128 | tf_op jit(solution)/shard_map/ppermute | solution.py:325
  151.2 0.0 copy-start.2
  151.2 0.9 copy-done.2
  152.2 0.0 copy-start.4
  152.2 0.7 copy-done.4
  152.9 28.0 %mixer.1.mixer_ref = f32[256,256]{1,0:T(8,128)S(1)} custom-call(f32[256,256]{1,0:T(8,128)S(1)} %copy-done.2, f32[8,256]{1,0:T(8,128)S(1)} %copy-done.4, f32[8,128]{1,0:T(8,128)S(1)} %add.37.sums_ref), custom_call_target="tpu_custom_call" | custom-call | tf_op jit(solution)/shard_map/mixer/pallas_call | solution.py:260
  180.9 0.0 all-to-all-done.1
  180.9 8.7 %apply.1 = f32[256,48,128]{2,1,0:T(8,128)} custom-call(f32[256,256]{1,0:T(8,128)S(1)} %mixer.1.mixer_ref, f32[256,48,128]{2,1,0:T(8,128)} %bitcast.3.x_ref), custom_call_target="tpu_custom_call" | custom-call | tf_op jit(solution)/shard_map/apply/pallas_call | solution.py:291
  189.6 75.1 %all_to_all.16.x_ref = f32[16,16,48,128]{3,2,1,0:T(8,128)} all-to-all(f32[16,16,48,128]{3,2,1,0:T(8,128)} %bitcast.9), channel_id=1, replica_groups=mesh['mem'=16,'reach'=16] {'mem'}, dimensions={0} | all-to-all | bytes 12582912 | tf_op jit(solution)/shard_map/all_to_all | solution.py:365
  264.7 7.9 %unpack.1 = f32[16,48,2048]{2,1,0:T(8,128)} custom-call(f32[16,16,48,128]{3,2,1,0:T(8,128)} %all_to_all.16.x_ref), custom_call_target="tpu_custom_call" | custom-call | tf_op jit(solution)/shard_map/unpack/pallas_call | solution.py:309
  (9 shorter events, 0.0 us)
Async XLA Ops:
  0.0 1.0 copy-start
  1.0 0.7 copy-start.1
  1.7 0.7 copy-start.3
  2.4 9.0 %copy-start.5 = (s32[16,256]{1,0:T(8,128)S(1)}, s32[16,256]{1,0:T(8,128)}, u32[]{:S(2)}) copy-start(s32[16,256]{1,0:T(8,128)} %param.12) | copy-start | bytes 49156
  4.5 21.9 %collective-permute-start = (f32[16,48,128]{2,1,0:T(8,128)S(1)}, f32[16,48,128]{2,1,0:T(8,128)S(1)}, u32[]{:S(2)}, u32[]{:S(2)}) collective-permute-start(f32[16,48,128]{2,1,0:T(8,128)S(1)} %get-tuple-element.16), channel_id=1, source_target_pairs={{0,1},{1,2},{2,3},{3,4},{4,5},{5,6},{6,7},{7,8},{8,9},{9,10},{10,1... | collective-permute-start | bytes 1179656 | tf_op jit(solution)/shard_map/ppermute | solution.py:353
  6.4 20.0 %collective-permute-start.1 = (f32[16,48,128]{2,1,0:T(8,128)S(1)}, f32[16,48,128]{2,1,0:T(8,128)S(1)}, u32[]{:S(2)}, u32[]{:S(2)}) collective-permute-start(f32[16,48,128]{2,1,0:T(8,128)S(1)} %get-tuple-element.17), channel_id=1, source_target_pairs={{0,1},{1,2},{2,3},{3,4},{4,5},{5,6},{6,7},{7,8},{8,9},{9,10},{10,1... | collective-permute-start | bytes 1179656 | tf_op jit(solution)/shard_map/ppermute | solution.py:353
  45.6 4.8 %copy-start.6 = (s32[16]{0:T(128)S(1)}, s32[16]{0:T(128)}, u32[]{:S(2)}) copy-start(s32[16]{0:T(128)} %param.15) | copy-start | bytes 196
  45.6 135.3 %all-to-all-start.1 = ((f32[16,16,48,128]{3,2,1,0:T(8,128)}), f32[16,16,48,128]{3,2,1,0:T(8,128)}, u32[]{:S(2)}, u32[]{:S(2)}) async-start(f32[16,16,48,128]{3,2,1,0:T(8,128)} %get-tuple-element.26), calls=%async_computation.1 | async-start | bytes 12582912 | tf_op jit(solution)/shard_map/all_to_all | solution.py:359
  55.4 1.4 collective-permute-start.2
  57.4 3.6 %collective-permute-start.3 = (f32[8,128]{1,0:T(8,128)S(1)}, f32[8,128]{1,0:T(8,128)S(1)}, u32[]{:S(2)}, u32[]{:S(2)}) collective-permute-start(f32[8,128]{1,0:T(8,128)S(1)} %add.30), channel_id=1, source_target_pairs={{0,2},{1,3},{2,0},{3,1},{4,6},{5,7},{6,4},{7,5},{8,10},{9,11},{10,... | collective-permute-start | bytes 12296 | tf_op jit(solution)/shard_map/ppermute | solution.py:325
  61.0 4.5 %collective-permute-start.4 = (f32[8,128]{1,0:T(8,128)S(1)}, f32[8,128]{1,0:T(8,128)S(1)}, u32[]{:S(2)}, u32[]{:S(2)}) collective-permute-start(f32[8,128]{1,0:T(8,128)S(1)} %add.31), channel_id=1, source_target_pairs={{0,4},{1,5},{2,6},{3,7},{4,0},{5,1},{6,2},{7,3},{8,12},{9,13},{10,... | collective-permute-start | bytes 12296 | tf_op jit(solution)/shard_map/ppermute | solution.py:325
  65.5 7.5 %collective-permute-start.5 = (f32[8,128]{1,0:T(8,128)S(1)}, f32[8,128]{1,0:T(8,128)S(1)}, u32[]{:S(2)}, u32[]{:S(2)}) collective-permute-start(f32[8,128]{1,0:T(8,128)S(1)} %add.32), channel_id=1, source_target_pairs={{0,8},{1,9},{2,10},{3,11},{4,12},{5,13},{6,14},{7,15},{8,0},{9,1},... | collective-permute-start | bytes 12296 | tf_op jit(solution)/shard_map/ppermute | solution.py:325
  73.1 29.1 %collective-permute-start.6 = (f32[8,128]{1,0:T(8,128)S(1)}, f32[8,128]{1,0:T(8,128)S(1)}, u32[]{:S(2)}, u32[]{:S(2)}) collective-permute-start(f32[8,128]{1,0:T(8,128)S(1)} %add.33), channel_id=1, source_target_pairs={{0,16},{16,0},{32,48},{48,32},{64,80},{80,64},{96,112},{112,96},{1... | collective-permute-start | bytes 12296 | tf_op jit(solution)/shard_map/ppermute | solution.py:325
  102.1 5.3 %collective-permute-start.7 = (f32[8,128]{1,0:T(8,128)S(1)}, f32[8,128]{1,0:T(8,128)S(1)}, u32[]{:S(2)}, u32[]{:S(2)}) collective-permute-start(f32[8,128]{1,0:T(8,128)S(1)} %add.34), channel_id=1, source_target_pairs={{0,32},{16,48},{32,0},{48,16},{64,96},{80,112},{96,64},{112,80},{1... | collective-permute-start | bytes 12296 | tf_op jit(solution)/shard_map/ppermute | solution.py:325
  107.4 38.7 %collective-permute-start.8 = (f32[8,128]{1,0:T(8,128)S(1)}, f32[8,128]{1,0:T(8,128)S(1)}, u32[]{:S(2)}, u32[]{:S(2)}) collective-permute-start(f32[8,128]{1,0:T(8,128)S(1)} %add.35), channel_id=1, source_target_pairs={{0,64},{16,80},{32,96},{48,112},{64,0},{80,16},{96,32},{112,48},{1... | collective-permute-start | bytes 12296 | tf_op jit(solution)/shard_map/ppermute | solution.py:325
  146.1 5.1 %collective-permute-start.9 = (f32[8,128]{1,0:T(8,128)S(1)}, f32[8,128]{1,0:T(8,128)S(1)}, u32[]{:S(2)}, u32[]{:S(2)}) collective-permute-start(f32[8,128]{1,0:T(8,128)S(1)} %add.36), channel_id=1, source_target_pairs={{0,128},{16,144},{32,160},{48,176},{64,192},{80,208},{96,224},{112... | collective-permute-start | bytes 12296 | tf_op jit(solution)/shard_map/ppermute | solution.py:325
  151.2 1.0 copy-start.2
  152.2 0.7 copy-start.4

commit v2 on v1

--- a/solution.py
+++ b/solution.py
@@ -59,23 +59,26 @@
     mix3_ref[...] = jnp.concatenate([high, high, low], axis=1)
 
 
-def edge_kernel(x_ref, f_ref, v_ref, mixing_ref, c1_ref, c2_ref, mix3_ref):
-    prepare_mixing(mixing_ref, mix3_ref)
+def edge_of(x_ref, f_ref, v_ref, mix3):
     outflow = f_ref[:, :BL][None] * x_ref[:, :, :BL]
-    c1_before = select(outflow, selector(v_ref[:, :BL], 2 * BL))[:, :, BL:]
+    arriving = select(outflow, selector(v_ref[:, :BL], 2 * BL))[:, :, BL:]
     table = selector(v_ref[:, BL:], 2 * BL)
     x = x_ref[:, :, BL:]
     f = f_ref[:, BL:][None]
     outflow = f * x
     routed = select(outflow, table)
-    c1_ref[...] = routed[:, :, BL:]
-    x = x - outflow + (routed[:, :, :BL] + c1_before) + blend(x, mix3_ref[...])
-    c2_ref[...] = select(f * x, table)[:, :, BL:]
-
-
-def edge_carries(ensemble, fraction, positions, mixing, pair):
-    m, s, _ = ensemble.shape
-    carry = jax.ShapeDtypeStruct((m, s, BL), jnp.float32)
+    x = x - outflow + (routed[:, :, :BL] + arriving) + blend(x, mix3)
+    return routed[:, :, BL:], select(f * x, table)[:, :, BL:]
+
+
+def edge_kernel(x_ref, f_ref, v_ref, mixing_ref, carry_ref, mix3_ref):
+    prepare_mixing(mixing_ref, mix3_ref)
+    carry_ref[0], carry_ref[1] = edge_of(x_ref, f_ref, v_ref, mix3_ref[...])
+
+
+def edge_carries(ensemble, fraction, positions, mixing):
+    m, s, r = ensemble.shape
+    pair = r // (2 * BL) - 1
     return pl.pallas_call(
         edge_kernel,
         grid=(1,),
@@ -85,43 +88,65 @@
             pl.BlockSpec((1, 2 * BL), lambda g: (0, pair)),
             pl.BlockSpec((s, s), lambda g: (0, 0)),
         ],
-        out_specs=[pl.BlockSpec((m, s, BL), lambda g: (0, 0, 0))] * 2,
-        out_shape=[carry, carry],
+        out_specs=pl.BlockSpec((2, m, s, BL), lambda g: (0, 0, 0, 0)),
+        out_shape=jax.ShapeDtypeStruct((2, m, s, BL), jnp.float32),
         scratch_shapes=[pltpu.VMEM((s, 3 * s), jnp.bfloat16)],
         compiler_params=pltpu.CompilerParams(vmem_limit_bytes=VMEM_LIMIT),
         name="edge",
     )(ensemble, fraction, positions, mixing)
 
 
-def forecast_kernel(
-    x_ref, f_ref, v_ref, mixing_ref, slot_ref, c1_in, c2_in, *rest
-):
-    out_ref, seen_ref, mix3_ref, c1_ref, c2_ref = rest[-5:]
-
-    @pl.when(pl.program_id(0) == 0)
-    def _():
-        prepare_mixing(mixing_ref, mix3_ref)
-        c1_ref[...] = c1_in[...]
-        c2_ref[...] = c2_in[...]
-
+def forecast_step(x_ref, f_ref, v_ref, slot_ref, out_ref, pack_ref, mix3_ref, carry_ref, block):
     table = selector(v_ref[...], 2 * BL)
     f = f_ref[...][None]
     x = x_ref[...]
-    for carry in (c1_ref, c2_ref):
+    for step in range(2):
         outflow = f * x
         routed = select(outflow, table)
-        x = x - outflow + (routed[:, :, :BL] + carry[...]) + blend(x, mix3_ref[...])
-        carry[...] = routed[:, :, BL:]
+        x = x - outflow + (routed[:, :, :BL] + carry_ref[step]) + blend(x, mix3_ref[...])
+        carry_ref[step] = routed[:, :, BL:]
     out_ref[...] = x[None]
-    slots = slot_ref[0]
+    slots = slot_ref[pl.ds(block, 1), :]
     m, s, _ = x.shape
     state_of = slots // BL
-    reach_of = slots - state_of * BL
-    hot_reach = selector_columns(reach_of)
-    looked = select(x, hot_reach)
+    looked = select(x, selector_columns(slots - state_of * BL))
     rows = lax.broadcasted_iota(jnp.int32, (s, slots.shape[1]), 0)
     hot_state = (rows == state_of).astype(jnp.float32)
-    seen_ref[...] = jnp.sum(looked * hot_state[None], axis=1)[None]
+    seen = jnp.sum(looked * hot_state[None], axis=1)
+    mean = jnp.sum(seen, axis=0, keepdims=True) * (1.0 / m)
+    pert = seen - mean
+    moment = jnp.sum(pert * pert, axis=0, keepdims=True)
+    blocks = pack_ref.shape[0]
+    pack_ref[pl.ds(block, 1), :m, :] = seen[None]
+    pack_ref[:, pl.ds(m + block, 1), :] = jnp.broadcast_to(mean[None], (blocks,) + mean.shape)
+    pack_ref[:, pl.ds(m + blocks + block, 1), :] = jnp.broadcast_to(moment[None], (blocks,) + mean.shape)
+
+
+def inner_kernel(
+    x2_ref, f2_ref, v2_ref, x_ref, f_ref, v_ref, mixing_ref, slot_ref, out_ref, pack_ref, mix3_ref, carry_ref
+):
+    step = pl.program_id(0)
+
+    @pl.when(step == 0)
+    def _():
+        prepare_mixing(mixing_ref, mix3_ref)
+        carry_ref[0], carry_ref[1] = edge_of(x2_ref, f2_ref, v2_ref, mix3_ref[...])
+
+    forecast_step(x_ref, f_ref, v_ref, slot_ref, out_ref, pack_ref, mix3_ref, carry_ref, step + 2)
+
+
+def outer_kernel(
+    halo_ref, pack_in, held_ref, x_ref, f_ref, v_ref, mixing_ref, slot_ref, out_ref, pack_ref, mix3_ref, carry_ref
+):
+    step = pl.program_id(0)
+
+    @pl.when(step == 0)
+    def _():
+        prepare_mixing(mixing_ref, mix3_ref)
+        carry_ref[...] = halo_ref[...]
+        pack_ref[...] = pack_in[...]
+
+    forecast_step(x_ref, f_ref, v_ref, slot_ref, out_ref, pack_ref, mix3_ref, carry_ref, step)
 
 
 def selector_columns(reach_row):
@@ -132,75 +157,95 @@
     return jnp.concatenate([hot, hot], axis=1)
 
 
-def forecast_blocks(ensemble, fraction, positions, mixing, slots, c1, c2, first, number, held=None):
+def forecast_blocks(kernel, first, number, lead, lead_specs, ensemble, fraction, positions, mixing, slots, aliases):
     m, s, r = ensemble.shape
-    blocks = r // BL
-    cap = slots.shape[-1]
+    blocks, cap = slots.shape
     whole = lambda *shape: pl.BlockSpec(shape, lambda g: (0,) * len(shape))
-    in_specs = [
-        pl.BlockSpec((m, s, BL), lambda g: (0, 0, g + first)),
-        pl.BlockSpec((s, BL), lambda g: (0, g + first)),
-        pl.BlockSpec((1, BL), lambda g: (0, g + first)),
-        whole(s, s),
-        pl.BlockSpec((1, 1, cap), lambda g: (g + first, 0, 0)),
-        whole(m, s, BL),
-        whole(m, s, BL),
-    ]
-    operands = [ensemble, fraction, positions, mixing, slots, c1, c2]
-    aliases = {}
-    if held is not None:
-        in_specs += [pl.BlockSpec(memory_space=pl.ANY)] * 2
-        operands += list(held)
-        aliases = {7: 0, 8: 1}
+    pack = (blocks, m + 2 * blocks, cap)
     return pl.pallas_call(
-        forecast_kernel,
+        kernel,
         grid=(number,),
-        in_specs=in_specs,
-        out_specs=[
-            pl.BlockSpec((1, m, s, BL), lambda g: (g + first, 0, 0, 0)),
-            pl.BlockSpec((1, m, cap), lambda g: (g + first, 0, 0)),
+        in_specs=lead_specs
+        + [
+            pl.BlockSpec((m, s, BL), lambda g: (0, 0, g + first)),
+            pl.BlockSpec((s, BL), lambda g: (0, g + first)),
+            pl.BlockSpec((1, BL), lambda g: (0, g + first)),
+            whole(s, s),
+            whole(blocks, cap),
         ],
+        out_specs=[pl.BlockSpec((1, m, s, BL), lambda g: (g + first, 0, 0, 0)), whole(*pack)],
         out_shape=[
             jax.ShapeDtypeStruct((blocks, m, s, BL), jnp.float32),
-            jax.ShapeDtypeStruct((blocks, m, cap), jnp.float32),
+            jax.ShapeDtypeStruct(pack, jnp.float32),
         ],
         scratch_shapes=[
             pltpu.VMEM((s, 3 * s), jnp.bfloat16),
-            pltpu.VMEM((m, s, BL), jnp.float32),
-            pltpu.VMEM((m, s, BL), jnp.float32),
+            pltpu.VMEM((2, m, s, BL), jnp.float32),
         ],
         input_output_aliases=aliases,
         compiler_params=pltpu.CompilerParams(vmem_limit_bytes=VMEM_LIMIT),
-        name="forecast",
-    )(*operands)
-
-
-def innovation_kernel(seen_ref, values_ref, errors_ref, count_ref, gram_ref, right_ref, sums_ref):
-    seen = seen_ref[...]
-    runs, cap = seen.shape
-    count = count_ref[0, 0]
-    live = (lax.broadcasted_iota(jnp.int32, (1, cap), 1) < count).astype(jnp.float32)
+        name=kernel.__name__,
+    )(*lead, ensemble, fraction, positions, mixing, slots)
+
+
+def forecast(ensemble, fraction, positions, mixing, slots, halo):
+    m, s, r = ensemble.shape
+    blocks, cap = slots.shape
+    whole = lambda *shape: pl.BlockSpec(shape, lambda g: (0,) * len(shape))
+    rest = (ensemble, fraction, positions, mixing, slots)
+    out, pack = forecast_blocks(
+        inner_kernel, 2, blocks - 2, (ensemble, fraction, positions),
+        [whole(m, s, 2 * BL), whole(s, 2 * BL), whole(1, 2 * BL)], *rest, {},
+    )
+    return forecast_blocks(
+        outer_kernel, 0, 2, (halo, pack, out),
+        [whole(2, m, s, BL), whole(*pack.shape), pl.BlockSpec(memory_space=pl.ANY)], *rest, {2: 0},
+    )
+
+
+def innovation_kernel(
+    block_ref, own_count_ref, pack_ref, values_ref, errors_ref, count_ref, gram_ref, right_ref, sums_ref
+):
+    blocks, cap = values_ref.shape
+    sources = pack_ref.shape[0]
+    m = pack_ref.shape[1] - 2 * blocks
+    runs = sources * m
+    means = pack_ref[:, m : m + blocks, :]
+    mean = jnp.sum(means, axis=0) * (1.0 / sources)
+    drift = means - mean[None]
+    moment = jnp.sum(pack_ref[:, m + blocks :, :], axis=0) + m * jnp.sum(drift * drift, axis=0)
+    spread = moment / (runs - 1)
+    lanes = lax.broadcasted_iota(jnp.int32, (blocks, cap), 1)
+    live = (lanes < count_ref[...]).astype(jnp.float32)
+    departure = values_ref[...] - mean
+    errors = errors_ref[...]
+    terms = live * departure * departure / (errors * errors + spread)
+    statistic = jnp.sum(jnp.sum(terms, axis=0, keepdims=True), axis=1, keepdims=True)
+    total = jnp.sum(count_ref[...].astype(jnp.float32), axis=0, keepdims=True)
+    lanes = lax.broadcasted_iota(jnp.int32, sums_ref.shape, 1)
+    sums_ref[...] = jnp.where(lanes < 64, statistic, total)
+
+    own = block_ref[0]
+    seen = pack_ref[:, :m, :].reshape(runs, cap)
     mean = jnp.sum(seen, axis=0, keepdims=True) * (1.0 / runs)
     pert = seen - mean
-    spread = jnp.sum(pert * pert, axis=0, keepdims=True) / (runs - 1)
-    errors = errors_ref[...]
-    departure = values_ref[...] - mean
-    squared = errors * errors
-    statistic = jnp.sum(live * departure * departure / (squared + spread), axis=1, keepdims=True)
-    weight = live / squared
-    weighted = pert * weight
+    errors = errors_ref[pl.ds(own, 1), :]
+    lanes = lax.broadcasted_iota(jnp.int32, (1, cap), 1)
+    live = (lanes < own_count_ref[own]).astype(jnp.float32)
+    weighted = pert * (live / (errors * errors))
+    departure = values_ref[pl.ds(own, 1), :] - mean
     gram_ref[...] = dot(weighted, pert, NT)
     right_ref[...] = dot(jnp.broadcast_to(departure, (8, cap)), weighted, NT)
-    lanes = lax.broadcasted_iota(jnp.int32, sums_ref.shape, 1)
-    sums_ref[...] = jnp.where(lanes < 64, statistic, count.astype(jnp.float32))
-
-
-def innovations(seen, values, errors, count):
-    runs, cap = seen.shape
+
+
+def innovations(block, pack, values, errors, counts):
+    blocks = values.shape[0]
+    runs = pack.shape[0] * (pack.shape[1] - 2 * blocks)
     vmem = pl.BlockSpec(memory_space=pltpu.VMEM)
+    smem = pl.BlockSpec(memory_space=pltpu.SMEM)
     return pl.pallas_call(
         innovation_kernel,
-        in_specs=[vmem, vmem, vmem, pl.BlockSpec(memory_space=pltpu.SMEM)],
+        in_specs=[smem, smem, vmem, vmem, vmem, vmem],
         out_specs=[vmem] * 3,
         out_shape=[
             jax.ShapeDtypeStruct((runs, runs), jnp.float32),
@@ -208,7 +253,7 @@
             jax.ShapeDtypeStruct((8, 128), jnp.float32),
         ],
         name="innovation",
-    )(seen, values, errors, count)
+    )(block, counts, pack, values, errors, counts.reshape(blocks, 1))
 
 
 def small_inverse_factor(a):
@@ -299,24 +344,6 @@
     )(mixer, x)
 
 
-def unpack_kernel(x_ref, out_ref):
-    for b in range(x_ref.shape[0]):
-        out_ref[:, :, b * BL : (b + 1) * BL] = x_ref[b]
-
-
-def unpack(x):
-    blocks, m, s, lanes = x.shape
-    return pl.pallas_call(
-        unpack_kernel,
-        grid=(m // 2,),
-        in_specs=[pl.BlockSpec((blocks, 2, s, lanes), lambda g: (0, g, 0, 0))],
-        out_specs=pl.BlockSpec((2, s, blocks * lanes), lambda g: (g, 0, 0)),
-        out_shape=jax.ShapeDtypeStruct((m, s, blocks * lanes), jnp.float32),
-        compiler_params=pltpu.CompilerParams(vmem_limit_bytes=VMEM_LIMIT),
-        name="unpack",
-    )(x)
-
-
 def butterfly_sum(x, axes):
     for axis in axes:
         size = lax.axis_size(axis)
@@ -339,33 +366,22 @@
 ):
     m, s, r = ensemble.shape
     blocks = r // BL
-    cap = obs_index.shape[1]
-    mem_index = lax.axis_index("mem")
     reaches = lax.axis_size("reach")
-    positions = downstream_position.reshape(1, r)
-    slots = obs_index.reshape(blocks, 1, cap)
-    values = lax.dynamic_slice_in_dim(obs_value, mem_index, 1, 0)
-    errors = lax.dynamic_slice_in_dim(obs_error, mem_index, 1, 0)
-    count = lax.dynamic_slice_in_dim(obs_count, mem_index, 1, 0).reshape(1, 1)
-
-    routing = (ensemble, outgoing_fraction, positions, mixing)
-    route = [(i, i + 1) for i in range(reaches - 1)]
-    halo = [lax.ppermute(c, "reach", route) for c in edge_carries(*routing, blocks // 2 - 1)]
-    inner = edge_carries(*routing, 0)
-    held = forecast_blocks(*routing, slots, *inner, 2, blocks - 2)
-    forecast, seen = forecast_blocks(*routing, slots, *halo, 0, 2, held)
-
-    seen = lax.all_to_all(seen, "mem", split_axis=0, concat_axis=0, tiled=True)
-    gathered = lax.all_to_all(forecast, "mem", split_axis=0, concat_axis=0, tiled=True)
-    runs = blocks * m
-    gram, right, sums = innovations(seen.reshape(runs, cap), values, errors, count)
-    sums = butterfly_sum(sums, ("reach", "mem"))
+    block = lax.axis_index("mem").astype(jnp.int32).reshape(1)
+    routing = (ensemble, outgoing_fraction, downstream_position.reshape(1, r), mixing)
+    halo = lax.ppermute(edge_carries(*routing), "reach", [(i, i + 1) for i in range(reaches - 1)])
+    prior, pack = forecast(*routing, obs_index, halo)
+
+    pack = lax.all_to_all(pack, "mem", split_axis=0, concat_axis=0, tiled=True)
+    gathered = lax.all_to_all(prior, "mem", split_axis=0, concat_axis=0, tiled=True)
+    gram, right, sums = innovations(block, pack, obs_value, obs_error, obs_count)
+    sums = butterfly_sum(sums, ("reach",))
     mixer = mixer_of(gram, right, sums)
-    updated = apply_mixer(mixer, gathered.reshape(runs, s, BL))
+    updated = apply_mixer(mixer, gathered.reshape(blocks * m, s, BL))
     returned = lax.all_to_all(
         updated.reshape(blocks, m, s, BL), "mem", split_axis=0, concat_axis=0, tiled=True
     )
-    return unpack(returned)
+    return jnp.transpose(returned, (1, 2, 0, 3)).reshape(m, s, r)
 
 
 def solution(mesh):

time: 276 us -> 255 us (0.924)
  starting transfers between devices: 47.7 us -> 8.47 us
  blocking collectives: 90.7 us -> 105 us
  waiting for transfers between devices: 57.2 us -> 70.7 us
  Pallas kernels: 70.1 us -> 60.8 us
    all_to_all x1, waiting for transfers between devices: 0.01 us -> 55.4 us  [on_device(): lax.all_to_all(prior, 'mem', split_axis=0, concat_axis=0, tiled=True)]
    ppermute x8 -> x4, waiting for transfers between devices: 57.2 us -> 15.2 us  [butterfly_sum(): x = x + lax.ppermute(x, axis, [(i, i ^ step) for i in range(size)])]
    ppermute x8 -> x4, starting transfers between devices: 38 us -> 1.77 us  [butterfly_sum(): x = x + lax.ppermute(x, axis, [(i, i ^ step) for i in range(size)])]
    pallas_call x4 -> x3, Pallas kernels: 29.4 us -> 22.1 us  [the longest x2 19.6 us: forecast_blocks(): pl.pallas_call(kernel, grid=(number,), in_specs=lead_specs + [pl.BlockSpe...]
    all_to_all x1, blocking collectives: 75.1 us -> 82.3 us  [on_device(): lax.all_to_all(updated.reshape(blocks, m, s, BL), 'mem', split_axis=0, co...]
    all_to_all x1, blocking collectives: 15.6 us -> 22.2 us  [on_device(): pack = lax.all_to_all(pack, 'mem', split_axis=0, concat_axis=0, tiled=True)]
    reshape x1 -> x2, local copies, waits for them, and re-layouts: 0.01 us -> 4.24 us  [the longest x1 3.57 us: on_device(): return jnp.transpose(returned, (1, 2, 0, 3)).reshape(m, s, r)]
    ppermute x2 -> x1, starting transfers between devices: 4.94 us -> 1.92 us  [on_device(): lax.ppermute(edge_carries(*routing), 'reach', [(i, i + 1) for i in range(...]
  transfers between devices with their start and end apart: 11 -> 6, of which waited for: 8 -> 5; matrix products, arithmetic and copies ran while one was open for 1% -> 1% of each run, Pallas kernels for 18% -> 18%
where the time goes in v2:
time: 255 us; the launch traced here: 254 us
  blocking collectives  105 us (41%)
  waiting for transfers between devices  70.7 us (28%)
  Pallas kernels  60.8 us (24%)
  starting transfers between devices  8.47 us (3%)
  local copies, waits for them, and re-layouts  8.32 us (3%)
    all_to_all x1, blocking collectives, on_device(): lax.all_to_all(updated.reshape(blocks, m, s, BL), 'mem', split_axis=0, co...  82.3 us
    all_to_all x1, waiting for transfers between devices, on_device(): lax.all_to_all(prior, 'mem', split_axis=0, concat_axis=0, tiled=True)  55.4 us
    pallas_call x1, Pallas kernels, mixer_of(): pl.pallas_call(mixer_kernel, in_specs=[vmem] * 3, out_specs=vmem, out_sha...  28 us
    all_to_all x1, blocking collectives, on_device(): pack = lax.all_to_all(pack, 'mem', split_axis=0, concat_axis=0, tiled=True)  22.2 us
    pallas_call x2, Pallas kernels, forecast_blocks(): pl.pallas_call(kernel, grid=(number,), in_specs=lead_specs + [pl.BlockSpe...  19.6 us
    ppermute x4, waiting for transfers between devices, butterfly_sum(): x = x + lax.ppermute(x, axis, [(i, i ^ step) for i in range(size)])  15.2 us
    pallas_call x1, Pallas kernels, apply_mixer(): pl.pallas_call(apply_kernel, grid=(states // chunk,), in_specs=[pl.BlockS...  8.66 us
  transfers between devices with their start and end apart: 6, of which 5 were waited for; matrix products, arithmetic and copies ran while one was open for 1% of the time, Pallas kernels for 18%

profile of v2, /device:TPU:192, one launch (start us, length us, event | category | flops | bytes accessed | tf_op | source)
XLA Modules:
  0.0 253.5 jit_solution(9178387484338500310)
XLA Ops:
  0.0 0.0 copy-start
  0.0 1.0 copy-done
  1.0 0.0 copy-start.2
  1.0 0.7 copy-done.2
  1.7 0.0 copy-start.3
  1.7 0.7 copy-done.3
  2.4 0.0 copy-start.4
  2.4 2.0 edge.1
  4.5 1.9 collective-permute-start
  6.4 0.0 copy-done.4
  6.4 16.0 %inner_kernel.1 = (f32[16,16,48,128]{3,2,1,0:T(8,128)}, f32[16,48,256]{2,1,0:T(8,128)S(1)}) custom-call(f32[16,48,2048]{2,1,0:T(8,128)} %x_ref.5, f32[48,2048]{1,0:T(8,128)S(1)} %copy-done, s32[1,2048]{1,0:T(1,128)S(1)} %bitcast.12, f32[16,48,2048]{2,1,0:T(8,128)} %x_ref.5, f32[48,2048]{1,0:T(8,128)S(1)} %copy-done, s32[1,2048]{1,0:T(1,128)S(1)} %bitcast.13, ...), custom_call_target="tpu_custom_call" | custom-call | tf_op jit(solution)/shard_map/inner_kernel/pallas_call | solution.py:165
  22.3 0.0 collective-permute-done.halo_ref
  22.4 3.6 %outer_kernel.1 = (f32[16,16,48,128]{3,2,1,0:T(8,128)}, f32[16,48,256]{2,1,0:T(8,128)S(1)}) custom-call(f32[2,16,48,128]{3,2,1,0:T(8,128)S(1)} %collective-permute-done.halo_ref, f32[16,48,256]{2,1,0:T(8,128)S(1)} %get-tuple-element.12.pack_in, f32[16,16,48,128]{3,2,1,0:T(8,128)} %get-tuple-element.13.held_ref, ...), custom_call_target="tpu_custom_call", output_to_operand_aliasing={{0}: (2, {})} | custom-call | tf_op jit(solution)/shard_map/outer_kernel/pallas_call | solution.py:165
  26.0 22.2 %all_to_all.15.pack_ref = f32[16,48,256]{2,1,0:T(8,128)} all-to-all(f32[16,48,256]{2,1,0:T(8,128)S(1)} %get-tuple-element.14), channel_id=1, replica_groups=mesh['mem'=16,'reach'=16] {'mem'}, dimensions={0} | all-to-all | bytes 1572864 | tf_op jit(solution)/shard_map/all_to_all | solution.py:375
  48.1 0.0 copy-start.6
  48.1 4.8 %all-to-all-start.1 = ((f32[16,16,48,128]{3,2,1,0:T(8,128)}), f32[16,16,48,128]{3,2,1,0:T(8,128)}, u32[]{:S(2)}, u32[]{:S(2)}) async-start(f32[16,16,48,128]{3,2,1,0:T(8,128)} %get-tuple-element.18), calls=%async_computation.1 | async-start | bytes 12582912 | tf_op jit(solution)/shard_map/all_to_all | solution.py:376
  52.9 0.0 copy-done.6
  52.9 0.7 copy.10.count_ref
  53.6 2.5 innovation.1
  56.1 0.0 collective-permute-start.1
  56.1 1.4 collective-permute-done.1
  57.5 0.7 add.12
  58.2 0.0 collective-permute-start.2
  58.2 3.6 %collective-permute-done.2 = f32[8,128]{1,0:T(8,128)S(1)} collective-permute-done((f32[8,128]{1,0:T(8,128)S(1)}, f32[8,128]{1,0:T(8,128)S(1)}, u32[]{:S(2)}, u32[]{:S(2)}) %collective-permute-start.2) | collective-permute-done | bytes 4128 | tf_op jit(solution)/shard_map/ppermute | solution.py:352
  61.8 1.4 collective-permute-start.3
  63.2 3.1 %collective-permute-done.3 = f32[8,128]{1,0:T(8,128)S(1)} collective-permute-done((f32[8,128]{1,0:T(8,128)S(1)}, f32[8,128]{1,0:T(8,128)S(1)}, u32[]{:S(2)}, u32[]{:S(2)}) %collective-permute-start.3) | collective-permute-done | bytes 4128 | tf_op jit(solution)/shard_map/ppermute | solution.py:352
  66.3 0.3 collective-permute-start.4
  66.6 7.2 %collective-permute-done.4 = f32[8,128]{1,0:T(8,128)S(1)} collective-permute-done((f32[8,128]{1,0:T(8,128)S(1)}, f32[8,128]{1,0:T(8,128)S(1)}, u32[]{:S(2)}, u32[]{:S(2)}) %collective-permute-start.4) | collective-permute-done | bytes 4128 | tf_op jit(solution)/shard_map/ppermute | solution.py:352
  73.8 0.0 copy-start.1
  73.8 0.9 copy-done.1
  74.8 0.0 copy-start.5
  74.8 0.7 copy-done.5
  75.5 28.0 %mixer.1.mixer_ref = f32[256,256]{1,0:T(8,128)S(1)} custom-call(f32[256,256]{1,0:T(8,128)S(1)} %copy-done.1, f32[8,256]{1,0:T(8,128)S(1)} %copy-done.5, f32[8,128]{1,0:T(8,128)S(1)} %add.15.sums_ref), custom_call_target="tpu_custom_call" | custom-call | tf_op jit(solution)/shard_map/mixer/pallas_call | solution.py:305
  103.5 55.4 %all-to-all-done.1 = f32[16,16,48,128]{3,2,1,0:T(8,128)} async-done(((f32[16,16,48,128]{3,2,1,0:T(8,128)}), f32[16,16,48,128]{3,2,1,0:T(8,128)}, u32[]{:S(2)}, u32[]{:S(2)}) %all-to-all-start.1) | async-done | bytes 6291488 | tf_op jit(solution)/shard_map/all_to_all | solution.py:376
  158.9 8.7 %apply.1 = f32[256,48,128]{2,1,0:T(8,128)} custom-call(f32[256,256]{1,0:T(8,128)S(1)} %mixer.1.mixer_ref, f32[256,48,128]{2,1,0:T(8,128)} %bitcast.3.x_ref), custom_call_target="tpu_custom_call" | custom-call | tf_op jit(solution)/shard_map/apply/pallas_call | solution.py:336
  167.6 82.3 %all_to_all.16 = f32[16,16,48,128]{3,2,1,0:T(8,128)S(1)} all-to-all(f32[16,16,48,128]{3,2,1,0:T(8,128)} %bitcast.15), channel_id=1, replica_groups=mesh['mem'=16,'reach'=16] {'mem'}, dimensions={0} | all-to-all | bytes 12582912 | tf_op jit(solution)/shard_map/all_to_all | solution.py:381
  249.9 3.6 %copy_bitcast_fusion = f32[16,48,2048]{2,1,0:T(8,128)} fusion(f32[16,16,48,128]{3,2,1,0:T(8,128)S(1)} %all_to_all.16), kind=kLoop, calls=%fused_computation | loop fusion | bytes 12582912 | tf_op jit(solution)/shard_map/reshape | solution.py:384
  (3 shorter events, 0.0 us)
Async XLA Ops:
  0.0 1.0 copy-start
  1.0 0.7 copy-start.2
  1.7 0.7 copy-start.3
  2.4 4.0 %copy-start.4 = (s32[16,256]{1,0:T(8,128)S(1)}, s32[16,256]{1,0:T(8,128)}, u32[]{:S(2)}) copy-start(s32[16,256]{1,0:T(8,128)} %slot_ref.3) | copy-start | bytes 49156
  4.5 17.9 %collective-permute-start = (f32[2,16,48,128]{3,2,1,0:T(8,128)S(1)}, f32[2,16,48,128]{3,2,1,0:T(8,128)S(1)}, u32[]{:S(2)}, u32[]{:S(2)}) collective-permute-start(f32[2,16,48,128]{3,2,1,0:T(8,128)S(1)} %edge.1), channel_id=1, source_target_pairs={{0,1},{1,2},{2,3},{3,4},{4,5},{5,6},{6,7},{7,8},{8,9},{9,10},{10,1... | collective-permute-start | bytes 2359304 | tf_op jit(solution)/shard_map/ppermute | solution.py:372
  48.1 4.8 %copy-start.6 = (s32[16]{0:T(128)S(1)}, s32[16]{0:T(128)}, u32[]{:S(2)}) copy-start(s32[16]{0:T(128)} %own_count_ref.1) | copy-start | bytes 196
  48.1 110.8 %all-to-all-start.1 = ((f32[16,16,48,128]{3,2,1,0:T(8,128)}), f32[16,16,48,128]{3,2,1,0:T(8,128)}, u32[]{:S(2)}, u32[]{:S(2)}) async-start(f32[16,16,48,128]{3,2,1,0:T(8,128)} %get-tuple-element.18), calls=%async_computation.1 | async-start | bytes 12582912 | tf_op jit(solution)/shard_map/all_to_all | solution.py:376
  56.1 1.4 collective-permute-start.1
  58.2 3.6 %collective-permute-start.2 = (f32[8,128]{1,0:T(8,128)S(1)}, f32[8,128]{1,0:T(8,128)S(1)}, u32[]{:S(2)}, u32[]{:S(2)}) collective-permute-start(f32[8,128]{1,0:T(8,128)S(1)} %add.12), channel_id=1, source_target_pairs={{0,2},{1,3},{2,0},{3,1},{4,6},{5,7},{6,4},{7,5},{8,10},{9,11},{10,... | collective-permute-start | bytes 12296 | tf_op jit(solution)/shard_map/ppermute | solution.py:352
  61.8 4.5 %collective-permute-start.3 = (f32[8,128]{1,0:T(8,128)S(1)}, f32[8,128]{1,0:T(8,128)S(1)}, u32[]{:S(2)}, u32[]{:S(2)}) collective-permute-start(f32[8,128]{1,0:T(8,128)S(1)} %add.13), channel_id=1, source_target_pairs={{0,4},{1,5},{2,6},{3,7},{4,0},{5,1},{6,2},{7,3},{8,12},{9,13},{10,... | collective-permute-start | bytes 12296 | tf_op jit(solution)/shard_map/ppermute | solution.py:352
  66.3 7.5 %collective-permute-start.4 = (f32[8,128]{1,0:T(8,128)S(1)}, f32[8,128]{1,0:T(8,128)S(1)}, u32[]{:S(2)}, u32[]{:S(2)}) collective-permute-start(f32[8,128]{1,0:T(8,128)S(1)} %add.14), channel_id=1, source_target_pairs={{0,8},{1,9},{2,10},{3,11},{4,12},{5,13},{6,14},{7,15},{8,0},{9,1},... | collective-permute-start | bytes 12296 | tf_op jit(solution)/shard_map/ppermute | solution.py:352
  73.8 1.0 copy-start.1
  74.8 0.7 copy-start.5

commit v3 on v2

--- a/solution.py
+++ b/solution.py
@@ -96,18 +96,15 @@
     )(ensemble, fraction, positions, mixing)
 
 
-def forecast_step(x_ref, f_ref, v_ref, slot_ref, out_ref, pack_ref, mix3_ref, carry_ref, block):
-    table = selector(v_ref[...], 2 * BL)
-    f = f_ref[...][None]
-    x = x_ref[...]
+def forecast_step(x, f, v, slots, mix3, carry_ref):
+    m, s, _ = x.shape
+    table = selector(v, 2 * BL)
+    f = f[None]
     for step in range(2):
         outflow = f * x
         routed = select(outflow, table)
-        x = x - outflow + (routed[:, :, :BL] + carry_ref[step]) + blend(x, mix3_ref[...])
+        x = x - outflow + (routed[:, :, :BL] + carry_ref[step]) + blend(x, mix3)
         carry_ref[step] = routed[:, :, BL:]
-    out_ref[...] = x[None]
-    slots = slot_ref[pl.ds(block, 1), :]
-    m, s, _ = x.shape
     state_of = slots // BL
     looked = select(x, selector_columns(slots - state_of * BL))
     rows = lax.broadcasted_iota(jnp.int32, (s, slots.shape[1]), 0)
@@ -115,15 +112,27 @@
     seen = jnp.sum(looked * hot_state[None], axis=1)
     mean = jnp.sum(seen, axis=0, keepdims=True) * (1.0 / m)
     pert = seen - mean
-    moment = jnp.sum(pert * pert, axis=0, keepdims=True)
-    blocks = pack_ref.shape[0]
-    pack_ref[pl.ds(block, 1), :m, :] = seen[None]
-    pack_ref[:, pl.ds(m + block, 1), :] = jnp.broadcast_to(mean[None], (blocks,) + mean.shape)
-    pack_ref[:, pl.ds(m + blocks + block, 1), :] = jnp.broadcast_to(moment[None], (blocks,) + mean.shape)
+    return x, seen, mean, jnp.sum(pert * pert, axis=0, keepdims=True)
+
+
+def store_block(x, seen, near_ref, far_ref, at):
+    m, s, lanes = x.shape
+    rows = m // 2 * s
+    near_ref[at, :rows, :] = x[: m // 2].reshape(rows, lanes)
+    far_ref[at] = x[m // 2 :].reshape(rows, lanes)
+    near_ref[at, rows : rows + m, :] = seen[:, :BL]
+    near_ref[at, rows + m : rows + 2 * m, :] = seen[:, BL:]
+
+
+def store_moments(mean, moment, moments_ref, block):
+    blocks = moments_ref.shape[0] // 4
+    for k, part in enumerate((mean[:, :BL], mean[:, BL:], moment[:, :BL], moment[:, BL:])):
+        moments_ref[pl.ds(k * blocks + block, 1), :] = part
 
 
 def inner_kernel(
-    x2_ref, f2_ref, v2_ref, x_ref, f_ref, v_ref, mixing_ref, slot_ref, out_ref, pack_ref, mix3_ref, carry_ref
+    x2_ref, f2_ref, v2_ref, x_ref, f_ref, v_ref, mixing_ref, slot_ref,
+    near_ref, far_ref, moments_ref, mix3_ref, carry_ref,
 ):
     step = pl.program_id(0)
 
@@ -132,21 +141,45 @@
         prepare_mixing(mixing_ref, mix3_ref)
         carry_ref[0], carry_ref[1] = edge_of(x2_ref, f2_ref, v2_ref, mix3_ref[...])
 
-    forecast_step(x_ref, f_ref, v_ref, slot_ref, out_ref, pack_ref, mix3_ref, carry_ref, step + 2)
+    block = step + 2
+    x, seen, mean, moment = forecast_step(
+        x_ref[...], f_ref[...], v_ref[...], slot_ref[pl.ds(block, 1), :], mix3_ref[...], carry_ref
+    )
+    store_block(x, seen, near_ref, far_ref, 0)
+    store_moments(mean, moment, moments_ref, block)
 
 
 def outer_kernel(
-    halo_ref, pack_in, held_ref, x_ref, f_ref, v_ref, mixing_ref, slot_ref, out_ref, pack_ref, mix3_ref, carry_ref
+    x_ref, f_ref, v_ref, mixing_ref, slot_ref, halo_ref, moments_in, near_in, far_in,
+    near_ref, far_ref, mix3_ref, carry_ref, near_buffer, far_buffer, moments_buffer, spread_buffer, sems,
 ):
-    step = pl.program_id(0)
-
-    @pl.when(step == 0)
-    def _():
-        prepare_mixing(mixing_ref, mix3_ref)
-        carry_ref[...] = halo_ref[...]
-        pack_ref[...] = pack_in[...]
-
-    forecast_step(x_ref, f_ref, v_ref, slot_ref, out_ref, pack_ref, mix3_ref, carry_ref, step)
+    blocks = near_ref.shape[0]
+    prepare_mixing(mixing_ref, mix3_ref)
+    carry_ref[...] = halo_ref[...]
+    moments_buffer[...] = moments_in[...]
+    for block in range(2):
+        lanes = slice(block * BL, (block + 1) * BL)
+        x, seen, mean, moment = forecast_step(
+            x_ref[:, :, lanes], f_ref[:, lanes], v_ref[:, lanes], slot_ref[block : block + 1, :],
+            mix3_ref[...], carry_ref,
+        )
+        store_block(x, seen, near_buffer, far_buffer, block)
+        store_moments(mean, moment, moments_buffer, block)
+    first = near_buffer.shape[1] - moments_buffer.shape[0]
+    moments = moments_buffer[...]
+    near_buffer[:, first:, :] = jnp.broadcast_to(moments[None], (2,) + moments.shape)
+    spread_buffer[...] = jnp.broadcast_to(moments[None], spread_buffer.shape)
+    copies = [
+        pltpu.make_async_copy(near_buffer, near_ref.at[0:2], sems.at[0]),
+        pltpu.make_async_copy(far_buffer, far_ref.at[0:2], sems.at[1]),
+        pltpu.make_async_copy(
+            spread_buffer, near_ref.at[2:blocks, first : first + moments.shape[0], :], sems.at[2]
+        ),
+    ]
+    for copy in copies:
+        copy.start()
+    for copy in copies:
+        copy.wait()
 
 
 def selector_columns(reach_row):
@@ -157,63 +190,75 @@
     return jnp.concatenate([hot, hot], axis=1)
 
 
-def forecast_blocks(kernel, first, number, lead, lead_specs, ensemble, fraction, positions, mixing, slots, aliases):
-    m, s, r = ensemble.shape
-    blocks, cap = slots.shape
-    whole = lambda *shape: pl.BlockSpec(shape, lambda g: (0,) * len(shape))
-    pack = (blocks, m + 2 * blocks, cap)
-    return pl.pallas_call(
-        kernel,
-        grid=(number,),
-        in_specs=lead_specs
-        + [
-            pl.BlockSpec((m, s, BL), lambda g: (0, 0, g + first)),
-            pl.BlockSpec((s, BL), lambda g: (0, g + first)),
-            pl.BlockSpec((1, BL), lambda g: (0, g + first)),
-            whole(s, s),
-            whole(blocks, cap),
-        ],
-        out_specs=[pl.BlockSpec((1, m, s, BL), lambda g: (g + first, 0, 0, 0)), whole(*pack)],
-        out_shape=[
-            jax.ShapeDtypeStruct((blocks, m, s, BL), jnp.float32),
-            jax.ShapeDtypeStruct(pack, jnp.float32),
-        ],
-        scratch_shapes=[
-            pltpu.VMEM((s, 3 * s), jnp.bfloat16),
-            pltpu.VMEM((2, m, s, BL), jnp.float32),
-        ],
-        input_output_aliases=aliases,
-        compiler_params=pltpu.CompilerParams(vmem_limit_bytes=VMEM_LIMIT),
-        name=kernel.__name__,
-    )(*lead, ensemble, fraction, positions, mixing, slots)
-
-
 def forecast(ensemble, fraction, positions, mixing, slots, halo):
     m, s, r = ensemble.shape
     blocks, cap = slots.shape
     whole = lambda *shape: pl.BlockSpec(shape, lambda g: (0,) * len(shape))
-    rest = (ensemble, fraction, positions, mixing, slots)
-    out, pack = forecast_blocks(
-        inner_kernel, 2, blocks - 2, (ensemble, fraction, positions),
-        [whole(m, s, 2 * BL), whole(s, 2 * BL), whole(1, 2 * BL)], *rest, {},
-    )
-    return forecast_blocks(
-        outer_kernel, 0, 2, (halo, pack, out),
-        [whole(2, m, s, BL), whole(*pack.shape), pl.BlockSpec(memory_space=pl.ANY)], *rest, {2: 0},
-    )
+    held = pl.BlockSpec(memory_space=pl.ANY)
+    pair = [whole(m, s, 2 * BL), whole(s, 2 * BL), whole(1, 2 * BL)]
+    rows = m // 2 * s
+    extra = 2 * m + 4 * blocks
+    near = jax.ShapeDtypeStruct((blocks, rows + extra, BL), jnp.float32)
+    far = jax.ShapeDtypeStruct((blocks, rows, BL), jnp.float32)
+    mix3 = pltpu.VMEM((s, 3 * s), jnp.bfloat16)
+    carry = pltpu.VMEM((2, m, s, BL), jnp.float32)
+    routing = (ensemble, fraction, positions)
+    near_part, far_part, moments = pl.pallas_call(
+        inner_kernel,
+        grid=(blocks - 2,),
+        in_specs=pair
+        + [
+            pl.BlockSpec((m, s, BL), lambda g: (0, 0, g + 2)),
+            pl.BlockSpec((s, BL), lambda g: (0, g + 2)),
+            pl.BlockSpec((1, BL), lambda g: (0, g + 2)),
+            whole(s, s),
+            whole(blocks, cap),
+        ],
+        out_specs=[
+            pl.BlockSpec((1, rows + extra, BL), lambda g: (g + 2, 0, 0)),
+            pl.BlockSpec((1, rows, BL), lambda g: (g + 2, 0, 0)),
+            whole(4 * blocks, BL),
+        ],
+        out_shape=[near, far, jax.ShapeDtypeStruct((4 * blocks, BL), jnp.float32)],
+        scratch_shapes=[mix3, carry],
+        compiler_params=pltpu.CompilerParams(vmem_limit_bytes=VMEM_LIMIT),
+        name="inner",
+    )(*routing, *routing, mixing, slots)
+    return pl.pallas_call(
+        outer_kernel,
+        grid=(1,),
+        in_specs=pair + [whole(s, s), whole(blocks, cap), whole(2, m, s, BL), whole(4 * blocks, BL), held, held],
+        out_specs=[held, held],
+        out_shape=[near, far],
+        scratch_shapes=[
+            mix3,
+            carry,
+            pltpu.VMEM((2,) + near.shape[1:], jnp.float32),
+            pltpu.VMEM((2,) + far.shape[1:], jnp.float32),
+            pltpu.VMEM((4 * blocks, BL), jnp.float32),
+            pltpu.VMEM((blocks - 2, 4 * blocks, BL), jnp.float32),
+            pltpu.SemaphoreType.DMA((3,)),
+        ],
+        input_output_aliases={7: 0, 8: 1},
+        compiler_params=pltpu.CompilerParams(vmem_limit_bytes=VMEM_LIMIT),
+        name="outer",
+    )(*routing, mixing, slots, halo, moments, near_part, far_part)
 
 
 def innovation_kernel(
-    block_ref, own_count_ref, pack_ref, values_ref, errors_ref, count_ref, gram_ref, right_ref, sums_ref
+    block_ref, own_count_ref, near_ref, values_ref, errors_ref, count_ref, gram_ref, right_ref, sums_ref
 ):
     blocks, cap = values_ref.shape
-    sources = pack_ref.shape[0]
-    m = pack_ref.shape[1] - 2 * blocks
+    sources = near_ref.shape[0]
+    m = (near_ref.shape[1] - 4 * blocks) // 2
     runs = sources * m
-    means = pack_ref[:, m : m + blocks, :]
+    joined = lambda at, size: jnp.concatenate(
+        [near_ref[:, at : at + size, :], near_ref[:, at + size : at + 2 * size, :]], axis=2
+    )
+    means = joined(2 * m, blocks)
     mean = jnp.sum(means, axis=0) * (1.0 / sources)
     drift = means - mean[None]
-    moment = jnp.sum(pack_ref[:, m + blocks :, :], axis=0) + m * jnp.sum(drift * drift, axis=0)
+    moment = jnp.sum(joined(2 * m + 2 * blocks, blocks), axis=0) + m * jnp.sum(drift * drift, axis=0)
     spread = moment / (runs - 1)
     lanes = lax.broadcasted_iota(jnp.int32, (blocks, cap), 1)
     live = (lanes < count_ref[...]).astype(jnp.float32)
@@ -226,7 +271,7 @@
     sums_ref[...] = jnp.where(lanes < 64, statistic, total)
 
     own = block_ref[0]
-    seen = pack_ref[:, :m, :].reshape(runs, cap)
+    seen = joined(0, m).reshape(runs, cap)
     mean = jnp.sum(seen, axis=0, keepdims=True) * (1.0 / runs)
     pert = seen - mean
     errors = errors_ref[pl.ds(own, 1), :]
@@ -238,22 +283,32 @@
     right_ref[...] = dot(jnp.broadcast_to(departure, (8, cap)), weighted, NT)
 
 
-def innovations(block, pack, values, errors, counts):
-    blocks = values.shape[0]
-    runs = pack.shape[0] * (pack.shape[1] - 2 * blocks)
-    vmem = pl.BlockSpec(memory_space=pltpu.VMEM)
+def innovations(block, near, values, errors, counts, m):
+    blocks, cap = values.shape
+    sources, rows, lanes = near.shape
+    extra = 2 * m + 4 * blocks
+    runs = sources * m
+    whole = lambda *shape: pl.BlockSpec(shape, lambda g: (0,) * len(shape))
     smem = pl.BlockSpec(memory_space=pltpu.SMEM)
     return pl.pallas_call(
         innovation_kernel,
-        in_specs=[smem, smem, vmem, vmem, vmem, vmem],
-        out_specs=[vmem] * 3,
+        grid=(1,),
+        in_specs=[
+            smem,
+            smem,
+            pl.BlockSpec((sources, extra, lanes), lambda g: (0, rows // extra - 1, 0)),
+            whole(blocks, cap),
+            whole(blocks, cap),
+            whole(blocks, 1),
+        ],
+        out_specs=[whole(runs, runs), whole(8, runs), whole(8, 128)],
         out_shape=[
             jax.ShapeDtypeStruct((runs, runs), jnp.float32),
             jax.ShapeDtypeStruct((8, runs), jnp.float32),
             jax.ShapeDtypeStruct((8, 128), jnp.float32),
         ],
         name="innovation",
-    )(block, counts, pack, values, errors, counts.reshape(blocks, 1))
+    )(block, counts, near, values, errors, counts.reshape(blocks, 1))
 
 
 def small_inverse_factor(a):
@@ -312,16 +367,24 @@
     )(gram, right, sums)
 
 
-def apply_kernel(mixer_ref, x_ref, out_ref):
-    runs, states, lanes = x_ref.shape
+def apply_kernel(mixer_ref, near_ref, far_ref, out_ref):
+    sources, half, states, lanes = near_ref.shape
+    runs = 2 * sources * half
     high, low = halves(mixer_ref[...])
     wide = jnp.concatenate([high, low, high], axis=1)
-    x_rows = x_ref.reshape(runs * states, lanes)
+    flat = lambda ref: ref.reshape(sources * half * states, lanes)
+    near_rows, far_rows = flat(near_ref), flat(far_ref)
     out_rows = out_ref.reshape(runs * states, lanes)
+
+    def members(s):
+        parts = [
+            rows[pl.ds(s, sources * half, stride=states), :].reshape(sources, half, lanes)
+            for rows in (near_rows, far_rows)
+        ]
+        return jnp.concatenate(parts, axis=1).reshape(runs, lanes)
+
     for s in range(0, states, 2):
-        x = jnp.concatenate(
-            [x_rows[pl.ds(s + i, runs, stride=states), :] for i in range(2)], axis=1
-        )
+        x = jnp.concatenate([members(s), members(s + 1)], axis=1)
         mean = jnp.sum(x, axis=0, keepdims=True) * (1.0 / runs)
         x_high, x_low = halves(x - mean)
         out = mean + fast_dot(wide, jnp.concatenate([x_high, x_high, x_low], axis=0))
@@ -329,19 +392,19 @@
             out_rows[pl.ds(s + i, runs, stride=states), :] = out[:, i * lanes : (i + 1) * lanes]
 
 
-def apply_mixer(mixer, x):
-    runs, states, lanes = x.shape
-    chunk = 8
-    block = pl.BlockSpec((runs, chunk, lanes), lambda g: (0, g, 0))
+def apply_mixer(mixer, near, far, chunk=8):
+    sources, half, states, lanes = far.shape
+    runs = 2 * sources * half
+    part = pl.BlockSpec((sources, half, chunk, lanes), lambda g: (0, 0, g, 0))
     return pl.pallas_call(
         apply_kernel,
         grid=(states // chunk,),
-        in_specs=[pl.BlockSpec((runs, runs), lambda g: (0, 0)), block],
-        out_specs=block,
-        out_shape=jax.ShapeDtypeStruct(x.shape, jnp.float32),
+        in_specs=[pl.BlockSpec((runs, runs), lambda g: (0, 0)), part, part],
+        out_specs=pl.BlockSpec((runs, chunk, lanes), lambda g: (0, g, 0)),
+        out_shape=jax.ShapeDtypeStruct((runs, states, lanes), jnp.float32),
         compiler_params=pltpu.CompilerParams(vmem_limit_bytes=VMEM_LIMIT),
         name="apply",
-    )(mixer, x)
+    )(mixer, near, far)
 
 
 def butterfly_sum(x, axes):
@@ -370,14 +433,14 @@
     block = lax.axis_index("mem").astype(jnp.int32).reshape(1)
     routing = (ensemble, outgoing_fraction, downstream_position.reshape(1, r), mixing)
     halo = lax.ppermute(edge_carries(*routing), "reach", [(i, i + 1) for i in range(reaches - 1)])
-    prior, pack = forecast(*routing, obs_index, halo)
-
-    pack = lax.all_to_all(pack, "mem", split_axis=0, concat_axis=0, tiled=True)
-    gathered = lax.all_to_all(prior, "mem", split_axis=0, concat_axis=0, tiled=True)
-    gram, right, sums = innovations(block, pack, obs_value, obs_error, obs_count)
+    near, far = forecast(*routing, obs_index, halo)
+
+    near = lax.all_to_all(near, "mem", split_axis=0, concat_axis=0, tiled=True)
+    far = lax.all_to_all(far, "mem", split_axis=0, concat_axis=0, tiled=True)
+    gram, right, sums = innovations(block, near, obs_value, obs_error, obs_count, m)
     sums = butterfly_sum(sums, ("reach",))
     mixer = mixer_of(gram, right, sums)
-    updated = apply_mixer(mixer, gathered.reshape(blocks * m, s, BL))
+    updated = apply_mixer(mixer, near.reshape(blocks, -1, s, BL), far.reshape(blocks, -1, s, BL))
     returned = lax.all_to_all(
         updated.reshape(blocks, m, s, BL), "mem", split_axis=0, concat_axis=0, tiled=True
     )

time: 255 us -> 229 us (0.90)
  waiting for transfers between devices: 70.7 us -> 15.6 us
  blocking collectives: 105 us -> 134 us
    all_to_all x1, waiting for transfers between devices: 55.4 us -> 0.01 us  [on_device(): far = lax.all_to_all(far, 'mem', split_axis=0, concat_axis=0, tiled=True)]
    all_to_all x1, blocking collectives: 22.2 us -> 56.5 us  [on_device(): near = lax.all_to_all(near, 'mem', split_axis=0, concat_axis=0, tiled=True)]
    all_to_all x1, blocking collectives: 82.3 us -> 78 us  [on_device(): lax.all_to_all(updated.reshape(blocks, m, s, BL), 'mem', split_axis=0, co...]
  transfers between devices with their start and end apart: 6 -> 6, of which waited for: 5 -> 4; matrix products, arithmetic and copies ran while one was open for 1% -> 1% of each run, Pallas kernels for 18% -> 21%
where the time goes in v3:
time: 229 us; the launch traced here: 228 us
  blocking collectives  134 us (59%)
  Pallas kernels  61.2 us (27%)
  waiting for transfers between devices  15.6 us (7%)
  local copies, waits for them, and re-layouts  8.33 us (4%)
  starting transfers between devices  7.37 us (3%)
    all_to_all x1, blocking collectives, on_device(): lax.all_to_all(updated.reshape(blocks, m, s, BL), 'mem', split_axis=0, co...  78 us
    all_to_all x1, blocking collectives, on_device(): near = lax.all_to_all(near, 'mem', split_axis=0, concat_axis=0, tiled=True)  56.5 us
    pallas_call x1, Pallas kernels, mixer_of(): pl.pallas_call(mixer_kernel, in_specs=[vmem] * 3, out_specs=vmem, out_sha...  28 us
    pallas_call x1, Pallas kernels, forecast(): pl.pallas_call(inner_kernel, grid=(blocks - 2,), in_specs=pair + [pl.Bloc...  16.5 us
    ppermute x4, waiting for transfers between devices, butterfly_sum(): x = x + lax.ppermute(x, axis, [(i, i ^ step) for i in range(size)])  15.5 us
    pallas_call x1, Pallas kernels, apply_mixer(): pl.pallas_call(apply_kernel, grid=(states // chunk,), in_specs=[pl.BlockS...  8.18 us
  transfers between devices with their start and end apart: 6, of which 4 were waited for; matrix products, arithmetic and copies ran while one was open for 1% of the time, Pallas kernels for 21%

profile of v3, /device:TPU:192, one launch (start us, length us, event | category | flops | bytes accessed | tf_op | source)
XLA Modules:
  0.0 227.7 jit_solution(7980317541025190962)
XLA Ops:
  0.0 0.0 copy-start
  0.0 1.0 copy-done
  1.0 0.0 copy-start.2
  1.0 0.7 copy-done.2
  1.7 0.0 copy-start.3
  1.7 0.7 copy-done.3
  2.4 0.0 copy-start.4
  2.4 2.0 edge.1
  4.5 1.9 collective-permute-start
  6.4 0.0 copy-done.4
  6.4 16.5 %inner.1 = (f32[16,480,128]{2,1,0:T(8,128)}, f32[16,384,128]{2,1,0:T(8,128)}, f32[64,128]{1,0:T(8,128)S(1)}) custom-call(f32[16,48,2048]{2,1,0:T(8,128)} %x_ref.5, f32[48,2048]{1,0:T(8,128)S(1)} %copy-done, s32[1,2048]{1,0:T(1,128)S(1)} %bitcast.14, f32[16,48,2048]{2,1,0:T(8,128)} %x_ref.5, f32[48,2048]{1,0:T(8,128)S(1)} %copy-done, s32[1,2048]{1,0:T(1,128)S(1)} %bitcast.15, ...), custom_call_target="tpu_custom_call" | custom-call | tf_op jit(solution)/shard_map/inner/pallas_call | solution.py:206
  22.9 0.0 collective-permute-done.halo_ref
  22.9 4.0 %outer.1 = (f32[16,480,128]{2,1,0:T(8,128)}, f32[16,384,128]{2,1,0:T(8,128)}) custom-call(f32[16,48,2048]{2,1,0:T(8,128)} %x_ref.5, f32[48,2048]{1,0:T(8,128)S(1)} %copy-done, s32[1,2048]{1,0:T(1,128)S(1)} %bitcast.16, f32[48,48]{1,0:T(8,128)S(1)} %copy-done.2, s32[16,256]{1,0:T(8,128)S(1)} %copy-done.4, ...), custom_call_target="tpu_custom_call", output_to_operand_aliasing={{0}: (7, {}), {1}: (8, {})} | custom-call | tf_op jit(solution)/shard_map/outer/pallas_call | solution.py:227
  26.9 0.0 copy-start.6
  26.9 56.5 %all_to_all.15.near_ref = f32[16,480,128]{2,1,0:T(8,128)} all-to-all(f32[16,480,128]{2,1,0:T(8,128)} %get-tuple-element.16), channel_id=1, replica_groups=mesh['mem'=16,'reach'=16] {'mem'}, dimensions={0} | all-to-all | bytes 7864320 | tf_op jit(solution)/shard_map/all_to_all | solution.py:438
  83.4 4.0 %all-to-all-start.1 = ((f32[16,384,128]{2,1,0:T(8,128)}), f32[16,384,128]{2,1,0:T(8,128)S(1)}, u32[]{:S(2)}, u32[]{:S(2)}) async-start(f32[16,384,128]{2,1,0:T(8,128)} %get-tuple-element.20), calls=%async_computation.1 | async-start | bytes 6291456 | tf_op jit(solution)/shard_map/all_to_all | solution.py:439
  87.4 0.0 copy-done.6
  87.4 0.7 copy.11.count_ref
  88.1 2.5 %innovation.1 = (f32[256,256]{1,0:T(8,128)}, f32[8,256]{1,0:T(8,128)}, f32[8,128]{1,0:T(8,128)}) custom-call(s32[1]{0:T(128)} %bitcast.block_ref, s32[16]{0:T(128)} %own_count_ref.1, f32[16,480,128]{2,1,0:T(8,128)} %all_to_all.15.near_ref, f32[16,256]{1,0:T(8,128)} %values_ref.1, f32[16,256]{1,0:T(8,128)} %errors_ref.1, s32[16,1]{1,0:T(8,128)} %copy.11.count_ref), custom_call_target="tpu_custom_call" | custom-call | tf_op jit(solution)/shard_map/innovation/pallas_call | solution.py:293
  90.6 0.0 collective-permute-start.1
  90.6 1.4 collective-permute-done.1
  92.0 0.7 add.12
  92.6 0.0 collective-permute-start.2
  92.7 3.6 %collective-permute-done.2 = f32[8,128]{1,0:T(8,128)S(1)} collective-permute-done((f32[8,128]{1,0:T(8,128)S(1)}, f32[8,128]{1,0:T(8,128)S(1)}, u32[]{:S(2)}, u32[]{:S(2)}) %collective-permute-start.2) | collective-permute-done | bytes 4128 | tf_op jit(solution)/shard_map/ppermute | solution.py:415
  96.3 1.4 collective-permute-start.3
  97.7 3.1 %collective-permute-done.3 = f32[8,128]{1,0:T(8,128)S(1)} collective-permute-done((f32[8,128]{1,0:T(8,128)S(1)}, f32[8,128]{1,0:T(8,128)S(1)}, u32[]{:S(2)}, u32[]{:S(2)}) %collective-permute-start.3) | collective-permute-done | bytes 4128 | tf_op jit(solution)/shard_map/ppermute | solution.py:415
  100.8 0.0 collective-permute-start.4
  100.8 7.5 %collective-permute-done.4 = f32[8,128]{1,0:T(8,128)S(1)} collective-permute-done((f32[8,128]{1,0:T(8,128)S(1)}, f32[8,128]{1,0:T(8,128)S(1)}, u32[]{:S(2)}, u32[]{:S(2)}) %collective-permute-start.4) | collective-permute-done | bytes 4128 | tf_op jit(solution)/shard_map/ppermute | solution.py:415
  108.3 0.0 copy-start.1
  108.3 0.9 copy-done.1
  109.2 0.0 copy-start.5
  109.2 0.7 copy-done.5
  109.9 28.0 %mixer.1.mixer_ref = f32[256,256]{1,0:T(8,128)S(1)} custom-call(f32[256,256]{1,0:T(8,128)S(1)} %copy-done.1, f32[8,256]{1,0:T(8,128)S(1)} %copy-done.5, f32[8,128]{1,0:T(8,128)S(1)} %add.15.sums_ref), custom_call_target="tpu_custom_call" | custom-call | tf_op jit(solution)/shard_map/mixer/pallas_call | solution.py:360
  138.0 0.0 all-to-all-done.1
  138.0 8.2 %apply.1 = f32[256,48,128]{2,1,0:T(8,128)} custom-call(f32[256,256]{1,0:T(8,128)S(1)} %mixer.1.mixer_ref, f32[16,10,48,128]{3,2,1,0:T(8,128)} %bitcast.17, f32[16,8,48,128]{3,2,1,0:T(8,128)S(1)} %bitcast.12), custom_call_target="tpu_custom_call" | custom-call | tf_op jit(solution)/shard_map/apply/pallas_call | solution.py:399
  146.2 78.0 %all_to_all.16 = f32[16,16,48,128]{3,2,1,0:T(8,128)S(1)} all-to-all(f32[16,16,48,128]{3,2,1,0:T(8,128)} %bitcast.18), channel_id=1, replica_groups=mesh['mem'=16,'reach'=16] {'mem'}, dimensions={0} | all-to-all | bytes 12582912 | tf_op jit(solution)/shard_map/all_to_all | solution.py:444
  224.1 3.6 %copy_bitcast_fusion = f32[16,48,2048]{2,1,0:T(8,128)} fusion(f32[16,16,48,128]{3,2,1,0:T(8,128)S(1)} %all_to_all.16), kind=kLoop, calls=%fused_computation | loop fusion | bytes 12582912 | tf_op jit(solution)/shard_map/reshape | solution.py:447
  (3 shorter events, 0.0 us)
Async XLA Ops:
  0.0 1.0 copy-start
  1.0 0.7 copy-start.2
  1.7 0.7 copy-start.3
  2.4 3.9 %copy-start.4 = (s32[16,256]{1,0:T(8,128)S(1)}, s32[16,256]{1,0:T(8,128)}, u32[]{:S(2)}) copy-start(s32[16,256]{1,0:T(8,128)} %slot_ref.3) | copy-start | bytes 49156
  4.5 18.4 %collective-permute-start = (f32[2,16,48,128]{3,2,1,0:T(8,128)S(1)}, f32[2,16,48,128]{3,2,1,0:T(8,128)S(1)}, u32[]{:S(2)}, u32[]{:S(2)}) collective-permute-start(f32[2,16,48,128]{3,2,1,0:T(8,128)S(1)} %edge.1), channel_id=1, source_target_pairs={{0,1},{1,2},{2,3},{3,4},{4,5},{5,6},{6,7},{7,8},{8,9},{9,10},{10,1... | collective-permute-start | bytes 2359304 | tf_op jit(solution)/shard_map/ppermute | solution.py:435
  26.9 60.5 %copy-start.6 = (s32[16]{0:T(128)S(1)}, s32[16]{0:T(128)}, u32[]{:S(2)}) copy-start(s32[16]{0:T(128)} %own_count_ref.1) | copy-start | bytes 196
  83.4 54.6 %all-to-all-start.1 = ((f32[16,384,128]{2,1,0:T(8,128)}), f32[16,384,128]{2,1,0:T(8,128)S(1)}, u32[]{:S(2)}, u32[]{:S(2)}) async-start(f32[16,384,128]{2,1,0:T(8,128)} %get-tuple-element.20), calls=%async_computation.1 | async-start | bytes 6291456 | tf_op jit(solution)/shard_map/all_to_all | solution.py:439
  90.6 1.4 collective-permute-start.1
  92.6 3.6 %collective-permute-start.2 = (f32[8,128]{1,0:T(8,128)S(1)}, f32[8,128]{1,0:T(8,128)S(1)}, u32[]{:S(2)}, u32[]{:S(2)}) collective-permute-start(f32[8,128]{1,0:T(8,128)S(1)} %add.12), channel_id=1, source_target_pairs={{0,2},{1,3},{2,0},{3,1},{4,6},{5,7},{6,4},{7,5},{8,10},{9,11},{10,... | collective-permute-start | bytes 12296 | tf_op jit(solution)/shard_map/ppermute | solution.py:415
  96.3 4.5 %collective-permute-start.3 = (f32[8,128]{1,0:T(8,128)S(1)}, f32[8,128]{1,0:T(8,128)S(1)}, u32[]{:S(2)}, u32[]{:S(2)}) collective-permute-start(f32[8,128]{1,0:T(8,128)S(1)} %add.13), channel_id=1, source_target_pairs={{0,4},{1,5},{2,6},{3,7},{4,0},{5,1},{6,2},{7,3},{8,12},{9,13},{10,... | collective-permute-start | bytes 12296 | tf_op jit(solution)/shard_map/ppermute | solution.py:415
  100.8 7.5 %collective-permute-start.4 = (f32[8,128]{1,0:T(8,128)S(1)}, f32[8,128]{1,0:T(8,128)S(1)}, u32[]{:S(2)}, u32[]{:S(2)}) collective-permute-start(f32[8,128]{1,0:T(8,128)S(1)} %add.14), channel_id=1, source_target_pairs={{0,8},{1,9},{2,10},{3,11},{4,12},{5,13},{6,14},{7,15},{8,0},{9,1},... | collective-permute-start | bytes 12296 | tf_op jit(solution)/shard_map/ppermute | solution.py:415
  108.3 1.0 copy-start.1
  109.2 0.7 copy-start.5

commit v4 on v3

--- a/solution.py
+++ b/solution.py
@@ -10,7 +10,7 @@
 NT = (((1,), (1,)), ((), ()))
 NN = (((1,), (0,)), ((), ()))
 TN = (((0,), (0,)), ((), ()))
-VMEM_LIMIT = 48 * 1024 * 1024
+VMEM_LIMIT = 24 * 1024 * 1024
 
 
 def dot(a, b, dims=NN):
@@ -27,17 +27,29 @@
     return high, low
 
 
-def selector(index_row, size):
-    rows = lax.broadcasted_iota(jnp.int32, (size, index_row.shape[1]), 0)
-    hot = (rows == index_row).astype(jnp.float32).astype(jnp.bfloat16)
-    return jnp.concatenate([hot, hot], axis=1)
+def one_hot(index, iota):
+    return (index == iota).astype(jnp.float32).astype(jnp.bfloat16)
+
+
+def target_table(position_row):
+    reaches = position_row.shape[1]
+    column = jnp.broadcast_to(position_row, (reaches, reaches)).T
+    lanes = lax.broadcasted_iota(jnp.int32, (reaches, reaches), 1)
+    hot = jnp.concatenate([one_hot(column, lanes), one_hot(column, lanes + reaches)], axis=1)
+    return jnp.concatenate([hot, hot], axis=0)
+
+
+def slot_table(reach_row):
+    rows = lax.broadcasted_iota(jnp.int32, (BL, reach_row.shape[1]), 0)
+    hot = one_hot(reach_row, rows)
+    return jnp.concatenate([hot, hot], axis=0)
 
 
 def select(x, table):
     m, s, r = x.shape
     high, low = halves(x.reshape(m * s, r))
-    out = fast_dot(jnp.concatenate([high, low], axis=1), table, NT)
-    return out.reshape(m, s, table.shape[0])
+    out = fast_dot(jnp.concatenate([high, low], axis=1), table)
+    return out.reshape(m, s, table.shape[1])
 
 
 def blend(x, mix3):
@@ -61,8 +73,8 @@
 
 def edge_of(x_ref, f_ref, v_ref, mix3):
     outflow = f_ref[:, :BL][None] * x_ref[:, :, :BL]
-    arriving = select(outflow, selector(v_ref[:, :BL], 2 * BL))[:, :, BL:]
-    table = selector(v_ref[:, BL:], 2 * BL)
+    arriving = select(outflow, target_table(v_ref[:, :BL]))[:, :, BL:]
+    table = target_table(v_ref[:, BL:])
     x = x_ref[:, :, BL:]
     f = f_ref[:, BL:][None]
     outflow = f * x
@@ -98,7 +110,7 @@
 
 def forecast_step(x, f, v, slots, mix3, carry_ref):
     m, s, _ = x.shape
-    table = selector(v, 2 * BL)
+    table = target_table(v)
     f = f[None]
     for step in range(2):
         outflow = f * x
@@ -106,7 +118,7 @@
         x = x - outflow + (routed[:, :, :BL] + carry_ref[step]) + blend(x, mix3)
         carry_ref[step] = routed[:, :, BL:]
     state_of = slots // BL
-    looked = select(x, selector_columns(slots - state_of * BL))
+    looked = select(x, slot_table(slots - state_of * BL))
     rows = lax.broadcasted_iota(jnp.int32, (s, slots.shape[1]), 0)
     hot_state = (rows == state_of).astype(jnp.float32)
     seen = jnp.sum(looked * hot_state[None], axis=1)
@@ -141,12 +153,15 @@
         prepare_mixing(mixing_ref, mix3_ref)
         carry_ref[0], carry_ref[1] = edge_of(x2_ref, f2_ref, v2_ref, mix3_ref[...])
 
-    block = step + 2
-    x, seen, mean, moment = forecast_step(
-        x_ref[...], f_ref[...], v_ref[...], slot_ref[pl.ds(block, 1), :], mix3_ref[...], carry_ref
-    )
-    store_block(x, seen, near_ref, far_ref, 0)
-    store_moments(mean, moment, moments_ref, block)
+    for i in range(2):
+        block = 2 * step + 2 + i
+        lanes = slice(i * BL, (i + 1) * BL)
+        x, seen, mean, moment = forecast_step(
+            x_ref[:, :, lanes], f_ref[:, lanes], v_ref[:, lanes], slot_ref[pl.ds(block, 1), :],
+            mix3_ref[...], carry_ref,
+        )
+        store_block(x, seen, near_ref, far_ref, i)
+        store_moments(mean, moment, moments_ref, block)
 
 
 def outer_kernel(
@@ -182,14 +197,6 @@
         copy.wait()
 
 
-def selector_columns(reach_row):
-    slots = reach_row.shape[1]
-    rows = lax.broadcasted_iota(jnp.int32, (BL, slots), 0)
-    hot = (rows == reach_row).astype(jnp.float32)
-    hot = hot.T.astype(jnp.bfloat16)
-    return jnp.concatenate([hot, hot], axis=1)
-
-
 def forecast(ensemble, fraction, positions, mixing, slots, halo):
     m, s, r = ensemble.shape
     blocks, cap = slots.shape
@@ -205,18 +212,18 @@
     routing = (ensemble, fraction, positions)
     near_part, far_part, moments = pl.pallas_call(
         inner_kernel,
-        grid=(blocks - 2,),
+        grid=(blocks // 2 - 1,),
         in_specs=pair
         + [
-            pl.BlockSpec((m, s, BL), lambda g: (0, 0, g + 2)),
-            pl.BlockSpec((s, BL), lambda g: (0, g + 2)),
-            pl.BlockSpec((1, BL), lambda g: (0, g + 2)),
+            pl.BlockSpec((m, s, 2 * BL), lambda g: (0, 0, g + 1)),
+            pl.BlockSpec((s, 2 * BL), lambda g: (0, g + 1)),
+            pl.BlockSpec((1, 2 * BL), lambda g: (0, g + 1)),
             whole(s, s),
             whole(blocks, cap),
         ],
         out_specs=[
-            pl.BlockSpec((1, rows + extra, BL), lambda g: (g + 2, 0, 0)),
-            pl.BlockSpec((1, rows, BL), lambda g: (g + 2, 0, 0)),
+            pl.BlockSpec((2, rows + extra, BL), lambda g: (g + 1, 0, 0)),
+            pl.BlockSpec((2, rows, BL), lambda g: (g + 1, 0, 0)),
             whole(4 * blocks, BL),
         ],
         out_shape=[near, far, jax.ShapeDtypeStruct((4 * blocks, BL), jnp.float32)],
@@ -315,22 +322,39 @@
     n = a.shape[0]
     rows = lax.broadcasted_iota(jnp.int32, (n, n), 0)
     cols = lax.broadcasted_iota(jnp.int32, (n, n), 1)
-    eye = (rows == cols).astype(jnp.float32)
-    both = jnp.concatenate([a, eye], axis=1)
-    below = lax.broadcasted_iota(jnp.int32, (n, 1), 0)
-    scales = jnp.zeros((n, 1), jnp.float32)
-    for j in range(n):
-        pivot = both[j : j + 1, j : j + 1]
-        row = both[j : j + 1, :] * (1.0 / pivot)
-        factor = jnp.where(below > j, both[:, j : j + 1], 0.0)
-        scales = jnp.where(below == j, pivot, scales)
-        both = both - factor * row
-    return both[:, n:] * (1.0 / jnp.sqrt(scales))
+    both = jnp.concatenate([a, (rows == cols).astype(jnp.float32)], axis=1)
+    groups = [both[k : k + 8] for k in range(0, n, 8)]
+    sub = lax.broadcasted_iota(jnp.int32, (8, 2 * n), 0)
+    lane = lambda x, j: jnp.broadcast_to(x[:, j : j + 1], x.shape)
+    line = lambda x, i: jnp.broadcast_to(x[i : i + 1], x.shape)
+    scales = []
+    for j in range(0, n, 2):
+        k, i = divmod(j, 8)
+        head = groups[k]
+        first = [lane(g, j) for g in groups[k:]]
+        second = [lane(g, j + 1) for g in groups[k:]]
+        p, q, t = line(first[0], i), line(second[0], i), line(second[0], i + 1)
+        top, bottom = line(head, i), line(head, i + 1)
+        scale_top = 1.0 / p
+        scale_bottom = p * (1.0 / (p * t - q * q))
+        slope = q * scale_top
+        bottom = bottom - slope * top
+        bottom_row = bottom * scale_bottom
+        top_row = top * scale_top - slope * bottom_row
+        groups[k:] = [
+            g - f * top_row - h * bottom_row for g, f, h in zip(groups[k:], first, second)
+        ]
+        groups[k] = jnp.where(sub > i + 1, groups[k], jnp.where(sub == i + 1, bottom, head))
+        if i == 0:
+            scales.append(scale_top)
+        scales[k] = jnp.where(sub > i, scale_bottom, jnp.where(sub == i, scale_top, scales[k]))
+    inverse = jnp.concatenate([g * jnp.sqrt(c) for g, c in zip(groups, scales)], axis=0)
+    return inverse[:, n:]
 
 
 def inverse_factor(a):
     n = a.shape[0]
-    if n <= 32:
+    if n <= 64:
         return small_inverse_factor(a)
     h = n // 2
     first = inverse_factor(a[:h, :h])

time: 229 us -> 222 us (0.969)
  Pallas kernels: 61.2 us -> 46.2 us
  local copies, waits for them, and re-layouts: 8.33 us -> 13.2 us
    pallas_call x1, Pallas kernels: 28 us -> 21.7 us  [mixer_of(): pl.pallas_call(mixer_kernel, in_specs=[vmem] * 3, out_specs=vmem, out_sha...]
    unnamed x14 -> x18, local copies, waits for them, and re-layouts: 4.08 us -> 8.98 us
    pallas_call x1, Pallas kernels: 16.5 us -> 12.6 us  [forecast(): pl.pallas_call(inner_kernel, grid=(blocks // 2 - 1,), in_specs=pair + [pl...]
    pallas_call x1, Pallas kernels: 8.18 us -> 5.79 us  [apply_mixer(): pl.pallas_call(apply_kernel, grid=(states // chunk,), in_specs=[pl.BlockS...]
  transfers between devices with their start and end apart: 6 -> 6, of which waited for: 4 -> 4; matrix products, arithmetic and copies ran while one was open for 1% -> 1% of each run, Pallas kernels for 21% -> 17%
where the time goes in v4:
time: 222 us; the launch traced here: 219 us
  blocking collectives  136 us (61%)
  Pallas kernels  46.2 us (21%)
  waiting for transfers between devices  15.6 us (7%)
  local copies, waits for them, and re-layouts  13.2 us (6%)
  starting transfers between devices  7.37 us (3%)
    all_to_all x1, blocking collectives, on_device(): lax.all_to_all(updated.reshape(blocks, m, s, BL), 'mem', split_axis=0, co...  79.3 us
    all_to_all x1, blocking collectives, on_device(): near = lax.all_to_all(near, 'mem', split_axis=0, concat_axis=0, tiled=True)  56.3 us
    pallas_call x1, Pallas kernels, mixer_of(): pl.pallas_call(mixer_kernel, in_specs=[vmem] * 3, out_specs=vmem, out_sha...  21.7 us
    ppermute x4, waiting for transfers between devices, butterfly_sum(): x = x + lax.ppermute(x, axis, [(i, i ^ step) for i in range(size)])  15.5 us
    pallas_call x1, Pallas kernels, forecast(): pl.pallas_call(inner_kernel, grid=(blocks // 2 - 1,), in_specs=pair + [pl...  12.6 us
    unnamed x18, local copies, waits for them, and re-layouts  8.98 us
    pallas_call x1, Pallas kernels, apply_mixer(): pl.pallas_call(apply_kernel, grid=(states // chunk,), in_specs=[pl.BlockS...  5.79 us
  transfers between devices with their start and end apart: 6, of which 4 were waited for; matrix products, arithmetic and copies ran while one was open for 1% of the time, Pallas kernels for 17%

profile of v4, /device:TPU:192, one launch (start us, length us, event | category | flops | bytes accessed | tf_op | source)
XLA Modules:
  0.0 218.7 jit_solution(9555917302383611505)
XLA Ops:
  0.0 0.0 copy-start
  0.0 2.8 %copy-done = f32[16,48,2048]{2,1,0:T(8,128)S(1)} copy-done((f32[16,48,2048]{2,1,0:T(8,128)S(1)}, f32[16,48,2048]{2,1,0:T(8,128)}, u32[]{:S(2)}) %copy-start) | copy-done | bytes 6291480
  2.8 0.0 copy-start.2
  2.8 1.0 copy-done.2
  3.8 0.0 copy-start.4
  3.8 0.7 copy-done.4
  4.5 0.0 copy-start.5
  4.5 0.7 copy-done.5
  5.2 0.0 copy-start.6
  5.2 0.9 edge.1
  6.1 1.9 collective-permute-start
  8.0 0.0 copy-done.6
  8.1 12.6 %inner.1 = (f32[16,480,128]{2,1,0:T(8,128)S(1)}, f32[16,384,128]{2,1,0:T(8,128)}, f32[64,128]{1,0:T(8,128)S(1)}) custom-call(f32[16,48,2048]{2,1,0:T(8,128)S(1)} %copy-done, f32[48,2048]{1,0:T(8,128)S(1)} %copy-done.2, s32[1,2048]{1,0:T(1,128)S(1)} %bitcast.16, f32[16,48,2048]{2,1,0:T(8,128)S(1)} %copy-done, f32[48,2048]{1,0:T(8,128)S(1)} %copy-done.2, ...), custom_call_target="tpu_custom_call" | custom-call | tf_op jit(solution)/shard_map/inner/pallas_call | solution.py:213
  20.6 0.0 collective-permute-done.halo_ref
  20.7 2.8 %outer.1 = (f32[16,480,128]{2,1,0:T(8,128)S(1)}, f32[16,384,128]{2,1,0:T(8,128)}) custom-call(f32[16,48,2048]{2,1,0:T(8,128)S(1)} %copy-done, f32[48,2048]{1,0:T(8,128)S(1)} %copy-done.2, s32[1,2048]{1,0:T(1,128)S(1)} %bitcast.18, f32[48,48]{1,0:T(8,128)S(1)} %copy-done.4, s32[16,256]{1,0:T(8,128)S(1)} %copy-done.6, ...), custom_call_target="tpu_custom_call", output_to_operand_aliasing={{0}: (7, {}), {1}: (8, {})} | custom-call | tf_op jit(solution)/shard_map/outer/pallas_call | solution.py:234
  23.4 0.0 copy-start.8
  23.4 56.3 %all_to_all.15.near_ref = f32[16,480,128]{2,1,0:T(8,128)} all-to-all(f32[16,480,128]{2,1,0:T(8,128)S(1)} %get-tuple-element.16), channel_id=1, replica_groups=mesh['mem'=16,'reach'=16] {'mem'}, dimensions={0} | all-to-all | bytes 7864320 | tf_op jit(solution)/shard_map/all_to_all | solution.py:462
  79.7 4.0 %all-to-all-start.1 = ((f32[16,384,128]{2,1,0:T(8,128)}), f32[16,384,128]{2,1,0:T(8,128)S(1)}, u32[]{:S(2)}, u32[]{:S(2)}) async-start(f32[16,384,128]{2,1,0:T(8,128)} %get-tuple-element.20), calls=%async_computation.1 | async-start | bytes 6291456 | tf_op jit(solution)/shard_map/all_to_all | solution.py:463
  83.7 0.0 copy-done.8
  83.8 0.7 copy.11.count_ref
  84.4 2.5 %innovation.1 = (f32[256,256]{1,0:T(8,128)}, f32[8,256]{1,0:T(8,128)}, f32[8,128]{1,0:T(8,128)}) custom-call(s32[1]{0:T(128)} %bitcast.block_ref, s32[16]{0:T(128)} %own_count_ref.1, f32[16,480,128]{2,1,0:T(8,128)} %all_to_all.15.near_ref, f32[16,256]{1,0:T(8,128)} %values_ref.1, f32[16,256]{1,0:T(8,128)} %errors_ref.1, s32[16,1]{1,0:T(8,128)} %copy.11.count_ref), custom_call_target="tpu_custom_call" | custom-call | tf_op jit(solution)/shard_map/innovation/pallas_call | solution.py:300
  86.9 0.0 collective-permute-start.1
  86.9 1.4 collective-permute-done.1
  88.3 0.7 add.12
  89.0 0.0 collective-permute-start.2
  89.0 3.6 %collective-permute-done.2 = f32[8,128]{1,0:T(8,128)S(1)} collective-permute-done((f32[8,128]{1,0:T(8,128)S(1)}, f32[8,128]{1,0:T(8,128)S(1)}, u32[]{:S(2)}, u32[]{:S(2)}) %collective-permute-start.2) | collective-permute-done | bytes 4128 | tf_op jit(solution)/shard_map/ppermute | solution.py:439
  92.6 1.5 collective-permute-start.3
  94.1 3.1 %collective-permute-done.3 = f32[8,128]{1,0:T(8,128)S(1)} collective-permute-done((f32[8,128]{1,0:T(8,128)S(1)}, f32[8,128]{1,0:T(8,128)S(1)}, u32[]{:S(2)}, u32[]{:S(2)}) %collective-permute-start.3) | collective-permute-done | bytes 4128 | tf_op jit(solution)/shard_map/ppermute | solution.py:439
  97.1 0.0 collective-permute-start.4
  97.1 7.5 %collective-permute-done.4 = f32[8,128]{1,0:T(8,128)S(1)} collective-permute-done((f32[8,128]{1,0:T(8,128)S(1)}, f32[8,128]{1,0:T(8,128)S(1)}, u32[]{:S(2)}, u32[]{:S(2)}) %collective-permute-start.4) | collective-permute-done | bytes 4128 | tf_op jit(solution)/shard_map/ppermute | solution.py:439
  104.6 0.0 copy-start.3
  104.6 0.9 copy-done.3
  105.6 0.0 copy-start.7
  105.6 0.7 copy-done.7
  106.3 21.7 %mixer.1.mixer_ref = f32[256,256]{1,0:T(8,128)S(1)} custom-call(f32[256,256]{1,0:T(8,128)S(1)} %copy-done.3, f32[8,256]{1,0:T(8,128)S(1)} %copy-done.7, f32[8,128]{1,0:T(8,128)S(1)} %add.15.sums_ref), custom_call_target="tpu_custom_call" | custom-call | tf_op jit(solution)/shard_map/mixer/pallas_call | solution.py:384
  128.0 0.0 all-to-all-done.1
  128.0 0.0 copy-start.1
  128.0 2.1 copy-done.1
  130.1 5.8 %apply.1 = f32[256,48,128]{2,1,0:T(8,128)S(1)} custom-call(f32[256,256]{1,0:T(8,128)S(1)} %mixer.1.mixer_ref, f32[16,10,48,128]{3,2,1,0:T(8,128)S(1)} %bitcast.12, f32[16,8,48,128]{3,2,1,0:T(8,128)S(1)} %bitcast.14), custom_call_target="tpu_custom_call" | custom-call | tf_op jit(solution)/shard_map/apply/pallas_call | solution.py:423
  135.9 79.3 %all_to_all.16 = f32[16,16,48,128]{3,2,1,0:T(8,128)S(1)} all-to-all(f32[16,16,48,128]{3,2,1,0:T(8,128)S(1)} %bitcast.13), channel_id=1, replica_groups=mesh['mem'=16,'reach'=16] {'mem'}, dimensions={0} | all-to-all | bytes 12582912 | tf_op jit(solution)/shard_map/all_to_all | solution.py:468
  215.2 3.6 %copy_bitcast_fusion = f32[16,48,2048]{2,1,0:T(8,128)} fusion(f32[16,16,48,128]{3,2,1,0:T(8,128)S(1)} %all_to_all.16), kind=kLoop, calls=%fused_computation | loop fusion | bytes 12582912 | tf_op jit(solution)/shard_map/reshape | solution.py:471
  (3 shorter events, 0.0 us)
Async XLA Ops:
  0.0 2.8 %copy-start = (f32[16,48,2048]{2,1,0:T(8,128)S(1)}, f32[16,48,2048]{2,1,0:T(8,128)}, u32[]{:S(2)}) copy-start(f32[16,48,2048]{2,1,0:T(8,128)} %x_ref.5) | copy-start | bytes 18874372
  2.8 1.0 copy-start.2
  3.8 0.7 copy-start.4
  4.5 0.7 copy-start.5
  5.2 2.8 %copy-start.6 = (s32[16,256]{1,0:T(8,128)S(1)}, s32[16,256]{1,0:T(8,128)}, u32[]{:S(2)}) copy-start(s32[16,256]{1,0:T(8,128)} %slot_ref.3) | copy-start | bytes 49156
  6.1 14.5 %collective-permute-start = (f32[2,16,48,128]{3,2,1,0:T(8,128)S(1)}, f32[2,16,48,128]{3,2,1,0:T(8,128)S(1)}, u32[]{:S(2)}, u32[]{:S(2)}) collective-permute-start(f32[2,16,48,128]{3,2,1,0:T(8,128)S(1)} %edge.1), channel_id=1, source_target_pairs={{0,1},{1,2},{2,3},{3,4},{4,5},{5,6},{6,7},{7,8},{8,9},{9,10},{10,1... | collective-permute-start | bytes 2359304 | tf_op jit(solution)/shard_map/ppermute | solution.py:459
  23.4 60.3 %copy-start.8 = (s32[16]{0:T(128)S(1)}, s32[16]{0:T(128)}, u32[]{:S(2)}) copy-start(s32[16]{0:T(128)} %own_count_ref.1) | copy-start | bytes 196
  79.7 48.2 %all-to-all-start.1 = ((f32[16,384,128]{2,1,0:T(8,128)}), f32[16,384,128]{2,1,0:T(8,128)S(1)}, u32[]{:S(2)}, u32[]{:S(2)}) async-start(f32[16,384,128]{2,1,0:T(8,128)} %get-tuple-element.20), calls=%async_computation.1 | async-start | bytes 6291456 | tf_op jit(solution)/shard_map/all_to_all | solution.py:463
  86.9 1.4 collective-permute-start.1
  89.0 3.6 %collective-permute-start.2 = (f32[8,128]{1,0:T(8,128)S(1)}, f32[8,128]{1,0:T(8,128)S(1)}, u32[]{:S(2)}, u32[]{:S(2)}) collective-permute-start(f32[8,128]{1,0:T(8,128)S(1)} %add.12), channel_id=1, source_target_pairs={{0,2},{1,3},{2,0},{3,1},{4,6},{5,7},{6,4},{7,5},{8,10},{9,11},{10,... | collective-permute-start | bytes 12296 | tf_op jit(solution)/shard_map/ppermute | solution.py:439
  92.6 4.5 %collective-permute-start.3 = (f32[8,128]{1,0:T(8,128)S(1)}, f32[8,128]{1,0:T(8,128)S(1)}, u32[]{:S(2)}, u32[]{:S(2)}) collective-permute-start(f32[8,128]{1,0:T(8,128)S(1)} %add.13), channel_id=1, source_target_pairs={{0,4},{1,5},{2,6},{3,7},{4,0},{5,1},{6,2},{7,3},{8,12},{9,13},{10,... | collective-permute-start | bytes 12296 | tf_op jit(solution)/shard_map/ppermute | solution.py:439
  97.1 7.5 %collective-permute-start.4 = (f32[8,128]{1,0:T(8,128)S(1)}, f32[8,128]{1,0:T(8,128)S(1)}, u32[]{:S(2)}, u32[]{:S(2)}) collective-permute-start(f32[8,128]{1,0:T(8,128)S(1)} %add.14), channel_id=1, source_target_pairs={{0,8},{1,9},{2,10},{3,11},{4,12},{5,13},{6,14},{7,15},{8,0},{9,1},... | collective-permute-start | bytes 12296 | tf_op jit(solution)/shard_map/ppermute | solution.py:439
  104.6 1.0 copy-start.3
  105.6 0.7 copy-start.7
  128.0 2.1 copy-start.1

commit v5 on v4

--- a/solution.py
+++ b/solution.py
@@ -1,3 +1,5 @@
+import functools
+
 import jax
 import jax.numpy as jnp
 from jax import lax
@@ -10,7 +12,8 @@
 NT = (((1,), (1,)), ((), ()))
 NN = (((1,), (0,)), ((), ()))
 TN = (((0,), (0,)), ((), ()))
-VMEM_LIMIT = 24 * 1024 * 1024
+VMEM_LIMIT = 16 * 1024 * 1024
+SMALL_LIMIT = 8 * 1024 * 1024
 
 
 def dot(a, b, dims=NN):
@@ -252,8 +255,15 @@
     )(*routing, mixing, slots, halo, moments, near_part, far_part)
 
 
+def member_order(runs, m, turned):
+    rows = lax.broadcasted_iota(jnp.int32, (runs, runs), 0)
+    cols = lax.broadcasted_iota(jnp.int32, (runs, runs), 1)
+    reversed_rows = runs - m - rows + 2 * (rows % m)
+    return (jnp.where(turned == 1, reversed_rows, rows) == cols).astype(jnp.float32)
+
+
 def innovation_kernel(
-    block_ref, own_count_ref, near_ref, values_ref, errors_ref, count_ref, gram_ref, right_ref, sums_ref
+    place_ref, count_ref, near_ref, values_ref, errors_ref, gram_ref, right_ref, sums_ref
 ):
     blocks, cap = values_ref.shape
     sources = near_ref.shape[0]
@@ -268,29 +278,33 @@
     moment = jnp.sum(joined(2 * m + 2 * blocks, blocks), axis=0) + m * jnp.sum(drift * drift, axis=0)
     spread = moment / (runs - 1)
     lanes = lax.broadcasted_iota(jnp.int32, (blocks, cap), 1)
-    live = (lanes < count_ref[...]).astype(jnp.float32)
+    rows = lax.broadcasted_iota(jnp.int32, (blocks, cap), 0)
+    counts = jnp.zeros((blocks, cap), jnp.int32)
+    for k in range(blocks):
+        counts = jnp.where(rows == k, count_ref[k], counts)
+    live = (lanes < counts).astype(jnp.float32)
     departure = values_ref[...] - mean
     errors = errors_ref[...]
     terms = live * departure * departure / (errors * errors + spread)
     statistic = jnp.sum(jnp.sum(terms, axis=0, keepdims=True), axis=1, keepdims=True)
-    total = jnp.sum(count_ref[...].astype(jnp.float32), axis=0, keepdims=True)
+    total = jnp.sum(counts[:, :1].astype(jnp.float32), axis=0, keepdims=True)
     lanes = lax.broadcasted_iota(jnp.int32, sums_ref.shape, 1)
     sums_ref[...] = jnp.where(lanes < 64, statistic, total)
 
-    own = block_ref[0]
-    seen = joined(0, m).reshape(runs, cap)
+    own = place_ref[0]
+    seen = dot(member_order(runs, m, place_ref[1]), joined(0, m).reshape(runs, cap))
     mean = jnp.sum(seen, axis=0, keepdims=True) * (1.0 / runs)
     pert = seen - mean
     errors = errors_ref[pl.ds(own, 1), :]
     lanes = lax.broadcasted_iota(jnp.int32, (1, cap), 1)
-    live = (lanes < own_count_ref[own]).astype(jnp.float32)
+    live = (lanes < count_ref[own]).astype(jnp.float32)
     weighted = pert * (live / (errors * errors))
     departure = values_ref[pl.ds(own, 1), :] - mean
     gram_ref[...] = dot(weighted, pert, NT)
     right_ref[...] = dot(jnp.broadcast_to(departure, (8, cap)), weighted, NT)
 
 
-def innovations(block, near, values, errors, counts, m):
+def innovations(place, near, values, errors, counts, m):
     blocks, cap = values.shape
     sources, rows, lanes = near.shape
     extra = 2 * m + 4 * blocks
@@ -306,7 +320,6 @@
             pl.BlockSpec((sources, extra, lanes), lambda g: (0, rows // extra - 1, 0)),
             whole(blocks, cap),
             whole(blocks, cap),
-            whole(blocks, 1),
         ],
         out_specs=[whole(runs, runs), whole(8, runs), whole(8, 128)],
         out_shape=[
@@ -315,7 +328,7 @@
             jax.ShapeDtypeStruct((8, 128), jnp.float32),
         ],
         name="innovation",
-    )(block, counts, near, values, errors, counts.reshape(blocks, 1))
+    )(place, counts, near, values, errors)
 
 
 def small_inverse_factor(a):
@@ -367,7 +380,7 @@
     )
 
 
-def mixer_kernel(gram_ref, right_ref, sums_ref, mixer_ref):
+def mixer_kernel(m, place_ref, gram_ref, right_ref, sums_ref, mixer_ref):
     runs = gram_ref.shape[0]
     inflation = 0.5 + sums_ref[0:1, 0:1] / sums_ref[0:1, 64:65]
     rows = lax.broadcasted_iota(jnp.int32, (runs, runs), 0)
@@ -376,19 +389,21 @@
     inverse = inverse_factor(system)
     half_way = dot(right_ref[...], inverse, NT)
     mean_weight = dot(half_way, inverse)
-    mixer_ref[...] = mean_weight[0:1] + jnp.sqrt(jnp.float32(runs - 1)) * inverse
-
-
-def mixer_of(gram, right, sums):
+    mixer = mean_weight[0:1] + jnp.sqrt(jnp.float32(runs - 1)) * inverse
+    order = member_order(runs, m, place_ref[1])
+    mixer_ref[...] = dot(order, dot(mixer, order, NT))
+
+
+def mixer_of(place, gram, right, sums, m):
     vmem = pl.BlockSpec(memory_space=pltpu.VMEM)
     return pl.pallas_call(
-        mixer_kernel,
-        in_specs=[vmem] * 3,
+        functools.partial(mixer_kernel, m),
+        in_specs=[pl.BlockSpec(memory_space=pltpu.SMEM)] + [vmem] * 3,
         out_specs=vmem,
         out_shape=jax.ShapeDtypeStruct(gram.shape, jnp.float32),
-        compiler_params=pltpu.CompilerParams(vmem_limit_bytes=VMEM_LIMIT),
+        compiler_params=pltpu.CompilerParams(vmem_limit_bytes=SMALL_LIMIT),
         name="mixer",
-    )(gram, right, sums)
+    )(place, gram, right, sums)
 
 
 def apply_kernel(mixer_ref, near_ref, far_ref, out_ref):
@@ -431,6 +446,40 @@
     )(mixer, near, far)
 
 
+def unpack_kernel(x_ref, out_ref, sems):
+    copies = [
+        pltpu.make_async_copy(x_ref.at[b], out_ref.at[:, :, pl.ds(b * BL, BL)], sems.at[b])
+        for b in range(x_ref.shape[0])
+    ]
+    for copy in copies:
+        copy.start()
+    for copy in copies:
+        copy.wait()
+
+
+def unpack(x):
+    blocks, m, s, lanes = x.shape
+    return pl.pallas_call(
+        unpack_kernel,
+        in_specs=[pl.BlockSpec(memory_space=pltpu.VMEM)],
+        out_specs=pl.BlockSpec(memory_space=pl.ANY),
+        out_shape=jax.ShapeDtypeStruct((m, s, blocks * lanes), jnp.float32),
+        scratch_shapes=[pltpu.SemaphoreType.DMA((blocks,))],
+        compiler_params=pltpu.CompilerParams(vmem_limit_bytes=SMALL_LIMIT),
+        name="unpack",
+    )(x)
+
+
+def exchange(x):
+    size, reaches = lax.axis_size("mem"), lax.axis_size("reach")
+    groups = [
+        [(size - 1 - i if r % 2 else i) * reaches + r for i in range(size)] for r in range(reaches)
+    ]
+    return lax.all_to_all(
+        x, ("mem", "reach"), split_axis=0, concat_axis=0, tiled=True, axis_index_groups=groups
+    )
+
+
 def butterfly_sum(x, axes):
     for axis in axes:
         size = lax.axis_size(axis)
@@ -454,21 +503,22 @@
     m, s, r = ensemble.shape
     blocks = r // BL
     reaches = lax.axis_size("reach")
-    block = lax.axis_index("mem").astype(jnp.int32).reshape(1)
+    mem = lax.axis_index("mem").astype(jnp.int32)
+    turned = (lax.axis_index("reach") % 2).astype(jnp.int32)
+    block = jnp.where(turned == 1, lax.axis_size("mem") - 1 - mem, mem)
+    place = jnp.stack([block, turned])
     routing = (ensemble, outgoing_fraction, downstream_position.reshape(1, r), mixing)
     halo = lax.ppermute(edge_carries(*routing), "reach", [(i, i + 1) for i in range(reaches - 1)])
     near, far = forecast(*routing, obs_index, halo)
 
-    near = lax.all_to_all(near, "mem", split_axis=0, concat_axis=0, tiled=True)
-    far = lax.all_to_all(far, "mem", split_axis=0, concat_axis=0, tiled=True)
-    gram, right, sums = innovations(block, near, obs_value, obs_error, obs_count, m)
+    near = exchange(near)
+    far = exchange(far)
+    gram, right, sums = innovations(place, near, obs_value, obs_error, obs_count, m)
     sums = butterfly_sum(sums, ("reach",))
-    mixer = mixer_of(gram, right, sums)
+    mixer = mixer_of(place, gram, right, sums, m)
     updated = apply_mixer(mixer, near.reshape(blocks, -1, s, BL), far.reshape(blocks, -1, s, BL))
-    returned = lax.all_to_all(
-        updated.reshape(blocks, m, s, BL), "mem", split_axis=0, concat_axis=0, tiled=True
-    )
-    return jnp.transpose(returned, (1, 2, 0, 3)).reshape(m, s, r)
+    returned = exchange(updated.reshape(blocks, m, s, BL))
+    return unpack(returned)
 
 
 def solution(mesh):

time: 222 us -> 218 us (0.982)
  blocking collectives: 136 us -> 129 us
  Pallas kernels: 46.2 us -> 51.1 us
  starting transfers between devices: 7.37 us -> 11.8 us
  local copies, waits for them, and re-layouts: 13.2 us -> 8.97 us
  waiting for transfers between devices: 15.6 us -> 13.1 us
    all_to_all x2, blocking collectives: 136 us -> 129 us  [exchange(): lax.all_to_all(x, ('mem', 'reach'), split_axis=0, concat_axis=0, tiled=Tr...]
    pallas_call x1 -> x2, Pallas kernels: 21.7 us -> 26 us  [the longest x1 23.3 us: mixer_of(): pl.pallas_call(functools.partial(mixer_kernel, m), in_specs=[pl.BlockSpec...]
    reshape x2 -> x0, local copies, waits for them, and re-layouts: 4.25 us -> none  [the longest x1 3.57 us: on_device(): return jnp.transpose(returned, (1, 2, 0, 3)).reshape(m, s, r)]
    ppermute x4, starting transfers between devices: 1.46 us -> 5.27 us  [butterfly_sum(): x = x + lax.ppermute(x, axis, [(i, i ^ step) for i in range(size)])]
    ppermute x4, waiting for transfers between devices: 15.5 us -> 13.1 us  [butterfly_sum(): x = x + lax.ppermute(x, axis, [(i, i ^ step) for i in range(size)])]
  transfers between devices with their start and end apart: 6 -> 6, of which waited for: 4 -> 4; matrix products, arithmetic and copies ran while one was open for 1% -> 1% of each run, Pallas kernels for 17% -> 18%
where the time goes in v5:
time: 218 us; the launch traced here: 215 us
  blocking collectives  129 us (59%)
  Pallas kernels  51.1 us (23%)
  waiting for transfers between devices  13.1 us (6%)
  starting transfers between devices  11.8 us (5%)
  local copies, waits for them, and re-layouts  8.97 us (4%)
    all_to_all x2, blocking collectives, exchange(): lax.all_to_all(x, ('mem', 'reach'), split_axis=0, concat_axis=0, tiled=Tr...  129 us
    pallas_call x1, Pallas kernels, mixer_of(): pl.pallas_call(functools.partial(mixer_kernel, m), in_specs=[pl.BlockSpec...  23.3 us
    ppermute x4, waiting for transfers between devices, butterfly_sum(): x = x + lax.ppermute(x, axis, [(i, i ^ step) for i in range(size)])  13.1 us
    pallas_call x1, Pallas kernels, forecast(): pl.pallas_call(inner_kernel, grid=(blocks // 2 - 1,), in_specs=pair + [pl...  12.6 us
    unnamed x18, local copies, waits for them, and re-layouts  8.97 us
    pallas_call x1, Pallas kernels, apply_mixer(): pl.pallas_call(apply_kernel, grid=(states // chunk,), in_specs=[pl.BlockS...  5.78 us
    ppermute x4, starting transfers between devices, butterfly_sum(): x = x + lax.ppermute(x, axis, [(i, i ^ step) for i in range(size)])  5.27 us
    all_to_all x1, starting transfers between devices, exchange(): lax.all_to_all(x, ('mem', 'reach'), split_axis=0, concat_axis=0, tiled=Tr...  4.62 us
  transfers between devices with their start and end apart: 6, of which 4 were waited for; matrix products, arithmetic and copies ran while one was open for 1% of the time, Pallas kernels for 18%

profile of v5, /device:TPU:192, one launch (start us, length us, event | category | flops | bytes accessed | tf_op | source)
XLA Modules:
  0.0 215.5 jit_solution(14980192602779373601)
XLA Ops:
  0.0 0.0 copy-start
  0.0 2.8 %copy-done = f32[16,48,2048]{2,1,0:T(8,128)S(1)} copy-done((f32[16,48,2048]{2,1,0:T(8,128)S(1)}, f32[16,48,2048]{2,1,0:T(8,128)}, u32[]{:S(2)}) %copy-start) | copy-done | bytes 6291480
  2.8 0.0 copy-start.2
  2.8 1.0 copy-done.2
  3.8 0.0 copy-start.4
  3.8 0.7 copy-done.4
  4.5 0.0 copy-start.5
  4.5 0.7 copy-done.5
  5.2 0.0 copy-start.6
  5.2 0.9 edge.1
  6.1 1.9 collective-permute-start
  8.0 0.0 copy-done.6
  8.1 12.6 %inner.1 = (f32[16,480,128]{2,1,0:T(8,128)S(1)}, f32[16,384,128]{2,1,0:T(8,128)}, f32[64,128]{1,0:T(8,128)S(1)}) custom-call(f32[16,48,2048]{2,1,0:T(8,128)S(1)} %copy-done, f32[48,2048]{1,0:T(8,128)S(1)} %copy-done.2, s32[1,2048]{1,0:T(1,128)S(1)} %bitcast.10, f32[16,48,2048]{2,1,0:T(8,128)S(1)} %copy-done, f32[48,2048]{1,0:T(8,128)S(1)} %copy-done.2, ...), custom_call_target="tpu_custom_call" | custom-call | tf_op jit(solution)/shard_map/inner/pallas_call | solution.py:216
  20.6 0.0 collective-permute-done.halo_ref
  20.7 2.8 %outer.1 = (f32[16,480,128]{2,1,0:T(8,128)S(1)}, f32[16,384,128]{2,1,0:T(8,128)}) custom-call(f32[16,48,2048]{2,1,0:T(8,128)S(1)} %copy-done, f32[48,2048]{1,0:T(8,128)S(1)} %copy-done.2, s32[1,2048]{1,0:T(1,128)S(1)} %bitcast.12, f32[48,48]{1,0:T(8,128)S(1)} %copy-done.4, s32[16,256]{1,0:T(8,128)S(1)} %copy-done.6, ...), custom_call_target="tpu_custom_call", output_to_operand_aliasing={{0}: (7, {}), {1}: (8, {})} | custom-call | tf_op jit(solution)/shard_map/outer/pallas_call | solution.py:237
  23.4 54.1 %all_to_all.15.near_ref = f32[16,480,128]{2,1,0:T(8,128)} all-to-all(f32[16,480,128]{2,1,0:T(8,128)S(1)} %get-tuple-element.16), channel_id=1, replica_groups={{0,16,32,48,64,80,96,112,128,144,160,176,192,208,224,240},{241,225,209,..., dimensions={0} | all-to-all | bytes 7864320 | tf_op jit(solution)/shard_map/all_to_all | solution.py:478
  77.5 4.6 %all-to-all-start.1 = ((f32[16,384,128]{2,1,0:T(8,128)}), f32[16,384,128]{2,1,0:T(8,128)S(1)}, u32[]{:S(2)}, u32[]{:S(2)}) async-start(f32[16,384,128]{2,1,0:T(8,128)} %get-tuple-element.20), calls=%async_computation.1 | async-start | bytes 6291456 | tf_op jit(solution)/shard_map/all_to_all | solution.py:478
  82.2 0.7 pad_add_fusion.place_ref
  82.8 0.0 copy-start.8
  82.8 3.0 %innovation.1 = (f32[256,256]{1,0:T(8,128)}, f32[8,256]{1,0:T(8,128)}, f32[8,128]{1,0:T(8,128)}) custom-call(s32[2]{0:T(128)} %pad_add_fusion.place_ref, s32[16]{0:T(128)} %count_ref.1, f32[16,480,128]{2,1,0:T(8,128)} %all_to_all.15.near_ref, f32[16,256]{1,0:T(8,128)} %values_ref.1, f32[16,256]{1,0:T(8,128)} %errors_ref.1), custom_call_target="tpu_custom_call" | custom-call | tf_op jit(solution)/shard_map/innovation/pallas_call | solution.py:314
  85.8 1.7 collective-permute-start.1
  87.5 1.0 collective-permute-done.1
  88.5 0.7 add.17
  89.2 0.0 collective-permute-start.2
  89.2 3.6 %collective-permute-done.2 = f32[8,128]{1,0:T(8,128)S(1)} collective-permute-done((f32[8,128]{1,0:T(8,128)S(1)}, f32[8,128]{1,0:T(8,128)S(1)}, u32[]{:S(2)}, u32[]{:S(2)}) %collective-permute-start.2) | collective-permute-done | bytes 4128 | tf_op jit(solution)/shard_map/ppermute | solution.py:488
  92.8 1.4 collective-permute-start.3
  94.3 3.1 %collective-permute-done.3 = f32[8,128]{1,0:T(8,128)S(1)} collective-permute-done((f32[8,128]{1,0:T(8,128)S(1)}, f32[8,128]{1,0:T(8,128)S(1)}, u32[]{:S(2)}, u32[]{:S(2)}) %collective-permute-start.3) | collective-permute-done | bytes 4128 | tf_op jit(solution)/shard_map/ppermute | solution.py:488
  97.3 2.1 collective-permute-start.4
  99.5 5.4 %collective-permute-done.4 = f32[8,128]{1,0:T(8,128)S(1)} collective-permute-done((f32[8,128]{1,0:T(8,128)S(1)}, f32[8,128]{1,0:T(8,128)S(1)}, u32[]{:S(2)}, u32[]{:S(2)}) %collective-permute-start.4) | collective-permute-done | bytes 4128 | tf_op jit(solution)/shard_map/ppermute | solution.py:488
  104.9 0.0 copy-done.8
  104.9 0.0 copy-start.3
  104.9 0.9 copy-done.3
  105.8 0.0 copy-start.7
  105.8 0.7 copy-done.7
  106.5 23.3 %mixer.1.mixer_ref = f32[256,256]{1,0:T(8,128)S(1)} custom-call(s32[2]{0:T(128)S(1)} %copy-done.8, f32[256,256]{1,0:T(8,128)S(1)} %copy-done.3, f32[8,256]{1,0:T(8,128)S(1)} %copy-done.7, f32[8,128]{1,0:T(8,128)S(1)} %add.20.sums_ref), custom_call_target="tpu_custom_call" | custom-call | tf_op jit(solution)/shard_map/mixer/pallas_call | solution.py:399
  129.8 0.0 all-to-all-done.1
  129.8 0.0 copy-start.1
  129.8 2.1 copy-done.1
  131.9 5.8 %apply.1 = f32[256,48,128]{2,1,0:T(8,128)S(1)} custom-call(f32[256,256]{1,0:T(8,128)S(1)} %mixer.1.mixer_ref, f32[16,10,48,128]{3,2,1,0:T(8,128)S(1)} %bitcast.6, f32[16,8,48,128]{3,2,1,0:T(8,128)S(1)} %bitcast.8), custom_call_target="tpu_custom_call" | custom-call | tf_op jit(solution)/shard_map/apply/pallas_call | solution.py:438
  137.7 74.8 %all_to_all.16.x_ref = f32[16,16,48,128]{3,2,1,0:T(8,128)S(1)} all-to-all(f32[16,16,48,128]{3,2,1,0:T(8,128)S(1)} %bitcast.7), channel_id=1, replica_groups={{0,16,32,48,64,80,96,112,128,144,160,176,192,208,224,240},{241,225,209,..., dimensions={0} | all-to-all | bytes 12582912 | tf_op jit(solution)/shard_map/all_to_all | solution.py:478
  212.5 2.8 %unpack.1 = f32[16,48,2048]{2,1,0:T(8,128)} custom-call(f32[16,16,48,128]{3,2,1,0:T(8,128)S(1)} %all_to_all.16.x_ref), custom_call_target="tpu_custom_call" | custom-call | tf_op jit(solution)/shard_map/unpack/pallas_call | solution.py:462
  (3 shorter events, 0.0 us)
Async XLA Ops:
  0.0 2.8 %copy-start = (f32[16,48,2048]{2,1,0:T(8,128)S(1)}, f32[16,48,2048]{2,1,0:T(8,128)}, u32[]{:S(2)}) copy-start(f32[16,48,2048]{2,1,0:T(8,128)} %x_ref.5) | copy-start | bytes 18874372
  2.8 1.0 copy-start.2
  3.8 0.7 copy-start.4
  4.5 0.7 copy-start.5
  5.2 2.8 %copy-start.6 = (s32[16,256]{1,0:T(8,128)S(1)}, s32[16,256]{1,0:T(8,128)}, u32[]{:S(2)}) copy-start(s32[16,256]{1,0:T(8,128)} %slot_ref.3) | copy-start | bytes 49156
  6.1 14.5 %collective-permute-start = (f32[2,16,48,128]{3,2,1,0:T(8,128)S(1)}, f32[2,16,48,128]{3,2,1,0:T(8,128)S(1)}, u32[]{:S(2)}, u32[]{:S(2)}) collective-permute-start(f32[2,16,48,128]{3,2,1,0:T(8,128)S(1)} %edge.1), channel_id=1, source_target_pairs={{0,1},{1,2},{2,3},{3,4},{4,5},{5,6},{6,7},{7,8},{8,9},{9,10},{10,1... | collective-permute-start | bytes 2359304 | tf_op jit(solution)/shard_map/ppermute | solution.py:511
  77.5 52.3 %all-to-all-start.1 = ((f32[16,384,128]{2,1,0:T(8,128)}), f32[16,384,128]{2,1,0:T(8,128)S(1)}, u32[]{:S(2)}, u32[]{:S(2)}) async-start(f32[16,384,128]{2,1,0:T(8,128)} %get-tuple-element.20), calls=%async_computation.1 | async-start | bytes 6291456 | tf_op jit(solution)/shard_map/all_to_all | solution.py:478
  82.8 22.0 %copy-start.8 = (s32[2]{0:T(128)S(1)}, s32[2]{0:T(128)}, u32[]{:S(2)}) copy-start(s32[2]{0:T(128)} %pad_add_fusion.place_ref) | copy-start | bytes 28
  85.8 2.7 %collective-permute-start.1 = (f32[8,128]{1,0:T(8,128)}, f32[8,128]{1,0:T(8,128)S(1)}, u32[]{:S(2)}, u32[]{:S(2)}) collective-permute-start(f32[8,128]{1,0:T(8,128)} %get-tuple-element.19), channel_id=1, source_target_pairs={{0,1},{1,0},{2,3},{3,2},{4,5},{5,4},{6,7},{7,6},{8,9},{9,8},{10,11... | collective-permute-start | bytes 12296 | tf_op jit(solution)/shard_map/ppermute | solution.py:488
  89.2 3.6 %collective-permute-start.2 = (f32[8,128]{1,0:T(8,128)S(1)}, f32[8,128]{1,0:T(8,128)S(1)}, u32[]{:S(2)}, u32[]{:S(2)}) collective-permute-start(f32[8,128]{1,0:T(8,128)S(1)} %add.17), channel_id=1, source_target_pairs={{0,2},{1,3},{2,0},{3,1},{4,6},{5,7},{6,4},{7,5},{8,10},{9,11},{10,... | collective-permute-start | bytes 12296 | tf_op jit(solution)/shard_map/ppermute | solution.py:488
  92.8 4.5 %collective-permute-start.3 = (f32[8,128]{1,0:T(8,128)S(1)}, f32[8,128]{1,0:T(8,128)S(1)}, u32[]{:S(2)}, u32[]{:S(2)}) collective-permute-start(f32[8,128]{1,0:T(8,128)S(1)} %add.18), channel_id=1, source_target_pairs={{0,4},{1,5},{2,6},{3,7},{4,0},{5,1},{6,2},{7,3},{8,12},{9,13},{10,... | collective-permute-start | bytes 12296 | tf_op jit(solution)/shard_map/ppermute | solution.py:488
  97.3 7.5 %collective-permute-start.4 = (f32[8,128]{1,0:T(8,128)S(1)}, f32[8,128]{1,0:T(8,128)S(1)}, u32[]{:S(2)}, u32[]{:S(2)}) collective-permute-start(f32[8,128]{1,0:T(8,128)S(1)} %add.19), channel_id=1, source_target_pairs={{0,8},{1,9},{2,10},{3,11},{4,12},{5,13},{6,14},{7,15},{8,0},{9,1},... | collective-permute-start | bytes 12296 | tf_op jit(solution)/shard_map/ppermute | solution.py:488
  104.9 1.0 copy-start.3
  105.8 0.7 copy-start.7
  129.8 2.1 copy-start.1

commit v6 on v5

--- a/solution.py
+++ b/solution.py
@@ -263,7 +263,7 @@
 
 
 def innovation_kernel(
-    place_ref, count_ref, near_ref, values_ref, errors_ref, gram_ref, right_ref, sums_ref
+    place_ref, count_ref, near_ref, values_ref, errors_ref, gram_ref, sums_ref
 ):
     blocks, cap = values_ref.shape
     sources = near_ref.shape[0]
@@ -291,8 +291,8 @@
     lanes = lax.broadcasted_iota(jnp.int32, sums_ref.shape, 1)
     sums_ref[...] = jnp.where(lanes < 64, statistic, total)
 
-    own = place_ref[0]
-    seen = dot(member_order(runs, m, place_ref[1]), joined(0, m).reshape(runs, cap))
+    own = lax.shift_right_logical(place_ref[0], 1)
+    seen = dot(member_order(runs, m, place_ref[0] & 1), joined(0, m).reshape(runs, cap))
     mean = jnp.sum(seen, axis=0, keepdims=True) * (1.0 / runs)
     pert = seen - mean
     errors = errors_ref[pl.ds(own, 1), :]
@@ -300,8 +300,8 @@
     live = (lanes < count_ref[own]).astype(jnp.float32)
     weighted = pert * (live / (errors * errors))
     departure = values_ref[pl.ds(own, 1), :] - mean
-    gram_ref[...] = dot(weighted, pert, NT)
-    right_ref[...] = dot(jnp.broadcast_to(departure, (8, cap)), weighted, NT)
+    gram_ref[:runs, :] = dot(weighted, pert, NT)
+    gram_ref[runs:, :] = dot(jnp.broadcast_to(departure, (8, cap)), weighted, NT)
 
 
 def innovations(place, near, values, errors, counts, m):
@@ -321,10 +321,9 @@
             whole(blocks, cap),
             whole(blocks, cap),
         ],
-        out_specs=[whole(runs, runs), whole(8, runs), whole(8, 128)],
+        out_specs=[whole(runs + 8, runs), whole(8, 128)],
         out_shape=[
-            jax.ShapeDtypeStruct((runs, runs), jnp.float32),
-            jax.ShapeDtypeStruct((8, runs), jnp.float32),
+            jax.ShapeDtypeStruct((runs + 8, runs), jnp.float32),
             jax.ShapeDtypeStruct((8, 128), jnp.float32),
         ],
         name="innovation",
@@ -380,30 +379,34 @@
     )
 
 
-def mixer_kernel(m, place_ref, gram_ref, right_ref, sums_ref, mixer_ref):
-    runs = gram_ref.shape[0]
+def mixer_kernel(m, place_ref, gram_ref, sums_ref, mixer_ref):
+    runs = gram_ref.shape[1]
     inflation = 0.5 + sums_ref[0:1, 0:1] / sums_ref[0:1, 64:65]
     rows = lax.broadcasted_iota(jnp.int32, (runs, runs), 0)
     cols = lax.broadcasted_iota(jnp.int32, (runs, runs), 1)
-    system = gram_ref[...] + jnp.where(rows == cols, (runs - 1) / inflation, 0.0)
+    system = gram_ref[:runs, :] + jnp.where(rows == cols, (runs - 1) / inflation, 0.0)
     inverse = inverse_factor(system)
-    half_way = dot(right_ref[...], inverse, NT)
+    half_way = dot(gram_ref[runs:, :], inverse, NT)
     mean_weight = dot(half_way, inverse)
     mixer = mean_weight[0:1] + jnp.sqrt(jnp.float32(runs - 1)) * inverse
-    order = member_order(runs, m, place_ref[1])
-    mixer_ref[...] = dot(order, dot(mixer, order, NT))
-
-
-def mixer_of(place, gram, right, sums, m):
+    turned = place_ref[0] & 1
+    mixer = dot(mixer, member_order(runs, m, turned), NT)
+    groups = runs // m
+    for g in range(groups):
+        spot = jnp.where(turned == 1, groups - 1 - g, g)
+        mixer_ref[pl.ds(pl.multiple_of(spot * m, m), m), :] = mixer[g * m : (g + 1) * m]
+
+
+def mixer_of(place, gram, sums, m):
     vmem = pl.BlockSpec(memory_space=pltpu.VMEM)
     return pl.pallas_call(
         functools.partial(mixer_kernel, m),
-        in_specs=[pl.BlockSpec(memory_space=pltpu.SMEM)] + [vmem] * 3,
+        in_specs=[pl.BlockSpec(memory_space=pltpu.SMEM)] + [vmem] * 2,
         out_specs=vmem,
-        out_shape=jax.ShapeDtypeStruct(gram.shape, jnp.float32),
+        out_shape=jax.ShapeDtypeStruct((gram.shape[1],) * 2, jnp.float32),
         compiler_params=pltpu.CompilerParams(vmem_limit_bytes=SMALL_LIMIT),
         name="mixer",
-    )(place, gram, right, sums)
+    )(place, gram, sums)
 
 
 def apply_kernel(mixer_ref, near_ref, far_ref, out_ref):
@@ -506,16 +509,16 @@
     mem = lax.axis_index("mem").astype(jnp.int32)
     turned = (lax.axis_index("reach") % 2).astype(jnp.int32)
     block = jnp.where(turned == 1, lax.axis_size("mem") - 1 - mem, mem)
-    place = jnp.stack([block, turned])
+    place = (2 * block + turned).reshape(1)
     routing = (ensemble, outgoing_fraction, downstream_position.reshape(1, r), mixing)
     halo = lax.ppermute(edge_carries(*routing), "reach", [(i, i + 1) for i in range(reaches - 1)])
     near, far = forecast(*routing, obs_index, halo)
 
     near = exchange(near)
     far = exchange(far)
-    gram, right, sums = innovations(place, near, obs_value, obs_error, obs_count, m)
+    gram, sums = innovations(place, near, obs_value, obs_error, obs_count, m)
     sums = butterfly_sum(sums, ("reach",))
-    mixer = mixer_of(place, gram, right, sums, m)
+    mixer = mixer_of(place, gram, sums, m)
     updated = apply_mixer(mixer, near.reshape(blocks, -1, s, BL), far.reshape(blocks, -1, s, BL))
     returned = exchange(updated.reshape(blocks, m, s, BL))
     return unpack(returned)

time: 218 us -> 216 us (level)
    unnamed x18 -> x14, local copies, waits for them, and re-layouts: 8.97 us -> 8.28 us
  transfers between devices with their start and end apart: 6 -> 6, of which waited for: 4 -> 4; matrix products, arithmetic and copies ran while one was open for 1% -> 0% of each run, Pallas kernels for 18% -> 18%
where the time goes in v6:
time: 216 us; the launch traced here: 213 us
  blocking collectives  129 us (60%)
  Pallas kernels  50 us (23%)
  waiting for transfers between devices  13.1 us (6%)
  starting transfers between devices  11.8 us (5%)
  local copies, waits for them, and re-layouts  8.28 us (4%)
    all_to_all x2, blocking collectives, exchange(): lax.all_to_all(x, ('mem', 'reach'), split_axis=0, concat_axis=0, tiled=Tr...  129 us
    pallas_call x1, Pallas kernels, mixer_of(): pl.pallas_call(functools.partial(mixer_kernel, m), in_specs=[pl.BlockSpec...  22.2 us
    ppermute x4, waiting for transfers between devices, butterfly_sum(): x = x + lax.ppermute(x, axis, [(i, i ^ step) for i in range(size)])  13.1 us
    pallas_call x1, Pallas kernels, forecast(): pl.pallas_call(inner_kernel, grid=(blocks // 2 - 1,), in_specs=pair + [pl...  12.6 us
    unnamed x14, local copies, waits for them, and re-layouts  8.28 us
    pallas_call x1, Pallas kernels, apply_mixer(): pl.pallas_call(apply_kernel, grid=(states // chunk,), in_specs=[pl.BlockS...  5.79 us
    ppermute x4, starting transfers between devices, butterfly_sum(): x = x + lax.ppermute(x, axis, [(i, i ^ step) for i in range(size)])  5.26 us
    all_to_all x1, starting transfers between devices, exchange(): lax.all_to_all(x, ('mem', 'reach'), split_axis=0, concat_axis=0, tiled=Tr...  4.63 us
  transfers between devices with their start and end apart: 6, of which 4 were waited for; matrix products, arithmetic and copies ran while one was open for 0% of the time, Pallas kernels for 18%

profile of v6, /device:TPU:192, one launch (start us, length us, event | category | flops | bytes accessed | tf_op | source)
XLA Modules:
  0.0 213.1 jit_solution(17995163323411123563)
XLA Ops:
  0.0 0.0 copy-start
  0.0 2.8 %copy-done = f32[16,48,2048]{2,1,0:T(8,128)S(1)} copy-done((f32[16,48,2048]{2,1,0:T(8,128)S(1)}, f32[16,48,2048]{2,1,0:T(8,128)}, u32[]{:S(2)}) %copy-start) | copy-done | bytes 6291480
  2.8 0.0 copy-start.2
  2.8 1.0 copy-done.2
  3.8 0.0 copy-start.4
  3.8 0.7 copy-done.4
  4.5 0.0 copy-start.5
  4.5 0.7 copy-done.5
  5.2 0.0 copy-start.6
  5.2 0.9 edge.1
  6.1 1.9 collective-permute-start
  8.0 0.0 copy-done.6
  8.1 12.6 %inner.1 = (f32[16,480,128]{2,1,0:T(8,128)S(1)}, f32[16,384,128]{2,1,0:T(8,128)}, f32[64,128]{1,0:T(8,128)S(1)}) custom-call(f32[16,48,2048]{2,1,0:T(8,128)S(1)} %copy-done, f32[48,2048]{1,0:T(8,128)S(1)} %copy-done.2, s32[1,2048]{1,0:T(1,128)S(1)} %bitcast.9, f32[16,48,2048]{2,1,0:T(8,128)S(1)} %copy-done, f32[48,2048]{1,0:T(8,128)S(1)} %copy-done.2, ...), custom_call_target="tpu_custom_call" | custom-call | tf_op jit(solution)/shard_map/inner/pallas_call | solution.py:216
  20.6 0.0 collective-permute-done.halo_ref
  20.7 2.8 %outer.1 = (f32[16,480,128]{2,1,0:T(8,128)S(1)}, f32[16,384,128]{2,1,0:T(8,128)}) custom-call(f32[16,48,2048]{2,1,0:T(8,128)S(1)} %copy-done, f32[48,2048]{1,0:T(8,128)S(1)} %copy-done.2, s32[1,2048]{1,0:T(1,128)S(1)} %bitcast.11, f32[48,48]{1,0:T(8,128)S(1)} %copy-done.4, s32[16,256]{1,0:T(8,128)S(1)} %copy-done.6, ...), custom_call_target="tpu_custom_call", output_to_operand_aliasing={{0}: (7, {}), {1}: (8, {})} | custom-call | tf_op jit(solution)/shard_map/outer/pallas_call | solution.py:237
  23.4 54.1 %all_to_all.15.near_ref = f32[16,480,128]{2,1,0:T(8,128)} all-to-all(f32[16,480,128]{2,1,0:T(8,128)S(1)} %get-tuple-element.15), channel_id=1, replica_groups={{0,16,32,48,64,80,96,112,128,144,160,176,192,208,224,240},{241,225,209,..., dimensions={0} | all-to-all | bytes 7864320 | tf_op jit(solution)/shard_map/all_to_all | solution.py:481
  77.5 4.6 %all-to-all-start.1 = ((f32[16,384,128]{2,1,0:T(8,128)}), f32[16,384,128]{2,1,0:T(8,128)S(1)}, u32[]{:S(2)}, u32[]{:S(2)}) async-start(f32[16,384,128]{2,1,0:T(8,128)} %get-tuple-element.18), calls=%async_computation.1 | async-start | bytes 6291456 | tf_op jit(solution)/shard_map/all_to_all | solution.py:481
  82.2 3.0 %innovation.1 = (f32[264,256]{1,0:T(8,128)}, f32[8,128]{1,0:T(8,128)}) custom-call(s32[1]{0:T(128)} %bitcast.place_ref, s32[16]{0:T(128)} %count_ref.1, f32[16,480,128]{2,1,0:T(8,128)} %all_to_all.15.near_ref, f32[16,256]{1,0:T(8,128)} %values_ref.1, f32[16,256]{1,0:T(8,128)} %errors_ref.1), custom_call_target="tpu_custom_call" | custom-call | tf_op jit(solution)/shard_map/innovation/pallas_call | solution.py:314
  85.2 1.7 collective-permute-start.1
  86.8 1.0 collective-permute-done.1
  87.9 0.7 add.21
  88.5 0.0 collective-permute-start.2
  88.6 3.6 %collective-permute-done.2 = f32[8,128]{1,0:T(8,128)S(1)} collective-permute-done((f32[8,128]{1,0:T(8,128)S(1)}, f32[8,128]{1,0:T(8,128)S(1)}, u32[]{:S(2)}, u32[]{:S(2)}) %collective-permute-start.2) | collective-permute-done | bytes 4128 | tf_op jit(solution)/shard_map/ppermute | solution.py:491
  92.2 1.4 collective-permute-start.3
  93.6 3.1 %collective-permute-done.3 = f32[8,128]{1,0:T(8,128)S(1)} collective-permute-done((f32[8,128]{1,0:T(8,128)S(1)}, f32[8,128]{1,0:T(8,128)S(1)}, u32[]{:S(2)}, u32[]{:S(2)}) %collective-permute-start.3) | collective-permute-done | bytes 4128 | tf_op jit(solution)/shard_map/ppermute | solution.py:491
  96.7 2.2 %collective-permute-start.4 = (f32[8,128]{1,0:T(8,128)S(1)}, f32[8,128]{1,0:T(8,128)S(1)}, u32[]{:S(2)}, u32[]{:S(2)}) collective-permute-start(f32[8,128]{1,0:T(8,128)S(1)} %add.23), channel_id=1, source_target_pairs={{0,8},{1,9},{2,10},{3,11},{4,12},{5,13},{6,14},{7,15},{8,0},{9,1},... | collective-permute-start | bytes 12296 | tf_op jit(solution)/shard_map/ppermute | solution.py:491
  98.8 5.4 %collective-permute-done.4 = f32[8,128]{1,0:T(8,128)S(1)} collective-permute-done((f32[8,128]{1,0:T(8,128)S(1)}, f32[8,128]{1,0:T(8,128)S(1)}, u32[]{:S(2)}, u32[]{:S(2)}) %collective-permute-start.4) | collective-permute-done | bytes 4128 | tf_op jit(solution)/shard_map/ppermute | solution.py:491
  104.2 0.0 copy-start.3
  104.2 1.0 copy-done.3
  105.1 22.2 %mixer.1.mixer_ref = f32[256,256]{1,0:T(8,128)S(1)} custom-call(s32[1]{0:T(128)} %bitcast.place_ref, f32[264,256]{1,0:T(8,128)S(1)} %copy-done.3, f32[8,128]{1,0:T(8,128)S(1)} %add.24.sums_ref), custom_call_target="tpu_custom_call" | custom-call | tf_op jit(solution)/shard_map/mixer/pallas_call | solution.py:402
  127.4 0.0 all-to-all-done.1
  127.4 0.0 copy-start.1
  127.4 2.1 copy-done.1
  129.5 5.8 %apply.1 = f32[256,48,128]{2,1,0:T(8,128)S(1)} custom-call(f32[256,256]{1,0:T(8,128)S(1)} %mixer.1.mixer_ref, f32[16,10,48,128]{3,2,1,0:T(8,128)S(1)} %bitcast.5, f32[16,8,48,128]{3,2,1,0:T(8,128)S(1)} %bitcast.7), custom_call_target="tpu_custom_call" | custom-call | tf_op jit(solution)/shard_map/apply/pallas_call | solution.py:441
  135.3 74.8 %all_to_all.16.x_ref = f32[16,16,48,128]{3,2,1,0:T(8,128)S(1)} all-to-all(f32[16,16,48,128]{3,2,1,0:T(8,128)S(1)} %bitcast.6), channel_id=1, replica_groups={{0,16,32,48,64,80,96,112,128,144,160,176,192,208,224,240},{241,225,209,..., dimensions={0} | all-to-all | bytes 12582912 | tf_op jit(solution)/shard_map/all_to_all | solution.py:481
  210.1 2.8 %unpack.1 = f32[16,48,2048]{2,1,0:T(8,128)} custom-call(f32[16,16,48,128]{3,2,1,0:T(8,128)S(1)} %all_to_all.16.x_ref), custom_call_target="tpu_custom_call" | custom-call | tf_op jit(solution)/shard_map/unpack/pallas_call | solution.py:465
  (3 shorter events, 0.0 us)
Async XLA Ops:
  0.0 2.8 %copy-start = (f32[16,48,2048]{2,1,0:T(8,128)S(1)}, f32[16,48,2048]{2,1,0:T(8,128)}, u32[]{:S(2)}) copy-start(f32[16,48,2048]{2,1,0:T(8,128)} %x_ref.5) | copy-start | bytes 18874372
  2.8 1.0 copy-start.2
  3.8 0.7 copy-start.4
  4.5 0.7 copy-start.5
  5.2 2.8 %copy-start.6 = (s32[16,256]{1,0:T(8,128)S(1)}, s32[16,256]{1,0:T(8,128)}, u32[]{:S(2)}) copy-start(s32[16,256]{1,0:T(8,128)} %slot_ref.3) | copy-start | bytes 49156
  6.1 14.5 %collective-permute-start = (f32[2,16,48,128]{3,2,1,0:T(8,128)S(1)}, f32[2,16,48,128]{3,2,1,0:T(8,128)S(1)}, u32[]{:S(2)}, u32[]{:S(2)}) collective-permute-start(f32[2,16,48,128]{3,2,1,0:T(8,128)S(1)} %edge.1), channel_id=1, source_target_pairs={{0,1},{1,2},{2,3},{3,4},{4,5},{5,6},{6,7},{7,8},{8,9},{9,10},{10,1... | collective-permute-start | bytes 2359304 | tf_op jit(solution)/shard_map/ppermute | solution.py:514
  77.5 49.8 %all-to-all-start.1 = ((f32[16,384,128]{2,1,0:T(8,128)}), f32[16,384,128]{2,1,0:T(8,128)S(1)}, u32[]{:S(2)}, u32[]{:S(2)}) async-start(f32[16,384,128]{2,1,0:T(8,128)} %get-tuple-element.18), calls=%async_computation.1 | async-start | bytes 6291456 | tf_op jit(solution)/shard_map/all_to_all | solution.py:481
  85.2 2.7 %collective-permute-start.1 = (f32[8,128]{1,0:T(8,128)}, f32[8,128]{1,0:T(8,128)S(1)}, u32[]{:S(2)}, u32[]{:S(2)}) collective-permute-start(f32[8,128]{1,0:T(8,128)} %get-tuple-element.17), channel_id=1, source_target_pairs={{0,1},{1,0},{2,3},{3,2},{4,5},{5,4},{6,7},{7,6},{8,9},{9,8},{10,11... | collective-permute-start | bytes 12296 | tf_op jit(solution)/shard_map/ppermute | solution.py:491
  88.5 3.6 %collective-permute-start.2 = (f32[8,128]{1,0:T(8,128)S(1)}, f32[8,128]{1,0:T(8,128)S(1)}, u32[]{:S(2)}, u32[]{:S(2)}) collective-permute-start(f32[8,128]{1,0:T(8,128)S(1)} %add.21), channel_id=1, source_target_pairs={{0,2},{1,3},{2,0},{3,1},{4,6},{5,7},{6,4},{7,5},{8,10},{9,11},{10,... | collective-permute-start | bytes 12296 | tf_op jit(solution)/shard_map/ppermute | solution.py:491
  92.2 4.5 %collective-permute-start.3 = (f32[8,128]{1,0:T(8,128)S(1)}, f32[8,128]{1,0:T(8,128)S(1)}, u32[]{:S(2)}, u32[]{:S(2)}) collective-permute-start(f32[8,128]{1,0:T(8,128)S(1)} %add.22), channel_id=1, source_target_pairs={{0,4},{1,5},{2,6},{3,7},{4,0},{5,1},{6,2},{7,3},{8,12},{9,13},{10,... | collective-permute-start | bytes 12296 | tf_op jit(solution)/shard_map/ppermute | solution.py:491
  96.7 7.5 %collective-permute-start.4 = (f32[8,128]{1,0:T(8,128)S(1)}, f32[8,128]{1,0:T(8,128)S(1)}, u32[]{:S(2)}, u32[]{:S(2)}) collective-permute-start(f32[8,128]{1,0:T(8,128)S(1)} %add.23), channel_id=1, source_target_pairs={{0,8},{1,9},{2,10},{3,11},{4,12},{5,13},{6,14},{7,15},{8,0},{9,1},... | collective-permute-start | bytes 12296 | tf_op jit(solution)/shard_map/ppermute | solution.py:491
  104.2 1.0 copy-start.3
  127.4 2.1 copy-start.1

commit v7 on v6

--- a/solution.py
+++ b/solution.py
@@ -434,7 +434,7 @@
             out_rows[pl.ds(s + i, runs, stride=states), :] = out[:, i * lanes : (i + 1) * lanes]
 
 
-def apply_mixer(mixer, near, far, chunk=8):
+def apply_mixer(mixer, near, far, chunk=24):
     sources, half, states, lanes = far.shape
     runs = 2 * sources * half
     part = pl.BlockSpec((sources, half, chunk, lanes), lambda g: (0, 0, g, 0))

time: 216 us -> 215 us (level)
  no operation moved by 1% of the time
where the time goes in v7:
time: 215 us; the launch traced here: 212 us
  blocking collectives  129 us (60%)
  Pallas kernels  49.2 us (23%)
  waiting for transfers between devices  13.1 us (6%)
  starting transfers between devices  11.8 us (5%)
  local copies, waits for them, and re-layouts  8.28 us (4%)
    all_to_all x2, blocking collectives, exchange(): lax.all_to_all(x, ('mem', 'reach'), split_axis=0, concat_axis=0, tiled=Tr...  129 us
    pallas_call x1, Pallas kernels, mixer_of(): pl.pallas_call(functools.partial(mixer_kernel, m), in_specs=[pl.BlockSpec...  22.2 us
    ppermute x4, waiting for transfers between devices, butterfly_sum(): x = x + lax.ppermute(x, axis, [(i, i ^ step) for i in range(size)])  13.1 us
    pallas_call x1, Pallas kernels, forecast(): pl.pallas_call(inner_kernel, grid=(blocks // 2 - 1,), in_specs=pair + [pl...  12.6 us
    unnamed x14, local copies, waits for them, and re-layouts  8.28 us
    ppermute x4, starting transfers between devices, butterfly_sum(): x = x + lax.ppermute(x, axis, [(i, i ^ step) for i in range(size)])  5.26 us
    pallas_call x1, Pallas kernels, apply_mixer(): pl.pallas_call(apply_kernel, grid=(states // chunk,), in_specs=[pl.BlockS...  4.93 us
    all_to_all x1, starting transfers between devices, exchange(): lax.all_to_all(x, ('mem', 'reach'), split_axis=0, concat_axis=0, tiled=Tr...  4.63 us
  transfers between devices with their start and end apart: 6, of which 4 were waited for; matrix products, arithmetic and copies ran while one was open for 0% of the time, Pallas kernels for 18%

profile of v7, /device:TPU:192, one launch (start us, length us, event | category | flops | bytes accessed | tf_op | source)
XLA Modules:
  0.0 212.2 jit_solution(12295108058621557532)
XLA Ops:
  0.0 0.0 copy-start
  0.0 2.8 %copy-done = f32[16,48,2048]{2,1,0:T(8,128)S(1)} copy-done((f32[16,48,2048]{2,1,0:T(8,128)S(1)}, f32[16,48,2048]{2,1,0:T(8,128)}, u32[]{:S(2)}) %copy-start) | copy-done | bytes 6291480
  2.8 0.0 copy-start.2
  2.8 1.0 copy-done.2
  3.8 0.0 copy-start.4
  3.8 0.7 copy-done.4
  4.5 0.0 copy-start.5
  4.5 0.7 copy-done.5
  5.2 0.0 copy-start.6
  5.2 0.9 edge.1
  6.1 1.9 collective-permute-start
  8.0 0.0 copy-done.6
  8.1 12.6 %inner.1 = (f32[16,480,128]{2,1,0:T(8,128)S(1)}, f32[16,384,128]{2,1,0:T(8,128)}, f32[64,128]{1,0:T(8,128)S(1)}) custom-call(f32[16,48,2048]{2,1,0:T(8,128)S(1)} %copy-done, f32[48,2048]{1,0:T(8,128)S(1)} %copy-done.2, s32[1,2048]{1,0:T(1,128)S(1)} %bitcast.9, f32[16,48,2048]{2,1,0:T(8,128)S(1)} %copy-done, f32[48,2048]{1,0:T(8,128)S(1)} %copy-done.2, ...), custom_call_target="tpu_custom_call" | custom-call | tf_op jit(solution)/shard_map/inner/pallas_call | solution.py:216
  20.6 0.0 collective-permute-done.halo_ref
  20.7 2.8 %outer.1 = (f32[16,480,128]{2,1,0:T(8,128)S(1)}, f32[16,384,128]{2,1,0:T(8,128)}) custom-call(f32[16,48,2048]{2,1,0:T(8,128)S(1)} %copy-done, f32[48,2048]{1,0:T(8,128)S(1)} %copy-done.2, s32[1,2048]{1,0:T(1,128)S(1)} %bitcast.11, f32[48,48]{1,0:T(8,128)S(1)} %copy-done.4, s32[16,256]{1,0:T(8,128)S(1)} %copy-done.6, ...), custom_call_target="tpu_custom_call", output_to_operand_aliasing={{0}: (7, {}), {1}: (8, {})} | custom-call | tf_op jit(solution)/shard_map/outer/pallas_call | solution.py:237
  23.4 54.1 %all_to_all.15.near_ref = f32[16,480,128]{2,1,0:T(8,128)} all-to-all(f32[16,480,128]{2,1,0:T(8,128)S(1)} %get-tuple-element.15), channel_id=1, replica_groups={{0,16,32,48,64,80,96,112,128,144,160,176,192,208,224,240},{241,225,209,..., dimensions={0} | all-to-all | bytes 7864320 | tf_op jit(solution)/shard_map/all_to_all | solution.py:481
  77.5 4.6 %all-to-all-start.1 = ((f32[16,384,128]{2,1,0:T(8,128)}), f32[16,384,128]{2,1,0:T(8,128)S(1)}, u32[]{:S(2)}, u32[]{:S(2)}) async-start(f32[16,384,128]{2,1,0:T(8,128)} %get-tuple-element.18), calls=%async_computation.1 | async-start | bytes 6291456 | tf_op jit(solution)/shard_map/all_to_all | solution.py:481
  82.2 3.0 %innovation.1 = (f32[264,256]{1,0:T(8,128)}, f32[8,128]{1,0:T(8,128)}) custom-call(s32[1]{0:T(128)} %bitcast.place_ref, s32[16]{0:T(128)} %count_ref.1, f32[16,480,128]{2,1,0:T(8,128)} %all_to_all.15.near_ref, f32[16,256]{1,0:T(8,128)} %values_ref.1, f32[16,256]{1,0:T(8,128)} %errors_ref.1), custom_call_target="tpu_custom_call" | custom-call | tf_op jit(solution)/shard_map/innovation/pallas_call | solution.py:314
  85.2 1.7 collective-permute-start.1
  86.8 1.0 collective-permute-done.1
  87.9 0.7 add.21
  88.5 0.0 collective-permute-start.2
  88.6 3.6 %collective-permute-done.2 = f32[8,128]{1,0:T(8,128)S(1)} collective-permute-done((f32[8,128]{1,0:T(8,128)S(1)}, f32[8,128]{1,0:T(8,128)S(1)}, u32[]{:S(2)}, u32[]{:S(2)}) %collective-permute-start.2) | collective-permute-done | bytes 4128 | tf_op jit(solution)/shard_map/ppermute | solution.py:491
  92.2 1.4 collective-permute-start.3
  93.6 3.1 %collective-permute-done.3 = f32[8,128]{1,0:T(8,128)S(1)} collective-permute-done((f32[8,128]{1,0:T(8,128)S(1)}, f32[8,128]{1,0:T(8,128)S(1)}, u32[]{:S(2)}, u32[]{:S(2)}) %collective-permute-start.3) | collective-permute-done | bytes 4128 | tf_op jit(solution)/shard_map/ppermute | solution.py:491
  96.7 2.2 %collective-permute-start.4 = (f32[8,128]{1,0:T(8,128)S(1)}, f32[8,128]{1,0:T(8,128)S(1)}, u32[]{:S(2)}, u32[]{:S(2)}) collective-permute-start(f32[8,128]{1,0:T(8,128)S(1)} %add.23), channel_id=1, source_target_pairs={{0,8},{1,9},{2,10},{3,11},{4,12},{5,13},{6,14},{7,15},{8,0},{9,1},... | collective-permute-start | bytes 12296 | tf_op jit(solution)/shard_map/ppermute | solution.py:491
  98.8 5.4 %collective-permute-done.4 = f32[8,128]{1,0:T(8,128)S(1)} collective-permute-done((f32[8,128]{1,0:T(8,128)S(1)}, f32[8,128]{1,0:T(8,128)S(1)}, u32[]{:S(2)}, u32[]{:S(2)}) %collective-permute-start.4) | collective-permute-done | bytes 4128 | tf_op jit(solution)/shard_map/ppermute | solution.py:491
  104.2 0.0 copy-start.3
  104.2 1.0 copy-done.3
  105.1 22.2 %mixer.1.mixer_ref = f32[256,256]{1,0:T(8,128)S(1)} custom-call(s32[1]{0:T(128)} %bitcast.place_ref, f32[264,256]{1,0:T(8,128)S(1)} %copy-done.3, f32[8,128]{1,0:T(8,128)S(1)} %add.24.sums_ref), custom_call_target="tpu_custom_call" | custom-call | tf_op jit(solution)/shard_map/mixer/pallas_call | solution.py:402
  127.4 0.0 all-to-all-done.1
  127.4 0.0 copy-start.1
  127.4 2.1 copy-done.1
  129.5 4.9 %apply.1 = f32[256,48,128]{2,1,0:T(8,128)S(1)} custom-call(f32[256,256]{1,0:T(8,128)S(1)} %mixer.1.mixer_ref, f32[16,10,48,128]{3,2,1,0:T(8,128)S(1)} %bitcast.5, f32[16,8,48,128]{3,2,1,0:T(8,128)S(1)} %bitcast.7), custom_call_target="tpu_custom_call" | custom-call | tf_op jit(solution)/shard_map/apply/pallas_call | solution.py:441
  134.4 74.8 %all_to_all.16.x_ref = f32[16,16,48,128]{3,2,1,0:T(8,128)S(1)} all-to-all(f32[16,16,48,128]{3,2,1,0:T(8,128)S(1)} %bitcast.6), channel_id=1, replica_groups={{0,16,32,48,64,80,96,112,128,144,160,176,192,208,224,240},{241,225,209,..., dimensions={0} | all-to-all | bytes 12582912 | tf_op jit(solution)/shard_map/all_to_all | solution.py:481
  209.3 2.8 %unpack.1 = f32[16,48,2048]{2,1,0:T(8,128)} custom-call(f32[16,16,48,128]{3,2,1,0:T(8,128)S(1)} %all_to_all.16.x_ref), custom_call_target="tpu_custom_call" | custom-call | tf_op jit(solution)/shard_map/unpack/pallas_call | solution.py:465
  (3 shorter events, 0.0 us)
Async XLA Ops:
  0.0 2.8 %copy-start = (f32[16,48,2048]{2,1,0:T(8,128)S(1)}, f32[16,48,2048]{2,1,0:T(8,128)}, u32[]{:S(2)}) copy-start(f32[16,48,2048]{2,1,0:T(8,128)} %x_ref.5) | copy-start | bytes 18874372
  2.8 1.0 copy-start.2
  3.8 0.7 copy-start.4
  4.5 0.7 copy-start.5
  5.2 2.8 %copy-start.6 = (s32[16,256]{1,0:T(8,128)S(1)}, s32[16,256]{1,0:T(8,128)}, u32[]{:S(2)}) copy-start(s32[16,256]{1,0:T(8,128)} %slot_ref.3) | copy-start | bytes 49156
  6.1 14.5 %collective-permute-start = (f32[2,16,48,128]{3,2,1,0:T(8,128)S(1)}, f32[2,16,48,128]{3,2,1,0:T(8,128)S(1)}, u32[]{:S(2)}, u32[]{:S(2)}) collective-permute-start(f32[2,16,48,128]{3,2,1,0:T(8,128)S(1)} %edge.1), channel_id=1, source_target_pairs={{0,1},{1,2},{2,3},{3,4},{4,5},{5,6},{6,7},{7,8},{8,9},{9,10},{10,1... | collective-permute-start | bytes 2359304 | tf_op jit(solution)/shard_map/ppermute | solution.py:514
  77.5 49.8 %all-to-all-start.1 = ((f32[16,384,128]{2,1,0:T(8,128)}), f32[16,384,128]{2,1,0:T(8,128)S(1)}, u32[]{:S(2)}, u32[]{:S(2)}) async-start(f32[16,384,128]{2,1,0:T(8,128)} %get-tuple-element.18), calls=%async_computation.1 | async-start | bytes 6291456 | tf_op jit(solution)/shard_map/all_to_all | solution.py:481
  85.2 2.7 %collective-permute-start.1 = (f32[8,128]{1,0:T(8,128)}, f32[8,128]{1,0:T(8,128)S(1)}, u32[]{:S(2)}, u32[]{:S(2)}) collective-permute-start(f32[8,128]{1,0:T(8,128)} %get-tuple-element.17), channel_id=1, source_target_pairs={{0,1},{1,0},{2,3},{3,2},{4,5},{5,4},{6,7},{7,6},{8,9},{9,8},{10,11... | collective-permute-start | bytes 12296 | tf_op jit(solution)/shard_map/ppermute | solution.py:491
  88.5 3.6 %collective-permute-start.2 = (f32[8,128]{1,0:T(8,128)S(1)}, f32[8,128]{1,0:T(8,128)S(1)}, u32[]{:S(2)}, u32[]{:S(2)}) collective-permute-start(f32[8,128]{1,0:T(8,128)S(1)} %add.21), channel_id=1, source_target_pairs={{0,2},{1,3},{2,0},{3,1},{4,6},{5,7},{6,4},{7,5},{8,10},{9,11},{10,... | collective-permute-start | bytes 12296 | tf_op jit(solution)/shard_map/ppermute | solution.py:491
  92.2 4.5 %collective-permute-start.3 = (f32[8,128]{1,0:T(8,128)S(1)}, f32[8,128]{1,0:T(8,128)S(1)}, u32[]{:S(2)}, u32[]{:S(2)}) collective-permute-start(f32[8,128]{1,0:T(8,128)S(1)} %add.22), channel_id=1, source_target_pairs={{0,4},{1,5},{2,6},{3,7},{4,0},{5,1},{6,2},{7,3},{8,12},{9,13},{10,... | collective-permute-start | bytes 12296 | tf_op jit(solution)/shard_map/ppermute | solution.py:491
  96.7 7.5 %collective-permute-start.4 = (f32[8,128]{1,0:T(8,128)S(1)}, f32[8,128]{1,0:T(8,128)S(1)}, u32[]{:S(2)}, u32[]{:S(2)}) collective-permute-start(f32[8,128]{1,0:T(8,128)S(1)} %add.23), channel_id=1, source_target_pairs={{0,8},{1,9},{2,10},{3,11},{4,12},{5,13},{6,14},{7,15},{8,0},{9,1},... | collective-permute-start | bytes 12296 | tf_op jit(solution)/shard_map/ppermute | solution.py:491
  104.2 1.0 copy-start.3
  127.4 2.1 copy-start.1
